TPU v7x, 128 devices: a whole 4x4x4 slice. The times are simulated.
128 devices in a mesh: group: 8 (over z, core), bulk: 16 (over x, y).
Axes of the slice: x: 4, y: 4, z: 4, core: 2. Of those that a mesh axis runs over, the one named last changes fastest.
Arguments:
- p_tiles: float32 [6144, 128, 128], P(('group', 'bulk')), may hold values from -0.5 to 0.5
- a_tiles: float32 [6144, 7, 128, 128], P(('group', 'bulk')), may hold values from -0.5 to 0.5
- col_ref: int32 [6144, 7], P(('group', 'bulk')), may hold values from 0 to 111, as said below
- send_list: int32 [128, 2, 32], P(('group', 'bulk')), may hold values from -1 to 47, as said below
- coarse_tile: int32 [6144, 7], P(('group', 'bulk')), may hold values from 0 to 127
Outputs:
- coarse_op: float32 [1024, 128, 128], P('group')
Inputs may be any that keep to these rules, and one draw needn't show every extreme that they name: `send_list`: entry [s, 0, j] is the local index of a fine block of device s that device s - 1 receives in slot j, entry [s, 1, j] one that device s + 1 receives; the slots of one entry hold distinct blocks, filled slots come first, -1 marks an empty slot. Device 0 sends nothing below and the last device nothing above; every other pair fills between 16 and 32 slots, and device 0 fills all 32 slots for device 1. `col_ref`: on device d, a value v under 48 names d's own fine block v; a value v of 48 or more names the tile that d receives in slot (v - 48) % 32 from the slab below if (v - 48) // 32 is 0, from the slab above if it is 1, always a filled slot. Every filled slot that d receives is named by exactly one coupling of d.
All inputs are finite; a program needn't handle non-finite values.
Results may differ from a plain program's by a relative error of at most 0.0003.
Values sent between devices are 32-bit elements; how exact they have to be, the bound alone decides.
No kernel may reach another device: no remote copies, remote signals or barrier semaphores. Data moves between devices by JAX's collectives and lax.ppermute only.
A program may use at most 192 MiB of HBM per device.

v0:
```python
import jax
import jax.numpy as jnp
from jax import lax
from jax.sharding import PartitionSpec as P

CT = 128


def shifted(block, axis, distance):
    devices = range(lax.axis_size(axis))
    route = [(i - distance, i) for i in devices if i - distance in devices]
    return lax.ppermute(block, axis, route)


def shards(p_tiles, a_tiles, col_ref, send_list, coarse_tile):
    blocks, cell_width, coarse = p_tiles.shape
    neighbours = a_tiles.shape[1]
    capacity = send_list.shape[2]
    outgoing = send_list[0].reshape(-1)
    chosen = jnp.take(p_tiles, jnp.maximum(outgoing, 0), axis=0)
    chosen = jnp.where((outgoing >= 0)[:, None, None], chosen, 0.0)
    chosen = chosen.reshape(2, capacity, cell_width, coarse)
    lower_tiles = shifted(chosen[1], ("group", "bulk"), 1)
    upper_tiles = shifted(chosen[0], ("group", "bulk"), -1)
    lookup_rows = jnp.concatenate([p_tiles, lower_tiles, upper_tiles], axis=0)
    right_tiles = jnp.take(lookup_rows, col_ref.reshape(-1), axis=0)
    couplings = a_tiles.reshape(blocks * neighbours, cell_width, cell_width)
    product = jnp.einsum("qxy,qyc->qxc", couplings, right_tiles, precision=lax.Precision.HIGHEST)
    triple = jnp.einsum(
        "ixa,ikxc->ikac",
        p_tiles,
        product.reshape(blocks, neighbours, cell_width, coarse),
        precision=lax.Precision.HIGHEST,
    )
    triple = triple.reshape(blocks * neighbours, coarse, coarse)
    tile_count = CT
    selector = (
        coarse_tile.reshape(-1)[None, :] == jnp.arange(tile_count, dtype=jnp.int32)[:, None]
    ).astype(jnp.float32)
    partial_op = jnp.einsum("sq,qac->sac", selector, triple, precision=lax.Precision.HIGHEST)
    operator = lax.psum(partial_op, "bulk")
    return operator


def solution(mesh):
    in_specs = (
        P(("group", "bulk"), None, None),
        P(("group", "bulk"), None, None, None),
        P(("group", "bulk"), None),
        P(("group", "bulk"), None, None),
        P(("group", "bulk"), None),
    )
    out_specs = P("group", None, None)
    return jax.shard_map(shards, mesh=mesh, in_specs=in_specs, out_specs=out_specs, check_vma=False)
```

profile of v0, /device:TPU:32, one launch (start us, length us, event | category | flops | bytes accessed | tf_op | source)
XLA Modules:
  0.0 367.5 jit_solution(11472771202731306196)
XLA Ops:
  6.5 0.0 all-reduce.2.cloned.1.call-start
  6.5 0.7 broadcast_compare_fusion.1
  7.2 0.7 broadcast_maximum_fusion
  7.9 0.1 ge.28
  8.0 0.1 le.29
  8.1 0.1 reshape.90
  8.2 4.7 %gather_fusion = f32[64,128,128]{2,1,0:T(8,128)} fusion(f32[48,128,128]{2,1,0:T(8,128)} %param.5, s32[1024]{0:T(1024)S(1)} %pad_clamp_fusion.1), kind=kCustom, calls=%fused_computation | custom fusion | bytes 8388864 | tf_op jit(solution)/shard_map/jit(_take)/gather | solution.py:20
  12.9 0.0 copy-start.1
  12.9 0.0 copy-start.2
  12.9 2.8 select_select_fusion
  15.7 2.3 fusion.12
  18.0 3.5 collective-permute-start
  21.5 6.3 %collective-permute-start.1 = (f32[32,128,128]{2,1,0:T(8,128)}, f32[32,128,128]{2,1,0:T(8,128)}, u32[]{:S(2)}, u32[]{:S(2)}) collective-permute-start(f32[32,128,128]{2,1,0:T(8,128)} %get-tuple-element.6), channel_id=1, source_target_pairs={{1,0},{2,1},{3,2},{4,3},{5,4},{6,5},{7,6},{8,7},{9,8},{10,9},{11,1... | collective-permute-start | bytes 6291464 | tf_op jit(solution)/shard_map/ppermute | solution.py:12
  27.8 0.0 copy-done.1
  27.8 0.1 copy.10
  27.9 0.1 reshape.84
  28.0 0.1 reshape.83
  28.1 0.0 copy-done.2
  28.1 0.1 copy.9
  28.2 0.1 eq.15
  28.4 43.0 %collective-permute-done = f32[32,128,128]{2,1,0:T(8,128)} collective-permute-done((f32[32,128,128]{2,1,0:T(8,128)}, f32[32,128,128]{2,1,0:T(8,128)}, u32[]{:S(2)}, u32[]{:S(2)}) %collective-permute-start) | collective-permute-done | bytes 2097184 | tf_op jit(solution)/shard_map/ppermute | solution.py:12
  71.4 1.3 collective-permute-done.1
  72.8 0.0 copy-done
  72.8 5.1 %pad_maximum_fusion = f32[112,128,128]{2,1,0:T(8,128)} fusion(f32[32,128,128]{2,1,0:T(8,128)} %collective-permute-done.1, f32[32,128,128]{2,1,0:T(8,128)} %collective-permute-done, f32[48,128,128]{2,1,0:T(8,128)S(1)} %copy-done), kind=kLoop, calls=%fused_computation.6 | loop fusion | flops 3670016 | bytes 14680064 | tf_op jit(solution)/shard_map/concatenate | solution.py:25
  77.8 17.3 %gather_fusion.1 = f32[336,128,128]{2,1,0:T(8,128)} fusion(f32[112,128,128]{2,1,0:T(8,128)} %pad_maximum_fusion, s32[1024]{0:T(1024)S(1)} %pad_clamp_fusion), kind=kCustom, calls=%fused_computation.1 | custom fusion | bytes 44041536 | tf_op jit(solution)/shard_map/jit(_take)/gather | solution.py:26
  95.1 48.4 %fusion = f32[336,128,128]{2,1,0:T(8,128)} fusion(f32[336,128,128]{2,1,0:T(8,128)} %bitcast.20, f32[336,128,128]{2,1,0:T(8,128)} %gather_fusion.1, pred[336]{0:T(512)(128)(4,1)S(1)} %compare_and_fusion), kind=kOutput, calls=%fused_computation.2 | convolution fusion | flops 8461221888 | bytes 66060624 | tf_op jit(solution)/shard_map/qxy,qyc->qxc/dot_general | solution.py:28
  143.5 24.2 %fusion.4 = f32[48,7,128,128]{3,2,1,0:T(8,128)} fusion(f32[48,7,128,128]{2,3,1,0:T(8,128)} %bitcast.18, f32[48,128,128]{2,1,0:T(8,128)S(1)} %copy-done), kind=kOutput, calls=%fused_computation.8 | convolution fusion | flops 8455716864 | bytes 47185920 | tf_op jit(solution)/shard_map/ixa,ikxc->ikac/dot_general | solution.py:29
  167.8 21.8 %copy.13 = f32[336,128,128]{2,0,1:T(8,128)} copy(f32[336,128,128]{1,2,0:T(8,128)} %bitcast.19) | data formatting | bytes 44040192 | tf_op jit(solution)/shard_map/reshape | solution.py:35
  189.5 15.5 %fusion.7 = f32[128,128,128]{2,0,1:T(8,128)} fusion(f32[336,128,128]{2,0,1:T(8,128)} %copy.13, s32[336]{0:T(512)S(1)} %eq.15), kind=kOutput, calls=%fused_computation.12 | convolution fusion | flops 8455759872 | bytes 30410048 | tf_op jit(solution)/shard_map/sq,qac->sac/dot_general | solution.py:40
  205.1 0.0 all-reduce.2.cloned.1.call-update
  205.1 144.0 %all-reduce.2.cloned.1.call-done = f32[128,128,128]{2,0,1:T(8,128)} async-done(((f32[128,128,128]{2,0,1:T(8,128)}), f32[128,128,128]{2,0,1:T(8,128)}) %all-reduce.2.cloned.1.call-update) | async-done | bytes 8388624 | tf_op jit(solution)/shard_map/psum | solution.py:41
  349.0 11.6 %copy.14 = f32[128,128,128]{2,1,0:T(8,128)} copy(f32[128,128,128]{2,0,1:T(8,128)} %all-reduce.2.cloned.1.call-done) | data formatting | bytes 16777216 | tf_op jit(solution)/shard_map/psum | solution.py:41
  (5 shorter events, 0.0 us)
Async XLA Ops:
  6.5 342.5 %all-reduce.2.cloned.1.call-start = ((), (), s32[]{:S(2)}) async-start(), calls=%async_computation | async-start | bytes 16777216 | tf_op jit(solution)/shard_map/psum | solution.py:41
  12.9 14.9 %copy-start.1 = (s32[48,7]{0,1:T(8,128)S(1)}, s32[48,7]{0,1:T(8,128)}, u32[]{:S(2)}) copy-start(s32[48,7]{0,1:T(8,128)} %param.7) | copy-start | bytes 4036
  12.9 15.3 %copy-start.2 = (s32[48,7]{0,1:T(8,128)S(1)}, s32[48,7]{0,1:T(8,128)}, u32[]{:S(2)}) copy-start(s32[48,7]{0,1:T(8,128)} %param.9) | copy-start | bytes 4036
  12.9 59.9 %copy-start = (f32[48,128,128]{2,1,0:T(8,128)S(1)}, f32[48,128,128]{2,1,0:T(8,128)}, u32[]{:S(2)}) copy-start(f32[48,128,128]{2,1,0:T(8,128)} %param.5) | copy-start | bytes 9437188
  18.0 53.4 %collective-permute-start = (f32[32,128,128]{2,1,0:T(8,128)}, f32[32,128,128]{2,1,0:T(8,128)}, u32[]{:S(2)}, u32[]{:S(2)}) collective-permute-start(f32[32,128,128]{2,1,0:T(8,128)} %get-tuple-element.5), channel_id=1, source_target_pairs={{0,1},{1,2},{2,3},{3,4},{4,5},{5,6},{6,7},{7,8},{8,9},{9,10},{10,1... | collective-permute-start | bytes 6291464 | tf_op jit(solution)/shard_map/ppermute | solution.py:12
  21.5 51.3 %collective-permute-start.1 = (f32[32,128,128]{2,1,0:T(8,128)}, f32[32,128,128]{2,1,0:T(8,128)}, u32[]{:S(2)}, u32[]{:S(2)}) collective-permute-start(f32[32,128,128]{2,1,0:T(8,128)} %get-tuple-element.6), channel_id=1, source_target_pairs={{1,0},{2,1},{3,2},{4,3},{5,4},{6,5},{7,6},{8,7},{9,8},{10,9},{11,1... | collective-permute-start | bytes 6291464 | tf_op jit(solution)/shard_map/ppermute | solution.py:12
Sparse Core Ops, SparseCore 0:
  205.2 143.7 all-reduce.1
where the time goes:
time: 369 us; the launch traced here: 368 us
  waiting for transfers between devices  188 us (51%)
  matrix products  88.2 us (24%)
  local copies, waits for them, and re-layouts  58.5 us (16%)
  between operations  13.5 us (4%)
  starting transfers between devices  9.77 us (3%)
  other arithmetic  9.28 us (3%)
    psum x1, waiting for transfers between devices, shards(): operator = lax.psum(partial_op, 'bulk')  144 us
    dot_general x1, matrix products, shards(): jnp.einsum('qxy,qyc->qxc', couplings, right_tiles, precision=lax.Precisio...  48.4 us
    ppermute x2, waiting for transfers between devices, shifted(): return lax.ppermute(block, axis, route)  44.4 us
    dot_general x1, matrix products, shards(): jnp.einsum('ixa,ikxc->ikac', p_tiles, product.reshape(blocks, neighbours,...  24.2 us
    reshape x1, local copies, waits for them, and re-layouts, shards(): triple = triple.reshape(blocks * neighbours, coarse, coarse)  21.8 us
    gather x1, local copies, waits for them, and re-layouts, shards(): right_tiles = jnp.take(lookup_rows, col_ref.reshape(-1), axis=0)  17.3 us
    dot_general x1, matrix products, shards(): jnp.einsum('sq,qac->sac', selector, triple, precision=lax.Precision.HIGHEST)  15.5 us
    psum x1, local copies, waits for them, and re-layouts, shards(): operator = lax.psum(partial_op, 'bulk')  11.6 us
  transfers between devices with their start and end apart: 3, of which 3 were waited for; matrix products, arithmetic and copies ran while one was open for 0% of the time, Pallas kernels for 0%

commit v1 on v0

v1 whole, which is shorter than its diff:
```python
import functools

import jax
import jax.numpy as jnp
from jax import lax
from jax.experimental import pallas as pl
from jax.experimental.pallas import tpu as pltpu
from jax.sharding import PartitionSpec as P

F32 = jnp.float32
BF16 = jnp.bfloat16
SIDE = 4
MB = 1 << 20


def parts_of(x):
    high = x.astype(BF16)
    return high, (x - high.astype(F32)).astype(BF16)


def row_pair(x):
    return jnp.concatenate(parts_of(x), axis=1)


def column_pair(x):
    pair = row_pair(x)
    return jnp.concatenate([pair, pair], axis=0)


def fold(x):
    n = x.shape[1] // 2
    return x[:, :n] + x[:, n:]


def product(left_pair, right_pair):
    return fold(jnp.dot(left_pair, right_pair, preferred_element_type=F32))


def choose_kernel(send_ref, p_ref, low_ref, up_ref, held, sem):
    capacity = send_ref.shape[1]
    outs = ((0, low_ref), (1, up_ref))
    load = pltpu.make_async_copy(p_ref, held, sem.at[2])
    load.start()
    load.wait()

    @pl.loop(0, capacity)
    def _(j):
        for side, out in outs:
            tile = jnp.maximum(send_ref[side, j], 0)
            pltpu.make_async_copy(held.at[tile], out.at[j], sem.at[side]).start()

    for side, out in outs:
        pltpu.make_async_copy(held.at[pl.ds(0, capacity)], out, sem.at[side]).wait()


def choose(send, p_tiles):
    capacity = send.shape[1]
    tile = p_tiles.shape[1:]
    out = jax.ShapeDtypeStruct((capacity,) + tile, F32)
    return pl.pallas_call(
        choose_kernel,
        name="choose",
        out_shape=(out, out),
        in_specs=[pl.BlockSpec(memory_space=pltpu.SMEM), pl.BlockSpec(memory_space=pl.ANY)],
        out_specs=(pl.BlockSpec(memory_space=pl.ANY),) * 2,
        scratch_shapes=[pltpu.VMEM(p_tiles.shape, F32), pltpu.SemaphoreType.DMA((3,))],
        compiler_params=pltpu.CompilerParams(vmem_limit_bytes=16 * MB),
        cost_estimate=pl.CostEstimate(flops=0, bytes_accessed=4 * 32 * 65536, transcendentals=0),
    )(send, p_tiles)


BLOCKS = 4


def local_kernel(col_ref, target_ref, p_ref, a_ref, part_ref, left_ref, slot_ref, packed, total, left, sem):
    step = pl.program_id(0)
    blocks = p_ref.shape[0]
    slots = left_ref.shape[0] - 1
    spare = total.shape[0] - 1

    @pl.when(step == 0)
    def _():
        @pl.loop(0, blocks)
        def _(i):
            packed[i] = column_pair(p_ref[i])

        @pl.loop(0, spare + 1)
        def _(i):
            total[i] = jnp.zeros(total.shape[1:], F32)

        @pl.loop(0, slots)
        def _(i):
            slot_ref[i] = -1

    neighbours = a_ref.shape[1]
    for i in range(BLOCKS):
        f = step * BLOCKS + i
        rows = row_pair(p_ref[f].T)
        places = []
        for k in range(neighbours):
            v = col_ref[f * neighbours + k]
            t = target_ref[f * neighbours + k]
            remote = v >= blocks
            slot = jnp.where(remote, v - blocks, slots)
            slot_ref[slot] = t
            places.append((slot, jnp.where(remote, 0, v), jnp.where(remote, spare, t)))
        lefts = [product(rows, column_pair(a_ref[i, k])) for k in range(neighbours)]
        for w, (slot, _, _) in zip(lefts, places):
            left[slot] = w
        terms = [product(row_pair(w), packed[q]) for w, (_, q, _) in zip(lefts, places)]
        for term, (_, _, t) in zip(terms, places):
            total[t] += term

    @pl.when(step == pl.num_programs(0) - 1)
    def _():
        one = pltpu.make_async_copy(total, part_ref, sem.at[0])
        two = pltpu.make_async_copy(left, left_ref, sem.at[1])
        one.start()
        two.start()
        one.wait()
        two.wait()


def local_part(col, target, p_tiles, a_tiles, tiles, slots):
    blocks, bs, cw = p_tiles.shape
    neighbours = a_tiles.shape[1]
    part = jax.ShapeDtypeStruct((tiles + 1, cw, cw), F32)
    left = jax.ShapeDtypeStruct((slots + 1, cw, bs), F32)
    return pl.pallas_call(
        local_kernel,
        name="local_part",
        grid_spec=pltpu.PrefetchScalarGridSpec(
            num_scalar_prefetch=2,
            grid=(blocks // BLOCKS,),
            in_specs=[
                pl.BlockSpec((blocks, bs, cw), lambda f, *_: (0, 0, 0)),
                pl.BlockSpec((BLOCKS, neighbours, bs, bs), lambda f, *_: (f, 0, 0, 0)),
            ],
            out_specs=(
                pl.BlockSpec(memory_space=pl.ANY),
                pl.BlockSpec(memory_space=pl.ANY),
                pl.BlockSpec(memory_space=pltpu.SMEM),
            ),
            scratch_shapes=[
                pltpu.VMEM((blocks, 2 * bs, 2 * cw), BF16),
                pltpu.VMEM(part.shape, F32),
                pltpu.VMEM(left.shape, F32),
                pltpu.SemaphoreType.DMA((2,)),
            ],
        ),
        out_shape=(part, left, jax.ShapeDtypeStruct((slots + 8,), jnp.int32)),
        compiler_params=pltpu.CompilerParams(vmem_limit_bytes=44 * MB),
        cost_estimate=pl.CostEstimate(flops=24 * 10**9, bytes_accessed=36 * 10**6, transcendentals=0),
    )(col, target, p_tiles, a_tiles)


GROUP = 4


def remote_kernel(chunks, slot_ref, left_ref, lower_ref, upper_ref, part_ref, *rest):
    outs, (todo, total, held_left, held_right, sem, io_sem) = rest[: len(chunks)], rest[len(chunks) :]
    size = outs[0].shape[0]
    capacity = lower_ref.shape[0]
    spare = len(chunks) * size
    places = 2 * capacity + GROUP
    loads = [
        pltpu.make_async_copy(part_ref.at[pl.ds(c, size)], total.at[pl.ds(i * size, size)], io_sem.at[i])
        for i, c in enumerate(chunks)
    ]
    for load in loads:
        load.start()

    def find(j, n):
        t = slot_ref[j]
        place = jnp.int32(-1)
        for i, c in enumerate(chunks):
            place = jnp.where((t >= c) & (t < c + size), t - c + i * size, place)
        todo[n] = j
        todo[n + places] = place
        return n + (place >= 0).astype(jnp.int32)

    count = lax.fori_loop(0, 2 * capacity, find, jnp.int32(0))
    for i in range(GROUP):
        todo[count + i] = 0
        todo[count + i + places] = spare
    groups = (count + GROUP - 1) // GROUP

    def start(g):
        b = lax.rem(g, 2)
        for i in range(GROUP):
            j = todo[g * GROUP + i]
            pltpu.make_async_copy(left_ref.at[j], held_left.at[b, i], sem.at[0, b]).start()

            @pl.when(j < capacity)
            def _():
                pltpu.make_async_copy(lower_ref.at[j], held_right.at[b, i], sem.at[1, b]).start()

            @pl.when(j >= capacity)
            def _():
                pltpu.make_async_copy(upper_ref.at[j - capacity], held_right.at[b, i], sem.at[1, b]).start()

    @pl.when(groups > 0)
    def _():
        start(jnp.int32(0))

    for load in loads:
        load.wait()

    def step(g, carry):
        @pl.when(g + 1 < groups)
        def _():
            start(g + 1)

        b = lax.rem(g, 2)
        pltpu.make_async_copy(left_ref.at[pl.ds(0, GROUP)], held_left.at[b], sem.at[0, b]).wait()
        pltpu.make_async_copy(lower_ref.at[pl.ds(0, GROUP)], held_right.at[b], sem.at[1, b]).wait()
        terms = [product(row_pair(held_left[b, i]), column_pair(held_right[b, i])) for i in range(GROUP)]
        for i, term in enumerate(terms):
            total[todo[g * GROUP + i + places]] += term
        return carry

    lax.fori_loop(0, groups, step, 0)
    stores = [
        pltpu.make_async_copy(total.at[pl.ds(i * size, size)], out, io_sem.at[i]) for i, out in enumerate(outs)
    ]
    for store in stores:
        store.start()
    for store in stores:
        store.wait()


def remote_part(chunks, size, slots, left, lower, upper, part):
    tile = part.shape[1:]
    out = jax.ShapeDtypeStruct((size,) + tile, F32)
    n = len(chunks)
    anywhere = pl.BlockSpec(memory_space=pl.ANY)
    return pl.pallas_call(
        functools.partial(remote_kernel, chunks),
        name="remote_part",
        out_shape=(out,) * n,
        in_specs=[pl.BlockSpec(memory_space=pltpu.SMEM)] + [anywhere] * 4,
        out_specs=(anywhere,) * n,
        scratch_shapes=[
            pltpu.SMEM((4 * lower.shape[0] + 2 * GROUP,), jnp.int32),
            pltpu.VMEM((n * size + 1,) + tile, F32),
            pltpu.VMEM((2, GROUP) + tile, F32),
            pltpu.VMEM((2, GROUP) + tile, F32),
            pltpu.SemaphoreType.DMA((2, 2)),
            pltpu.SemaphoreType.DMA((n,)),
        ],
        compiler_params=pltpu.CompilerParams(vmem_limit_bytes=16 * MB),
        cost_estimate=pl.CostEstimate(flops=10**9, bytes_accessed=2 * n * size * 65536, transcendentals=0),
    )(slots, left, lower, upper, part)


def place_kernel(pieces, *refs):
    n = len(pieces)
    ins = refs[:n]
    out_ref, held, load_sem, store_sem = refs[-4:]
    at = lax.axis_index("bulk")
    x, y = at // SIDE, lax.rem(at, SIDE)
    quarter = 4
    loads, stores = [], []
    first = 0
    for ref, entries in zip(ins, pieces):
        loads.append(pltpu.make_async_copy(ref, held.at[pl.ds(first, ref.shape[0])], load_sem.at[len(loads)]))
        for i, (half, dx, dy) in enumerate(entries):
            where = half * 64 + lax.rem(x + dx, SIDE) * 16 + lax.rem(y + dy, SIDE) * quarter
            stores.append(
                pltpu.make_async_copy(
                    held.at[pl.ds(first + i * quarter, quarter)],
                    out_ref.at[pl.ds(where, quarter)],
                    store_sem.at[len(stores)],
                )
            )
        first += ref.shape[0]
    for load in loads:
        load.start()
    started = 0
    for load, entries in zip(loads, pieces):
        load.wait()
        for store in stores[started : started + len(entries)]:
            store.start()
        started += len(entries)
    for store in stores:
        store.wait()


def place(arrays, pieces, shape, out=None):
    anywhere = pl.BlockSpec(memory_space=pl.ANY)
    count = sum(len(entries) for entries in pieces)
    args = list(arrays) + ([] if out is None else [out])
    return pl.pallas_call(
        functools.partial(place_kernel, pieces),
        name="place",
        out_shape=jax.ShapeDtypeStruct(shape, F32),
        in_specs=[anywhere] * len(args),
        out_specs=anywhere,
        scratch_shapes=[
            pltpu.VMEM((count * 4,) + shape[1:], F32),
            pltpu.SemaphoreType.DMA((len(arrays),)),
            pltpu.SemaphoreType.DMA((count,)),
        ],
        compiler_params=pltpu.CompilerParams(vmem_limit_bytes=16 * MB),
        input_output_aliases={} if out is None else {len(arrays): 0},
        cost_estimate=pl.CostEstimate(flops=0, bytes_accessed=2 * count * 4 * 65536, transcendentals=0),
    )(*args)


def route(dx, dy):
    pairs = []
    for x in range(SIDE):
        for y in range(SIDE):
            pairs.append((x * SIDE + y, (x + dx) % SIDE * SIDE + (y + dy) % SIDE))
    return pairs


def push(block, axis, distance):
    dx, dy = (distance, 0) if axis == "x" else (0, distance)
    return lax.ppermute(block, "bulk", route(dx, dy))


def shifted(block, axis, distance):
    devices = range(lax.axis_size(axis))
    pairs = [(i - distance, i) for i in devices if i - distance in devices]
    return lax.ppermute(block, axis, pairs)


def shards(p_tiles, a_tiles, col_ref, send_list, coarse_tile):
    tiles = 128
    slots = 2 * send_list.shape[2]
    at = lax.axis_index("bulk")
    x, y = at // SIDE, at % SIDE
    second = coarse_tile // 64
    ahead_x = (coarse_tile // 16 - x) % SIDE
    ahead_y = (coarse_tile // 4 - y) % SIDE
    outer = jnp.where(second == 0, ahead_x, ahead_y)
    inner = jnp.where(second == 0, ahead_y, ahead_x)
    target = second * 64 + outer * 16 + inner * 4 + coarse_tile % 4

    to_lower, to_upper = choose(send_list[0], p_tiles)
    lower = shifted(to_upper, ("group", "bulk"), 1)
    upper = shifted(to_lower, ("group", "bulk"), -1)
    part, left, slot_tile = local_part(
        col_ref.reshape(-1), target.reshape(-1), p_tiles, a_tiles, tiles, slots
    )
    more = (slot_tile, left, lower, upper, part)
    far = remote_part((32, 40, 96, 104), 8, *more)
    near = remote_part((16, 24, 48, 56, 80, 88, 112, 120), 8, *more)
    here = remote_part((0, 8, 64, 72), 8, *more)

    axes = (("x", "y"), ("y", "x"))
    owned = []
    for half, (outer_axis, _) in enumerate(axes):
        far_a, far_b = far[2 * half : 2 * half + 2]
        up_a, up_b, down_a, down_b = near[4 * half : 4 * half + 4]
        here_a, here_b = here[2 * half : 2 * half + 2]
        first_up = push(far_a, outer_axis, 1)
        first_down = push(far_b, outer_axis, -1)
        second_up = push(up_b, outer_axis, 1)
        second_down = push(down_a, outer_axis, -1)
        third_up = push(up_a + first_up, outer_axis, 1)
        third_down = push(down_b + first_down, outer_axis, -1)
        owned.append((here_a + second_down + third_up, here_b + second_up + third_down))
    sums = []
    for half, (_, inner_axis) in enumerate(axes):
        one, two = owned[half]
        next_up = push(one[4:], inner_axis, 1)
        opposite = push(two[:4], inner_axis, 2)
        next_down = push(two[4:], inner_axis, -1)
        sums.append(one[:4] + next_up + opposite + next_down)
    gathered = []
    for half, (_, inner_axis) in enumerate(axes):
        own = sums[half]
        behind = push(own, inner_axis, 1)
        ahead = push(own, inner_axis, -1)
        opposite = push(own, inner_axis, 2)
        gathered.append((jnp.concatenate([own, ahead]), jnp.concatenate([opposite, behind])))
    early, early_pieces, late, late_pieces = [], [], [], []

    def entry(half, outer, inner):
        return (half, outer, inner) if half == 0 else (half, inner, outer)

    for half, (outer_axis, _) in enumerate(axes):
        one, two = gathered[half]
        behind_one = push(one, outer_axis, 1)
        ahead_two = push(two, outer_axis, -1)
        behind_two = push(two, outer_axis, 1)
        ahead_one = push(one, outer_axis, -1)
        far_one = push(behind_one, outer_axis, 1)
        far_two = push(ahead_two, outer_axis, -1)
        for arr, outer, inners in (
            (one, 0, (0, 1)),
            (two, 0, (2, 3)),
            (behind_one, 3, (0, 1)),
            (behind_two, 3, (2, 3)),
            (ahead_one, 1, (0, 1)),
            (ahead_two, 1, (2, 3)),
        ):
            early.append(arr)
            early_pieces.append([entry(half, outer, i) for i in inners])
        for arr, inners in ((far_one, (0, 1)), (far_two, (2, 3))):
            late.append(arr)
            late_pieces.append([entry(half, 2, i) for i in inners])
    shape = (tiles,) + p_tiles.shape[2:] * 2
    out = place(early, early_pieces, shape)
    return place(late, late_pieces, shape, out)


def solution(mesh):
    in_specs = (
        P(("group", "bulk"), None, None),
        P(("group", "bulk"), None, None, None),
        P(("group", "bulk"), None),
        P(("group", "bulk"), None, None),
        P(("group", "bulk"), None),
    )
    out_specs = P("group", None, None)
    return jax.shard_map(shards, mesh=mesh, in_specs=in_specs, out_specs=out_specs, check_vma=False)
```

time: 369 us -> 215 us (0.58)
  the two profiles are of different devices: /device:TPU:32 before, /device:TPU:72 now
where the time goes in v1:
time: 215 us; the launch traced here: 211 us
  waiting for transfers between devices  92.1 us (43%)
  starting transfers between devices  60.3 us (28%)
  Pallas kernels  47.5 us (22%)
  local copies, waits for them, and re-layouts  9.14 us (4%)
    ppermute x36, waiting for transfers between devices, push(): return lax.ppermute(block, 'bulk', route(dx, dy))  73.3 us
    ppermute x36, starting transfers between devices, push(): return lax.ppermute(block, 'bulk', route(dx, dy))  54.5 us
    pallas_call x1, Pallas kernels, local_part(): pl.pallas_call(local_kernel, name='local_part', grid_spec=pltpu.PrefetchS...  24.4 us
    ppermute x2, waiting for transfers between devices, shifted(): return lax.ppermute(block, axis, pairs)  18.8 us
    pallas_call x3, Pallas kernels, remote_part(): pl.pallas_call(functools.partial(remote_kernel, chunks), name='remote_par...  15.4 us
    unnamed x11, local copies, waits for them, and re-layouts  8.67 us
    ppermute x2, starting transfers between devices, shifted(): return lax.ppermute(block, axis, pairs)  5.84 us
    pallas_call x2, Pallas kernels, place(): pl.pallas_call(functools.partial(place_kernel, pieces), name='place', out...  4.93 us
  transfers between devices with their start and end apart: 38, of which 17 were waited for; matrix products, arithmetic and copies ran while one was open for 1% of the time, Pallas kernels for 18%

profile of v1, /device:TPU:72, one launch (start us, length us, event | category | flops | bytes accessed | tf_op | source)
XLA Modules:
  0.0 211.2 jit_solution(17188790026481109163)
XLA Ops:
  2.6 2.7 %choose.1 = (f32[32,128,128]{2,1,0:T(8,128)}, f32[32,128,128]{2,1,0:T(8,128)}) custom-call(s32[2,32]{1,0:T(2,128)S(1)} %bitcast.1, f32[48,128,128]{2,1,0:T(8,128)S(1)} %copy-done.1), custom_call_target="tpu_custom_call" | custom-call | bytes 8388608 | tf_op jit(solution)/shard_map/choose/pallas_call | solution.py:60
  5.3 3.5 %collective-permute-start = (f32[32,128,128]{2,1,0:T(8,128)}, f32[32,128,128]{2,1,0:T(8,128)S(1)}, u32[]{:S(2)}, u32[]{:S(2)}) collective-permute-start(f32[32,128,128]{2,1,0:T(8,128)} %get-tuple-element.28), channel_id=1, source_target_pairs={{0,1},{1,2},{2,3},{3,4},{4,5},{5,6},{6,7},{7,8},{8,9},{9,10},{10,1... | collective-permute-start | bytes 6291464 | tf_op jit(solution)/shard_map/ppermute | solution.py:326
  14.9 24.4 %local_part.1 = (f32[129,128,128]{2,1,0:T(8,128)}, f32[65,128,128]{2,1,0:T(8,128)S(1)}, s32[72]{0:T(128)S(1)}) custom-call(s32[336]{0:T(512)S(1)} %reshape.6.col_ref, s32[336]{0:T(512)S(1)} %reshape.7.target_ref, f32[48,128,128]{2,1,0:T(8,128)S(1)} %copy-done.2, f32[48,7,128,128]{3,2,1,0:T(8,128)} %a_ref.1), custom_call_target="tpu_custom_call" | custom-call | flops 24000000000 | bytes 36000000 | tf_op jit(solution)/shard_map/local_part/pallas_call | solution.py:129
  39.3 15.5 %collective-permute-done.lower_ref = f32[32,128,128]{2,1,0:T(8,128)S(1)} collective-permute-done((f32[32,128,128]{2,1,0:T(8,128)}, f32[32,128,128]{2,1,0:T(8,128)S(1)}, u32[]{:S(2)}, u32[]{:S(2)}) %collective-permute-start) | collective-permute-done | bytes 2097184 | tf_op jit(solution)/shard_map/ppermute | solution.py:326
  54.8 3.3 %collective-permute-done.1.upper_ref = f32[32,128,128]{2,1,0:T(8,128)} collective-permute-done((f32[32,128,128]{2,1,0:T(8,128)}, f32[32,128,128]{2,1,0:T(8,128)}, u32[]{:S(2)}, u32[]{:S(2)}) %collective-permute-start.1) | collective-permute-done | bytes 2097184 | tf_op jit(solution)/shard_map/ppermute | solution.py:326
  58.1 3.4 %copy-done = f32[129,128,128]{2,1,0:T(8,128)S(1)} copy-done((f32[129,128,128]{2,1,0:T(8,128)S(1)}, f32[129,128,128]{2,1,0:T(8,128)}, u32[]{:S(2)}) %copy-start) | copy-done | bytes 8454168
  61.5 4.5 %remote_part.5 = (f32[8,128,128]{2,1,0:T(8,128)S(1)}, f32[8,128,128]{2,1,0:T(8,128)S(1)}, f32[8,128,128]{2,1,0:T(8,128)S(1)}, f32[8,128,128]{2,1,0:T(8,128)S(1)}) custom-call(s32[72]{0:T(128)S(1)} %get-tuple-element.26.slot_ref, f32[65,128,128]{2,1,0:T(8,128)S(1)} %get-tuple-element.27.left_ref, f32[32,128,128]{2,1,0:T(8,128)S(1)} %collective-permute-done.lower_ref, ...), custom_call_target="tpu_custom_call" | custom-call | flops 1000000000 | bytes 4194304 | tf_op jit(solution)/shard_map/remote_part/pallas_call | solution.py:237
  66.0 2.5 %collective-permute-start.19 = (f32[8,128,128]{2,1,0:T(8,128)S(1)}, f32[8,128,128]{2,1,0:T(8,128)S(1)}, u32[]{:S(2)}, u32[]{:S(2)}) collective-permute-start(f32[8,128,128]{2,1,0:T(8,128)S(1)} %get-tuple-element.42), channel_id=1, source_target_pairs={{0,1},{1,2},{2,3},{3,0},{4,5},{5,6},{6,7},{7,4},{8,9},{9,10},{10,1... | collective-permute-start | bytes 1572872 | tf_op jit(solution)/shard_map/ppermute | solution.py:320
  69.7 3.2 %collective-permute-start.7 = (f32[8,128,128]{2,1,0:T(8,128)S(1)}, f32[8,128,128]{2,1,0:T(8,128)S(1)}, u32[]{:S(2)}, u32[]{:S(2)}) collective-permute-start(f32[8,128,128]{2,1,0:T(8,128)S(1)} %get-tuple-element.38), channel_id=1, source_target_pairs={{0,12},{1,13},{2,14},{3,15},{4,0},{5,1},{6,2},{7,3},{8,4},{9,5},{1... | collective-permute-start | bytes 1572872 | tf_op jit(solution)/shard_map/ppermute | solution.py:320
  72.9 7.6 %remote_part.4 = (f32[8,128,128]{2,1,0:T(8,128)S(1)}, f32[8,128,128]{2,1,0:T(8,128)S(1)}, f32[8,128,128]{2,1,0:T(8,128)S(1)}, f32[8,128,128]{2,1,0:T(8,128)S(1)}...) custom-call(s32[72]{0:T(128)S(1)} %get-tuple-element.26.slot_ref, ...), custom_call_target="tpu_custom_call" | custom-call | flops 1000000000 | bytes 8388608 | tf_op jit(solution)/shard_map/remote_part/pallas_call | solution.py:237
  80.5 4.2 %collective-permute-start.18 = (f32[8,128,128]{2,1,0:T(8,128)S(1)}, f32[8,128,128]{2,1,0:T(8,128)S(1)}, u32[]{:S(2)}, u32[]{:S(2)}) collective-permute-start(f32[8,128,128]{2,1,0:T(8,128)S(1)} %get-tuple-element.40), channel_id=1, source_target_pairs={{0,3},{1,0},{2,1},{3,2},{4,7},{5,4},{6,5},{7,6},{8,11},{9,8},{10,9... | collective-permute-start | bytes 1572872 | tf_op jit(solution)/shard_map/ppermute | solution.py:320
  87.6 3.3 %remote_part.3 = (f32[8,128,128]{2,1,0:T(8,128)S(1)}, f32[8,128,128]{2,1,0:T(8,128)S(1)}, f32[8,128,128]{2,1,0:T(8,128)S(1)}, f32[8,128,128]{2,1,0:T(8,128)S(1)}) custom-call(s32[72]{0:T(128)S(1)} %get-tuple-element.26.slot_ref, f32[65,128,128]{2,1,0:T(8,128)S(1)} %get-tuple-element.27.left_ref, f32[32,128,128]{2,1,0:T(8,128)S(1)} %collective-permute-done.lower_ref, ...), custom_call_target="tpu_custom_call" | custom-call | flops 1000000000 | bytes 4194304 | tf_op jit(solution)/shard_map/remote_part/pallas_call | solution.py:237
  91.0 2.8 %collective-permute-start.2 = (f32[8,128,128]{2,1,0:T(8,128)S(1)}, f32[8,128,128]{2,1,0:T(8,128)S(1)}, u32[]{:S(2)}, u32[]{:S(2)}) collective-permute-start(f32[8,128,128]{2,1,0:T(8,128)S(1)} %get-tuple-element.32), channel_id=1, source_target_pairs={{0,12},{1,13},{2,14},{3,15},{4,0},{5,1},{6,2},{7,3},{8,4},{9,5},{1... | collective-permute-start | bytes 1572872 | tf_op jit(solution)/shard_map/ppermute | solution.py:320
  93.9 3.2 %collective-permute-done.18 = f32[8,128,128]{2,1,0:T(8,128)S(1)} collective-permute-done((f32[8,128,128]{2,1,0:T(8,128)S(1)}, f32[8,128,128]{2,1,0:T(8,128)S(1)}, u32[]{:S(2)}, u32[]{:S(2)}) %collective-permute-start.18) | collective-permute-done | bytes 524320 | tf_op jit(solution)/shard_map/ppermute | solution.py:320
  97.1 2.6 %collective-permute-done.20 = f32[8,128,128]{2,1,0:T(8,128)S(1)} collective-permute-done((f32[8,128,128]{2,1,0:T(8,128)S(1)}, f32[8,128,128]{2,1,0:T(8,128)S(1)}, u32[]{:S(2)}, u32[]{:S(2)}) %collective-permute-start.20) | collective-permute-done | bytes 524320 | tf_op jit(solution)/shard_map/ppermute | solution.py:320
  99.9 9.2 %collective-permute-done.22 = f32[8,128,128]{2,1,0:T(8,128)S(1)} collective-permute-done((f32[8,128,128]{2,1,0:T(8,128)S(1)}, f32[8,128,128]{2,1,0:T(8,128)S(1)}, u32[]{:S(2)}, u32[]{:S(2)}) %collective-permute-start.22) | collective-permute-done | bytes 524320 | tf_op jit(solution)/shard_map/ppermute | solution.py:320
  112.8 10.7 %collective-permute-done.4 = f32[8,128,128]{2,1,0:T(8,128)S(1)} collective-permute-done((f32[8,128,128]{2,1,0:T(8,128)S(1)}, f32[8,128,128]{2,1,0:T(8,128)S(1)}, u32[]{:S(2)}, u32[]{:S(2)}) %collective-permute-start.4) | collective-permute-done | bytes 524320 | tf_op jit(solution)/shard_map/ppermute | solution.py:320
  125.2 3.1 %collective-permute-done.8 = f32[8,128,128]{2,1,0:T(8,128)S(1)} collective-permute-done((f32[8,128,128]{2,1,0:T(8,128)S(1)}, f32[8,128,128]{2,1,0:T(8,128)S(1)}, u32[]{:S(2)}, u32[]{:S(2)}) %collective-permute-start.8) | collective-permute-done | bytes 524320 | tf_op jit(solution)/shard_map/ppermute | solution.py:320
  128.5 3.1 %collective-permute-start.10 = (f32[4,128,128]{2,1,0:T(8,128)S(1)}, f32[4,128,128]{2,1,0:T(8,128)S(1)}, u32[]{:S(2)}, u32[]{:S(2)}) collective-permute-start(f32[4,128,128]{2,1,0:T(8,128)S(1)} %get-tuple-element.50), channel_id=1, source_target_pairs={{0,3},{1,0},{2,1},{3,2},{4,7},{5,4},{6,5},{7,6},{8,11},{9,8},{10,9... | collective-permute-start | bytes 786440 | tf_op jit(solution)/shard_map/ppermute | solution.py:320
  131.5 5.6 %collective-permute-start.9 = (f32[4,128,128]{2,1,0:T(8,128)S(1)}, f32[4,128,128]{2,1,0:T(8,128)S(1)}, u32[]{:S(2)}, u32[]{:S(2)}) collective-permute-start(f32[4,128,128]{2,1,0:T(8,128)S(1)} %get-tuple-element.49), channel_id=1, source_target_pairs={{0,2},{1,3},{2,0},{3,1},{4,6},{5,7},{6,4},{7,5},{8,10},{9,11},{10,... | collective-permute-start | bytes 786440 | tf_op jit(solution)/shard_map/ppermute | solution.py:320
  138.1 2.5 %collective-permute-start.27 = (f32[4,128,128]{2,1,0:T(8,128)S(1)}, f32[4,128,128]{2,1,0:T(8,128)S(1)}, u32[]{:S(2)}, u32[]{:S(2)}) collective-permute-start(f32[4,128,128]{2,1,0:T(8,128)S(1)} %fusion.1), channel_id=1, source_target_pairs={{0,12},{1,13},{2,14},{3,15},{4,0},{5,1},{6,2},{7,3},{8,4},{9,5},{1... | collective-permute-start | bytes 786440 | tf_op jit(solution)/shard_map/ppermute | solution.py:320
  142.4 4.1 %collective-permute-start.14 = (f32[4,128,128]{2,1,0:T(8,128)S(1)}, f32[4,128,128]{2,1,0:T(8,128)S(1)}, u32[]{:S(2)}, u32[]{:S(2)}) collective-permute-start(f32[4,128,128]{2,1,0:T(8,128)S(1)} %fusion.3), channel_id=1, source_target_pairs={{0,2},{1,3},{2,0},{3,1},{4,6},{5,7},{6,4},{7,5},{8,10},{9,11},{10,... | collective-permute-start | bytes 786440 | tf_op jit(solution)/shard_map/ppermute | solution.py:320
  148.1 3.0 %collective-permute-start.32 = (f32[8,128,128]{2,1,0:T(8,128)S(1)}, f32[8,128,128]{2,1,0:T(8,128)S(1)}, u32[]{:S(2)}, u32[]{:S(2)}) collective-permute-start(f32[8,128,128]{2,1,0:T(8,128)S(1)} %constant_dynamic-update-slice_fusion.2.refs_7_), channel_id=1, source_target_pairs={{0,3},{1,0},{2,1},{3,2},{4,7},{5,4},{6,5},{7,6},{8,11},{9,8},{10,9... | collective-permute-start | bytes 1572872 | tf_op jit(solution)/shard_map/ppermute | solution.py:320
  153.3 2.5 %collective-permute-start.28 = (f32[8,128,128]{2,1,0:T(8,128)S(1)}, f32[8,128,128]{2,1,0:T(8,128)S(1)}, u32[]{:S(2)}, u32[]{:S(2)}) collective-permute-start(f32[8,128,128]{2,1,0:T(8,128)S(1)} %pad_maximum_fusion.1.refs_6_), channel_id=1, source_target_pairs={{0,1},{1,2},{2,3},{3,0},{4,5},{5,6},{6,7},{7,4},{8,9},{9,10},{10,1... | collective-permute-start | bytes 1572872 | tf_op jit(solution)/shard_map/ppermute | solution.py:320
  155.8 15.8 %collective-permute-done.15 = f32[4,128,128]{2,1,0:T(8,128)S(1)} collective-permute-done((f32[4,128,128]{2,1,0:T(8,128)S(1)}, f32[4,128,128]{2,1,0:T(8,128)S(1)}, u32[]{:S(2)}, u32[]{:S(2)}) %collective-permute-start.15) | collective-permute-done | bytes 262176 | tf_op jit(solution)/shard_map/ppermute | solution.py:320
  171.6 3.1 %collective-permute-start.37 = (f32[8,128,128]{2,1,0:T(8,128)S(1)}, f32[8,128,128]{2,1,0:T(8,128)S(1)}, u32[]{:S(2)}, u32[]{:S(2)}) collective-permute-start(f32[8,128,128]{2,1,0:T(8,128)S(1)} %pad_maximum_fusion.1.refs_6_), channel_id=1, source_target_pairs={{0,3},{1,0},{2,1},{3,2},{4,7},{5,4},{6,5},{7,6},{8,11},{9,8},{10,9... | collective-permute-start | bytes 1572872 | tf_op jit(solution)/shard_map/ppermute | solution.py:320
  177.0 4.5 %collective-permute-done.28.refs_8_ = f32[8,128,128]{2,1,0:T(8,128)S(1)} collective-permute-done((f32[8,128,128]{2,1,0:T(8,128)S(1)}, f32[8,128,128]{2,1,0:T(8,128)S(1)}, u32[]{:S(2)}, u32[]{:S(2)}) %collective-permute-start.28) | collective-permute-done | bytes 524320 | tf_op jit(solution)/shard_map/ppermute | solution.py:320
  183.2 2.5 %collective-permute-start.33 = (f32[8,128,128]{2,1,0:T(8,128)S(1)}, f32[8,128,128]{2,1,0:T(8,128)S(1)}, u32[]{:S(2)}, u32[]{:S(2)}) collective-permute-start(f32[8,128,128]{2,1,0:T(8,128)S(1)} %collective-permute-done.32.refs_11_), channel_id=1, source_target_pairs={{0,3},{1,0},{2,1},{3,2},{4,7},{5,4},{6,5},{7,6},{8,11},{9,8},{10,9... | collective-permute-start | bytes 1572872 | tf_op jit(solution)/shard_map/ppermute | solution.py:320
  187.9 4.0 %collective-permute-done.34.refs_3_ = f32[8,128,128]{2,1,0:T(8,128)S(1)} collective-permute-done((f32[8,128,128]{2,1,0:T(8,128)S(1)}, f32[8,128,128]{2,1,0:T(8,128)S(1)}, u32[]{:S(2)}, u32[]{:S(2)}) %collective-permute-start.34) | collective-permute-done | bytes 524320 | tf_op jit(solution)/shard_map/ppermute | solution.py:320
  191.8 7.2 %collective-permute-done.12.refs_2_ = f32[8,128,128]{2,1,0:T(8,128)S(1)} collective-permute-done((f32[8,128,128]{2,1,0:T(8,128)S(1)}, f32[8,128,128]{2,1,0:T(8,128)S(1)}, u32[]{:S(2)}, u32[]{:S(2)}) %collective-permute-start.12) | collective-permute-done | bytes 524320 | tf_op jit(solution)/shard_map/ppermute | solution.py:320
  200.3 3.4 %place.2.refs_4_ = f32[128,128,128]{2,1,0:T(8,128)} custom-call(f32[8,128,128]{2,1,0:T(8,128)S(1)} %pad_maximum_fusion.refs_0_, f32[8,128,128]{2,1,0:T(8,128)S(1)} %constant_dynamic-update-slice_fusion.refs_1_, f32[8,128,128]{2,1,0:T(8,128)S(1)} %collective-permute-done.12.refs_2_, f32[8,128,128]{2,1,0:T(8,128)S(1)} %collective-permute-done.34.refs_3_, ...), custom_call_target="tpu_custom_call" | custom-call | bytes 12582912 | tf_op jit(solution)/shard_map/place/pallas_call | solution.py:293
  203.7 4.2 %collective-permute-done.17.refs_1_ = f32[8,128,128]{2,1,0:T(8,128)S(1)} collective-permute-done((f32[8,128,128]{2,1,0:T(8,128)S(1)}, f32[8,128,128]{2,1,0:T(8,128)S(1)}, u32[]{:S(2)}, u32[]{:S(2)}) %collective-permute-start.17) | collective-permute-done | bytes 524320 | tf_op jit(solution)/shard_map/ppermute | solution.py:320
  (84 shorter events, 35.4 us)
Async XLA Ops:
  5.3 49.5 %collective-permute-start = (f32[32,128,128]{2,1,0:T(8,128)}, f32[32,128,128]{2,1,0:T(8,128)S(1)}, u32[]{:S(2)}, u32[]{:S(2)}) collective-permute-start(f32[32,128,128]{2,1,0:T(8,128)} %get-tuple-element.28), channel_id=1, source_target_pairs={{0,1},{1,2},{2,3},{3,4},{4,5},{5,6},{6,7},{7,8},{8,9},{9,10},{10,1... | collective-permute-start | bytes 6291464 | tf_op jit(solution)/shard_map/ppermute | solution.py:326
  8.8 49.3 %collective-permute-start.1 = (f32[32,128,128]{2,1,0:T(8,128)}, f32[32,128,128]{2,1,0:T(8,128)}, u32[]{:S(2)}, u32[]{:S(2)}) collective-permute-start(f32[32,128,128]{2,1,0:T(8,128)} %get-tuple-element.29), channel_id=1, source_target_pairs={{1,0},{2,1},{3,2},{4,3},{5,4},{6,5},{7,6},{8,7},{9,8},{10,9},{11,1... | collective-permute-start | bytes 6291464 | tf_op jit(solution)/shard_map/ppermute | solution.py:326
  66.0 18.8 %collective-permute-start.19 = (f32[8,128,128]{2,1,0:T(8,128)S(1)}, f32[8,128,128]{2,1,0:T(8,128)S(1)}, u32[]{:S(2)}, u32[]{:S(2)}) collective-permute-start(f32[8,128,128]{2,1,0:T(8,128)S(1)} %get-tuple-element.42), channel_id=1, source_target_pairs={{0,1},{1,2},{2,3},{3,0},{4,5},{5,6},{6,7},{7,4},{8,9},{9,10},{10,1... | collective-permute-start | bytes 1572872 | tf_op jit(solution)/shard_map/ppermute | solution.py:320
  68.5 16.4 %collective-permute-start.23 = (f32[8,128,128]{2,1,0:T(8,128)S(1)}, f32[8,128,128]{2,1,0:T(8,128)S(1)}, u32[]{:S(2)}, u32[]{:S(2)}) collective-permute-start(f32[8,128,128]{2,1,0:T(8,128)S(1)} %get-tuple-element.46), channel_id=1, source_target_pairs={{0,3},{1,0},{2,1},{3,2},{4,7},{5,4},{6,5},{7,6},{8,11},{9,8},{10,9... | collective-permute-start | bytes 1572872 | tf_op jit(solution)/shard_map/ppermute | solution.py:320
  69.7 15.4 %collective-permute-start.3 = (f32[8,128,128]{2,1,0:T(8,128)S(1)}, f32[8,128,128]{2,1,0:T(8,128)S(1)}, u32[]{:S(2)}, u32[]{:S(2)}) collective-permute-start(f32[8,128,128]{2,1,0:T(8,128)S(1)} %get-tuple-element.34), channel_id=1, source_target_pairs={{0,4},{1,5},{2,6},{3,7},{4,8},{5,9},{6,10},{7,11},{8,12},{9,13},{1... | collective-permute-start | bytes 1572872 | tf_op jit(solution)/shard_map/ppermute | solution.py:320
  69.7 21.3 %collective-permute-start.7 = (f32[8,128,128]{2,1,0:T(8,128)S(1)}, f32[8,128,128]{2,1,0:T(8,128)S(1)}, u32[]{:S(2)}, u32[]{:S(2)}) collective-permute-start(f32[8,128,128]{2,1,0:T(8,128)S(1)} %get-tuple-element.38), channel_id=1, source_target_pairs={{0,12},{1,13},{2,14},{3,15},{4,0},{5,1},{6,2},{7,3},{8,4},{9,5},{1... | collective-permute-start | bytes 1572872 | tf_op jit(solution)/shard_map/ppermute | solution.py:320
  80.5 16.6 %collective-permute-start.18 = (f32[8,128,128]{2,1,0:T(8,128)S(1)}, f32[8,128,128]{2,1,0:T(8,128)S(1)}, u32[]{:S(2)}, u32[]{:S(2)}) collective-permute-start(f32[8,128,128]{2,1,0:T(8,128)S(1)} %get-tuple-element.40), channel_id=1, source_target_pairs={{0,3},{1,0},{2,1},{3,2},{4,7},{5,4},{6,5},{7,6},{8,11},{9,8},{10,9... | collective-permute-start | bytes 1572872 | tf_op jit(solution)/shard_map/ppermute | solution.py:320
  84.8 14.9 %collective-permute-start.20 = (f32[8,128,128]{2,1,0:T(8,128)S(1)}, f32[8,128,128]{2,1,0:T(8,128)S(1)}, u32[]{:S(2)}, u32[]{:S(2)}) collective-permute-start(f32[8,128,128]{2,1,0:T(8,128)S(1)} %add.102), channel_id=1, source_target_pairs={{0,1},{1,2},{2,3},{3,0},{4,5},{5,6},{6,7},{7,4},{8,9},{9,10},{10,1... | collective-permute-start | bytes 1572872 | tf_op jit(solution)/shard_map/ppermute | solution.py:320
  84.9 24.2 %collective-permute-start.22 = (f32[8,128,128]{2,1,0:T(8,128)S(1)}, f32[8,128,128]{2,1,0:T(8,128)S(1)}, u32[]{:S(2)}, u32[]{:S(2)}) collective-permute-start(f32[8,128,128]{2,1,0:T(8,128)S(1)} %get-tuple-element.44), channel_id=1, source_target_pairs={{0,1},{1,2},{2,3},{3,0},{4,5},{5,6},{6,7},{7,4},{8,9},{9,10},{10,1... | collective-permute-start | bytes 1572872 | tf_op jit(solution)/shard_map/ppermute | solution.py:320
  85.1 25.7 %collective-permute-start.24 = (f32[8,128,128]{2,1,0:T(8,128)S(1)}, f32[8,128,128]{2,1,0:T(8,128)S(1)}, u32[]{:S(2)}, u32[]{:S(2)}) collective-permute-start(f32[8,128,128]{2,1,0:T(8,128)S(1)} %add.106), channel_id=1, source_target_pairs={{0,3},{1,0},{2,1},{3,2},{4,7},{5,4},{6,5},{7,6},{8,11},{9,8},{10,9... | collective-permute-start | bytes 1572872 | tf_op jit(solution)/shard_map/ppermute | solution.py:320
  91.0 20.3 %collective-permute-start.2 = (f32[8,128,128]{2,1,0:T(8,128)S(1)}, f32[8,128,128]{2,1,0:T(8,128)S(1)}, u32[]{:S(2)}, u32[]{:S(2)}) collective-permute-start(f32[8,128,128]{2,1,0:T(8,128)S(1)} %get-tuple-element.32), channel_id=1, source_target_pairs={{0,12},{1,13},{2,14},{3,15},{4,0},{5,1},{6,2},{7,3},{8,4},{9,5},{1... | collective-permute-start | bytes 1572872 | tf_op jit(solution)/shard_map/ppermute | solution.py:320
  97.1 28.0 %collective-permute-start.6 = (f32[8,128,128]{2,1,0:T(8,128)S(1)}, f32[8,128,128]{2,1,0:T(8,128)S(1)}, u32[]{:S(2)}, u32[]{:S(2)}) collective-permute-start(f32[8,128,128]{2,1,0:T(8,128)S(1)} %get-tuple-element.36), channel_id=1, source_target_pairs={{0,4},{1,5},{2,6},{3,7},{4,8},{5,9},{6,10},{7,11},{8,12},{9,13},{1... | collective-permute-start | bytes 1572872 | tf_op jit(solution)/shard_map/ppermute | solution.py:320
  99.7 23.7 %collective-permute-start.4 = (f32[8,128,128]{2,1,0:T(8,128)S(1)}, f32[8,128,128]{2,1,0:T(8,128)S(1)}, u32[]{:S(2)}, u32[]{:S(2)}) collective-permute-start(f32[8,128,128]{2,1,0:T(8,128)S(1)} %add.93), channel_id=1, source_target_pairs={{0,4},{1,5},{2,6},{3,7},{4,8},{5,9},{6,10},{7,11},{8,12},{9,13},{1... | collective-permute-start | bytes 1572872 | tf_op jit(solution)/shard_map/ppermute | solution.py:320
  109.1 19.2 %collective-permute-start.8 = (f32[8,128,128]{2,1,0:T(8,128)S(1)}, f32[8,128,128]{2,1,0:T(8,128)S(1)}, u32[]{:S(2)}, u32[]{:S(2)}) collective-permute-start(f32[8,128,128]{2,1,0:T(8,128)S(1)} %add.97), channel_id=1, source_target_pairs={{0,12},{1,13},{2,14},{3,15},{4,0},{5,1},{6,2},{7,3},{8,4},{9,5},{1... | collective-permute-start | bytes 1572872 | tf_op jit(solution)/shard_map/ppermute | solution.py:320
  110.8 20.8 %collective-permute-start.21 = (f32[4,128,128]{2,1,0:T(8,128)S(1)}, f32[4,128,128]{2,1,0:T(8,128)S(1)}, u32[]{:S(2)}, u32[]{:S(2)}) collective-permute-start(f32[4,128,128]{2,1,0:T(8,128)S(1)} %slice.37), channel_id=1, source_target_pairs={{0,4},{1,5},{2,6},{3,7},{4,8},{5,9},{6,10},{7,11},{8,12},{9,13},{1... | collective-permute-start | bytes 786440 | tf_op jit(solution)/shard_map/ppermute | solution.py:320
  111.3 25.8 %collective-permute-start.25 = (f32[4,128,128]{2,1,0:T(8,128)S(1)}, f32[4,128,128]{2,1,0:T(8,128)S(1)}, u32[]{:S(2)}, u32[]{:S(2)}) collective-permute-start(f32[4,128,128]{2,1,0:T(8,128)S(1)} %get-tuple-element.47), channel_id=1, source_target_pairs={{0,8},{1,9},{2,10},{3,11},{4,12},{5,13},{6,14},{7,15},{8,0},{9,1},... | collective-permute-start | bytes 786440 | tf_op jit(solution)/shard_map/ppermute | solution.py:320
  123.5 13.7 %collective-permute-start.26 = (f32[4,128,128]{2,1,0:T(8,128)S(1)}, f32[4,128,128]{2,1,0:T(8,128)S(1)}, u32[]{:S(2)}, u32[]{:S(2)}) collective-permute-start(f32[4,128,128]{2,1,0:T(8,128)S(1)} %get-tuple-element.48), channel_id=1, source_target_pairs={{0,12},{1,13},{2,14},{3,15},{4,0},{5,1},{6,2},{7,3},{8,4},{9,5},{1... | collective-permute-start | bytes 786440 | tf_op jit(solution)/shard_map/ppermute | solution.py:320
  125.1 13.0 %collective-permute-start.5 = (f32[4,128,128]{2,1,0:T(8,128)S(1)}, f32[4,128,128]{2,1,0:T(8,128)S(1)}, u32[]{:S(2)}, u32[]{:S(2)}) collective-permute-start(f32[4,128,128]{2,1,0:T(8,128)S(1)} %slice.33), channel_id=1, source_target_pairs={{0,1},{1,2},{2,3},{3,0},{4,5},{5,6},{6,7},{7,4},{8,9},{9,10},{10,1... | collective-permute-start | bytes 786440 | tf_op jit(solution)/shard_map/ppermute | solution.py:320
  128.5 12.1 %collective-permute-start.10 = (f32[4,128,128]{2,1,0:T(8,128)S(1)}, f32[4,128,128]{2,1,0:T(8,128)S(1)}, u32[]{:S(2)}, u32[]{:S(2)}) collective-permute-start(f32[4,128,128]{2,1,0:T(8,128)S(1)} %get-tuple-element.50), channel_id=1, source_target_pairs={{0,3},{1,0},{2,1},{3,2},{4,7},{5,4},{6,5},{7,6},{8,11},{9,8},{10,9... | collective-permute-start | bytes 786440 | tf_op jit(solution)/shard_map/ppermute | solution.py:320
  138.1 14.4 %collective-permute-start.27 = (f32[4,128,128]{2,1,0:T(8,128)S(1)}, f32[4,128,128]{2,1,0:T(8,128)S(1)}, u32[]{:S(2)}, u32[]{:S(2)}) collective-permute-start(f32[4,128,128]{2,1,0:T(8,128)S(1)} %fusion.1), channel_id=1, source_target_pairs={{0,12},{1,13},{2,14},{3,15},{4,0},{5,1},{6,2},{7,3},{8,4},{9,5},{1... | collective-permute-start | bytes 786440 | tf_op jit(solution)/shard_map/ppermute | solution.py:320
  148.1 27.6 %collective-permute-start.32 = (f32[8,128,128]{2,1,0:T(8,128)S(1)}, f32[8,128,128]{2,1,0:T(8,128)S(1)}, u32[]{:S(2)}, u32[]{:S(2)}) collective-permute-start(f32[8,128,128]{2,1,0:T(8,128)S(1)} %constant_dynamic-update-slice_fusion.2.refs_7_), channel_id=1, source_target_pairs={{0,3},{1,0},{2,1},{3,2},{4,7},{5,4},{6,5},{7,6},{8,11},{9,8},{10,9... | collective-permute-start | bytes 1572872 | tf_op jit(solution)/shard_map/ppermute | solution.py:320
  151.1 25.8 %collective-permute-start.36 = (f32[8,128,128]{2,1,0:T(8,128)S(1)}, f32[8,128,128]{2,1,0:T(8,128)S(1)}, u32[]{:S(2)}, u32[]{:S(2)}) collective-permute-start(f32[8,128,128]{2,1,0:T(8,128)S(1)} %constant_dynamic-update-slice_fusion.2.refs_7_), channel_id=1, source_target_pairs={{0,1},{1,2},{2,3},{3,0},{4,5},{5,6},{6,7},{7,4},{8,9},{9,10},{10,1... | collective-permute-start | bytes 1572872 | tf_op jit(solution)/shard_map/ppermute | solution.py:320
  151.1 20.4 %collective-permute-start.15 = (f32[4,128,128]{2,1,0:T(8,128)S(1)}, f32[4,128,128]{2,1,0:T(8,128)S(1)}, u32[]{:S(2)}, u32[]{:S(2)}) collective-permute-start(f32[4,128,128]{2,1,0:T(8,128)S(1)} %fusion.3), channel_id=1, source_target_pairs={{0,1},{1,2},{2,3},{3,0},{4,5},{5,6},{6,7},{7,4},{8,9},{9,10},{10,1... | collective-permute-start | bytes 786440 | tf_op jit(solution)/shard_map/ppermute | solution.py:320
  152.5 22.2 %collective-permute-start.11 = (f32[4,128,128]{2,1,0:T(8,128)S(1)}, f32[4,128,128]{2,1,0:T(8,128)S(1)}, u32[]{:S(2)}, u32[]{:S(2)}) collective-permute-start(f32[4,128,128]{2,1,0:T(8,128)S(1)} %fusion.3), channel_id=1, source_target_pairs={{0,3},{1,0},{2,1},{3,2},{4,7},{5,4},{6,5},{7,6},{8,11},{9,8},{10,9... | collective-permute-start | bytes 786440 | tf_op jit(solution)/shard_map/ppermute | solution.py:320
  153.3 28.3 %collective-permute-start.28 = (f32[8,128,128]{2,1,0:T(8,128)S(1)}, f32[8,128,128]{2,1,0:T(8,128)S(1)}, u32[]{:S(2)}, u32[]{:S(2)}) collective-permute-start(f32[8,128,128]{2,1,0:T(8,128)S(1)} %pad_maximum_fusion.1.refs_6_), channel_id=1, source_target_pairs={{0,1},{1,2},{2,3},{3,0},{4,5},{5,6},{6,7},{7,4},{8,9},{9,10},{10,1... | collective-permute-start | bytes 1572872 | tf_op jit(solution)/shard_map/ppermute | solution.py:320
  174.7 13.1 %collective-permute-start.16 = (f32[8,128,128]{2,1,0:T(8,128)S(1)}, f32[8,128,128]{2,1,0:T(8,128)S(1)}, u32[]{:S(2)}, u32[]{:S(2)}) collective-permute-start(f32[8,128,128]{2,1,0:T(8,128)S(1)} %constant_dynamic-update-slice_fusion.refs_1_), channel_id=1, source_target_pairs={{0,12},{1,13},{2,14},{3,15},{4,0},{5,1},{6,2},{7,3},{8,4},{9,5},{1... | collective-permute-start | bytes 1572872 | tf_op jit(solution)/shard_map/ppermute | solution.py:320
  175.7 16.1 %collective-permute-start.34 = (f32[8,128,128]{2,1,0:T(8,128)S(1)}, f32[8,128,128]{2,1,0:T(8,128)S(1)}, u32[]{:S(2)}, u32[]{:S(2)}) collective-permute-start(f32[8,128,128]{2,1,0:T(8,128)S(1)} %constant_dynamic-update-slice_fusion.refs_1_), channel_id=1, source_target_pairs={{0,4},{1,5},{2,6},{3,7},{4,8},{5,9},{6,10},{7,11},{8,12},{9,13},{1... | collective-permute-start | bytes 1572872 | tf_op jit(solution)/shard_map/ppermute | solution.py:320
  177.0 22.1 %collective-permute-start.12 = (f32[8,128,128]{2,1,0:T(8,128)S(1)}, f32[8,128,128]{2,1,0:T(8,128)S(1)}, u32[]{:S(2)}, u32[]{:S(2)}) collective-permute-start(f32[8,128,128]{2,1,0:T(8,128)S(1)} %pad_maximum_fusion.refs_0_), channel_id=1, source_target_pairs={{0,4},{1,5},{2,6},{3,7},{4,8},{5,9},{6,10},{7,11},{8,12},{9,13},{1... | collective-permute-start | bytes 1572872 | tf_op jit(solution)/shard_map/ppermute | solution.py:320
  181.6 18.7 %collective-permute-start.35 = (f32[8,128,128]{2,1,0:T(8,128)S(1)}, f32[8,128,128]{2,1,0:T(8,128)S(1)}, u32[]{:S(2)}, u32[]{:S(2)}) collective-permute-start(f32[8,128,128]{2,1,0:T(8,128)S(1)} %pad_maximum_fusion.refs_0_), channel_id=1, source_target_pairs={{0,12},{1,13},{2,14},{3,15},{4,0},{5,1},{6,2},{7,3},{8,4},{9,5},{1... | collective-permute-start | bytes 1572872 | tf_op jit(solution)/shard_map/ppermute | solution.py:320
  183.2 20.5 %collective-permute-start.33 = (f32[8,128,128]{2,1,0:T(8,128)S(1)}, f32[8,128,128]{2,1,0:T(8,128)S(1)}, u32[]{:S(2)}, u32[]{:S(2)}) collective-permute-start(f32[8,128,128]{2,1,0:T(8,128)S(1)} %collective-permute-done.32.refs_11_), channel_id=1, source_target_pairs={{0,3},{1,0},{2,1},{3,2},{4,7},{5,4},{6,5},{7,6},{8,11},{9,8},{10,9... | collective-permute-start | bytes 1572872 | tf_op jit(solution)/shard_map/ppermute | solution.py:320
  187.9 15.8 %collective-permute-start.29 = (f32[8,128,128]{2,1,0:T(8,128)S(1)}, f32[8,128,128]{2,1,0:T(8,128)S(1)}, u32[]{:S(2)}, u32[]{:S(2)}) collective-permute-start(f32[8,128,128]{2,1,0:T(8,128)S(1)} %collective-permute-done.28.refs_8_), channel_id=1, source_target_pairs={{0,1},{1,2},{2,3},{3,0},{4,5},{5,6},{6,7},{7,4},{8,9},{9,10},{10,1... | collective-permute-start | bytes 1572872 | tf_op jit(solution)/shard_map/ppermute | solution.py:320
  191.8 16.1 %collective-permute-start.17 = (f32[8,128,128]{2,1,0:T(8,128)S(1)}, f32[8,128,128]{2,1,0:T(8,128)S(1)}, u32[]{:S(2)}, u32[]{:S(2)}) collective-permute-start(f32[8,128,128]{2,1,0:T(8,128)S(1)} %collective-permute-done.16.refs_5_), channel_id=1, source_target_pairs={{0,12},{1,13},{2,14},{3,15},{4,0},{5,1},{6,2},{7,3},{8,4},{9,5},{1... | collective-permute-start | bytes 1572872 | tf_op jit(solution)/shard_map/ppermute | solution.py:320
  (10 other events, 71.5 us)

commit v2 on v0

v2 whole, which is shorter than its diff:
```python
import functools

import jax
import jax.numpy as jnp
from jax import lax
from jax.experimental import pallas as pl
from jax.experimental.pallas import tpu as pltpu
from jax.sharding import PartitionSpec as P

F32 = jnp.float32
BF16 = jnp.bfloat16
SIDE = 4
MB = 1 << 20


def parts_of(x):
    high = x.astype(BF16)
    return high, (x - high.astype(F32)).astype(BF16)


def row_pair(x):
    return jnp.concatenate(parts_of(x), axis=1)


def column_pair(x):
    pair = row_pair(x)
    return jnp.concatenate([pair, pair], axis=0)


def fold(x):
    n = x.shape[1] // 2
    return x[:, :n] + x[:, n:]


def product(left_pair, right_pair):
    return fold(jnp.dot(left_pair, right_pair, preferred_element_type=F32))


def choose_kernel(send_ref, p_ref, *rest):
    outs, (held, load_sem, sem) = rest[:-3], rest[-3:]
    load = pltpu.make_async_copy(p_ref, held, load_sem)
    load.start()
    load.wait()
    for i, out in enumerate(outs):
        side, first = i % 2, sum(outs[j].shape[0] for j in range(i % 2, i, 2))

        @pl.loop(0, out.shape[0])
        def _(j):
            tile = jnp.maximum(send_ref[side, first + j], 0)
            pltpu.make_async_copy(held.at[tile], out.at[j], sem.at[i]).start()

    for i, out in enumerate(outs):
        pltpu.make_async_copy(held.at[pl.ds(0, out.shape[0])], out, sem.at[i]).wait()


def choose(send, p_tiles, sizes):
    tile = p_tiles.shape[1:]
    out = tuple(jax.ShapeDtypeStruct((size,) + tile, F32) for size in sizes for _ in range(2))
    return pl.pallas_call(
        choose_kernel,
        name="choose",
        out_shape=out,
        in_specs=[pl.BlockSpec(memory_space=pltpu.SMEM), pl.BlockSpec(memory_space=pltpu.HBM)],
        out_specs=(pl.BlockSpec(memory_space=pl.ANY),) * len(out),
        scratch_shapes=[
            pltpu.VMEM(p_tiles.shape, F32),
            pltpu.SemaphoreType.DMA,
            pltpu.SemaphoreType.DMA((len(out),)),
        ],
        compiler_params=pltpu.CompilerParams(vmem_limit_bytes=16 * MB),
        cost_estimate=pl.CostEstimate(flops=0, bytes_accessed=4 * 32 * 65536, transcendentals=0),
    )(send, p_tiles)


BLOCKS = 4


def local_kernel(
    col_ref, target_ref, p_hbm, a_ref, *refs
):
    part_refs, (left_ref, slot_ref, p_ref, packed, total, left, sem) = refs[:-7], refs[-7:]
    step = pl.program_id(0)
    blocks = p_ref.shape[0]
    slots = left_ref.shape[0] - 1
    spare = total.shape[0] - 1

    @pl.when(step == 0)
    def _():
        load = pltpu.make_async_copy(p_hbm, p_ref, sem.at[0])
        load.start()
        load.wait()

        @pl.loop(0, blocks)
        def _(i):
            packed[i] = column_pair(p_ref[i])

        @pl.loop(0, spare + 1)
        def _(i):
            total[i] = jnp.zeros(total.shape[1:], F32)

        @pl.loop(0, slots)
        def _(i):
            slot_ref[i] = -1

    neighbours = a_ref.shape[1]
    for i in range(BLOCKS):
        f = step * BLOCKS + i
        rows = row_pair(p_ref[f].T)
        places = []
        for k in range(neighbours):
            v = col_ref[f * neighbours + k]
            t = target_ref[f * neighbours + k]
            remote = v >= blocks
            slot = jnp.where(remote, v - blocks, slots)
            slot_ref[slot] = t
            places.append((slot, jnp.where(remote, 0, v), jnp.where(remote, spare, t)))
        lefts = [product(rows, column_pair(a_ref[i, k])) for k in range(neighbours)]
        for w, (slot, _, _) in zip(lefts, places):
            left[slot] = w
        terms = [product(row_pair(w), packed[q]) for w, (_, q, _) in zip(lefts, places)]
        for term, (_, _, t) in zip(terms, places):
            total[t] += term

    @pl.when(step == pl.num_programs(0) - 1)
    def _():
        stores = [pltpu.make_async_copy(left, left_ref, sem.at[len(part_refs)])]
        first = 0
        for i, part in enumerate(part_refs):
            stores.append(pltpu.make_async_copy(total.at[pl.ds(first, part.shape[0])], part, sem.at[i]))
            first += part.shape[0]
        for store in stores:
            store.start()
        for store in stores:
            store.wait()


def local_part(col, target, p_tiles, a_tiles, sizes, slots):
    blocks, bs, cw = p_tiles.shape
    neighbours = a_tiles.shape[1]
    parts = tuple(jax.ShapeDtypeStruct((size, cw, cw), F32) for size in sizes)
    left = jax.ShapeDtypeStruct((slots + 1, cw, bs), F32)
    return pl.pallas_call(
        local_kernel,
        name="local_part",
        grid_spec=pltpu.PrefetchScalarGridSpec(
            num_scalar_prefetch=2,
            grid=(blocks // BLOCKS,),
            in_specs=[
                pl.BlockSpec(memory_space=pltpu.HBM),
                pl.BlockSpec((BLOCKS, neighbours, bs, bs), lambda f, *_: (f, 0, 0, 0)),
            ],
            out_specs=(pl.BlockSpec(memory_space=pl.ANY),) * (len(parts) + 1)
            + (pl.BlockSpec(memory_space=pltpu.SMEM),),
            scratch_shapes=[
                pltpu.VMEM(p_tiles.shape, F32),
                pltpu.VMEM((blocks, 2 * bs, 2 * cw), BF16),
                pltpu.VMEM((sum(sizes) + 1, cw, cw), F32),
                pltpu.VMEM(left.shape, F32),
                pltpu.SemaphoreType.DMA((len(parts) + 1,)),
            ],
        ),
        out_shape=parts + (left, jax.ShapeDtypeStruct((slots + 8,), jnp.int32)),
        compiler_params=pltpu.CompilerParams(vmem_limit_bytes=28 * MB),
        cost_estimate=pl.CostEstimate(flops=10**9, bytes_accessed=10**7, transcendentals=0),
    )(col, target, p_tiles, a_tiles)


GROUP = 4


def remote_kernel(first, base, slot_ref, left_ref, lower_ref, upper_ref, *refs):
    parts, todo = refs[len(refs) // 2 : -1], refs[-1]
    capacity = lower_ref.shape[0]
    slots = (left_ref.shape[0] - 1) // 2
    places = 2 * capacity + GROUP
    held = sum(part.shape[0] for part in parts)

    def find(j, n):
        place = slot_ref[jnp.where(j < capacity, base + j, slots + base + j - capacity)] - first
        wanted = (place >= 0) & (place < held)
        todo[n] = j
        todo[n + places] = place
        return n + wanted.astype(jnp.int32)

    count = lax.fori_loop(0, 2 * capacity, find, jnp.int32(0))
    for i in range(GROUP):
        todo[count + i] = 0
        todo[count + i + places] = -1

    def step(g, carry):
        terms = []
        for i in range(GROUP):
            j = todo[g * GROUP + i]
            above = j >= capacity
            k = jnp.where(above, j - capacity, j)
            received = jnp.where(above, upper_ref[k], lower_ref[k])
            terms.append(product(row_pair(left_ref[base + k + jnp.where(above, slots, 0)]), column_pair(received)))
        for i, term in enumerate(terms):
            place = todo[g * GROUP + i + places]
            start = 0
            for part in parts:
                here = place - start

                @pl.when((here >= 0) & (here < part.shape[0]))
                def _():
                    part[here] += term

                start += part.shape[0]
        return carry

    lax.fori_loop(0, (count + GROUP - 1) // GROUP, step, 0)


def remote_part(first, base, slots, left, lower, upper, parts):
    n = len(parts)
    vmem = pl.BlockSpec(memory_space=pltpu.VMEM)
    return pl.pallas_call(
        functools.partial(remote_kernel, first, base),
        name="remote_part",
        out_shape=tuple(jax.ShapeDtypeStruct(part.shape, F32) for part in parts),
        in_specs=[pl.BlockSpec(memory_space=pltpu.SMEM)] + [vmem] * (3 + n),
        out_specs=(vmem,) * n,
        scratch_shapes=[pltpu.SMEM((4 * lower.shape[0] + 2 * GROUP,), jnp.int32)],
        input_output_aliases={4 + i: i for i in range(n)},
        compiler_params=pltpu.CompilerParams(vmem_limit_bytes=24 * MB),
        cost_estimate=pl.CostEstimate(flops=10**8, bytes_accessed=10**6, transcendentals=0),
    )(slots, left, lower, upper, *parts)


def place_kernel(pieces, *refs):
    n = len(pieces)
    ins = refs[:n]
    out_ref, held, load_sem, store_sem = refs[-4:]
    at = lax.axis_index("bulk")
    x, y = at // SIDE, lax.rem(at, SIDE)
    loads, stores = [], []
    first = 0
    for ref, entries in zip(ins, pieces):
        loads.append(pltpu.make_async_copy(ref, held.at[pl.ds(first, ref.shape[0])], load_sem.at[len(loads)]))
        for where, size, ox, oy, h in entries:
            ox, oy = (lax.rem(x + ox, SIDE), oy) if h == 0 else (ox, lax.rem(y + oy, SIDE))
            where = where + (ox * SIDE + oy) * size
            stores.append(
                pltpu.make_async_copy(
                    held.at[pl.ds(first, size)], out_ref.at[pl.ds(where, size)], store_sem.at[len(stores)]
                )
            )
            first += size
    for load in loads:
        load.start()
    started = 0
    for load, entries in zip(loads, pieces):
        load.wait()
        for store in stores[started : started + len(entries)]:
            store.start()
        started += len(entries)
    for store in stores:
        store.wait()


def place(arrays, pieces, shape, out=None):
    anywhere = pl.BlockSpec(memory_space=pl.ANY)
    hbm = pl.BlockSpec(memory_space=pltpu.HBM)
    count = sum(len(entries) for entries in pieces)
    held = sum(array.shape[0] for array in arrays)
    args = list(arrays) + ([] if out is None else [out])
    return pl.pallas_call(
        functools.partial(place_kernel, pieces),
        name="place",
        out_shape=jax.ShapeDtypeStruct(shape, F32),
        in_specs=[anywhere] * len(arrays) + [hbm] * (len(args) - len(arrays)),
        out_specs=hbm,
        scratch_shapes=[
            pltpu.VMEM((held,) + shape[1:], F32),
            pltpu.SemaphoreType.DMA((len(arrays),)),
            pltpu.SemaphoreType.DMA((count,)),
        ],
        compiler_params=pltpu.CompilerParams(vmem_limit_bytes=16 * MB),
        input_output_aliases={} if out is None else {len(arrays): 0},
        cost_estimate=pl.CostEstimate(flops=0, bytes_accessed=2 * held * 65536, transcendentals=0),
    )(*args)


def route(dx, dy):
    pairs = []
    for x in range(SIDE):
        for y in range(SIDE):
            pairs.append((x * SIDE + y, (x + dx) % SIDE * SIDE + (y + dy) % SIDE))
    return pairs


def push(block, axis, distance):
    dx, dy = (distance, 0) if axis == "x" else (0, distance)
    return lax.ppermute(block, "bulk", route(dx, dy))


def swap(block, axis, odd):
    pairs = []
    for x in range(SIDE):
        for y in range(SIDE):
            to = [x, y]
            i = 0 if axis == "x" else 1
            to[i] = ((to[i] + odd) % SIDE ^ 1) - odd
            pairs.append((x * SIDE + y, to[0] % SIDE * SIDE + to[1] % SIDE))
    return lax.ppermute(block, "bulk", pairs)


def shifted(block, axis, distance):
    devices = range(lax.axis_size(axis))
    pairs = [(i - distance, i) for i in devices if i - distance in devices]
    return lax.ppermute(block, axis, pairs)


FIRST = 16
EIGHTHS = (6, 7, 4, 1, 0, 2, 3, 5)


def shards(p_tiles, a_tiles, col_ref, send_list, coarse_tile):
    tiles = 128
    size = tiles // 2 // (SIDE * SIDE)
    eighth = 2 * size
    capacity = send_list.shape[2]
    at = lax.axis_index("bulk")
    x, y = at // SIDE, at % SIDE
    half = coarse_tile // (tiles // 2)
    owner = coarse_tile // size
    ahead_x, ahead_y = (owner // SIDE - x) % SIDE, (owner - y) % SIDE
    outer = jnp.where(half == 0, ahead_x, ahead_y)
    inner = jnp.where(half == 0, owner % SIDE, owner // SIDE % SIDE)
    key = outer * 2 + inner // 2
    where = sum(jnp.where(key == i, at_eighth, 0) for i, at_eighth in enumerate(EIGHTHS))
    target = ((where // 4 * 2 + half) * 4 + where % 4) * eighth + inner % 2 * size + coarse_tile % size

    sizes = (FIRST, capacity - FIRST)
    halo = []
    sent = choose(send_list[0], p_tiles, sizes)
    for i in range(len(sizes)):
        lower = shifted(sent[2 * i + 1], ("group", "bulk"), 1)
        upper = shifted(sent[2 * i], ("group", "bulk"), -1)
        halo.append((lower, upper))
    mid = tiles // 2
    early_sizes = [n * eighth for n in (2, 2, 2, 2)]
    late_sizes = [n * eighth for n in (1, 1, 2, 1, 1, 2)]
    *parts, left, slot_tile = local_part(
        col_ref.reshape(-1), target.reshape(-1), p_tiles, a_tiles, early_sizes + late_sizes, 2 * capacity
    )
    early, late = parts[: len(early_sizes)], parts[len(early_sizes) :]
    early = remote_part(0, 0, slot_tile, left, *halo[0], early)
    late = remote_part(mid, 0, slot_tile, left, *halo[0], late)
    firsts = remote_part(0, FIRST, slot_tile, left, *halo[1], early)
    rests = remote_part(mid, FIRST, slot_tile, left, *halo[1], late)

    axes = (("x", "y"), ("y", "x"))
    owned = []
    arrived = [
        (push(firsts[2 * h], axis, 1), push(firsts[2 * h + 1], axis, -1)) for h, (axis, _) in enumerate(axes)
    ]
    for h, (axis, _) in enumerate(axes):
        up, down, kept = rests[3 * h : 3 * h + 3]
        from_below, from_above = arrived[h]
        up = push(up + from_below[:eighth], axis, 1)
        down = push(down + from_above[:eighth], axis, -1)
        owned.append((kept[:eighth] + from_above[eighth:] + up, kept[eighth:] + from_below[eighth:] + down))
    gathered = []
    for h, (_, axis) in enumerate(axes):
        one, two = owned[h]
        one, two = one + swap(one, axis, 0), two + swap(two, axis, 1)
        one, two = one + swap(one, axis, 1), two + swap(two, axis, 0)
        gathered.append(jnp.concatenate([one, two]))
    first, first_pieces, last, last_pieces = [], [], [], []

    def entry(h, outer, inner):
        return (h * mid, size) + ((outer, inner) if h == 0 else (inner, outer)) + (h,)

    for h, (axis, _) in enumerate(axes):
        behind = push(gathered[h], axis, 1)
        ahead = push(gathered[h], axis, -1)
        far_one = push(behind[:eighth], axis, 1)
        far_two = push(ahead[eighth:], axis, -1)
        for array, outer in ((gathered[h], 0), (behind, 3), (ahead, 1)):
            first.append(array)
            first_pieces.append([entry(h, outer, i) for i in range(SIDE)])
        for array, inners in ((far_one, (0, 1)), (far_two, (2, 3))):
            last.append(array)
            last_pieces.append([entry(h, 2, i) for i in inners])
    shape = (tiles,) + p_tiles.shape[2:] * 2
    out = place(first, first_pieces, shape)
    return place(last, last_pieces, shape, out)


def solution(mesh):
    in_specs = (
        P(("group", "bulk"), None, None),
        P(("group", "bulk"), None, None, None),
        P(("group", "bulk"), None),
        P(("group", "bulk"), None, None),
        P(("group", "bulk"), None),
    )
    out_specs = P("group", None, None)
    return jax.shard_map(shards, mesh=mesh, in_specs=in_specs, out_specs=out_specs, check_vma=False)
```

time: 369 us -> 180 us (0.49)
  waiting for transfers between devices: 188 us -> 69.2 us
  matrix products: 88.2 us -> 0 us
  local copies, waits for them, and re-layouts: 58.5 us -> 5.7 us
  starting transfers between devices: 9.77 us -> 61.5 us
  Pallas kernels: 0 us -> 40.5 us
  between operations: 13.5 us -> 0.3 us
  other arithmetic: 9.28 us -> 2.21 us
    psum x1 -> x0, waiting for transfers between devices: 144 us -> none  [shards(): operator = lax.psum(partial_op, 'bulk')]
    dot_general x3 -> x0, matrix products: 88.2 us -> none  [the longest x1 48.4 us: shards(): jnp.einsum('qxy,qyc->qxc', couplings, right_tiles, precision=lax.Precisio...]
    ppermute x2 -> x28, starting transfers between devices: 9.77 us -> 61.5 us  [the longest x8 21.7 us: swap(): return lax.ppermute(block, 'bulk', pairs)]
    pallas_call x0 -> x8, Pallas kernels: none -> 40.5 us  [the longest x1 22.2 us: local_part(): pl.pallas_call(local_kernel, name='local_part', grid_spec=pltpu.PrefetchS...]
    ppermute x2 -> x28, waiting for transfers between devices: 44.4 us -> 69.2 us  [the longest x16 49 us: push(): return lax.ppermute(block, 'bulk', route(dx, dy))]
    gather x2 -> x0, local copies, waits for them, and re-layouts: 22 us -> none  [the longest x1 17.3 us: shards(): right_tiles = jnp.take(lookup_rows, col_ref.reshape(-1), axis=0)]
    reshape x3 -> x2, local copies, waits for them, and re-layouts: 22 us -> 0.24 us  [the longest x1 0.12 us: shards(): target.reshape(-1)]
    psum x1 -> x0, local copies, waits for them, and re-layouts: 11.6 us -> none  [shards(): operator = lax.psum(partial_op, 'bulk')]
  transfers between devices with their start and end apart: 3 -> 28, of which waited for: 3 -> 17; matrix products, arithmetic and copies ran while one was open for 0% -> 2% of each run, Pallas kernels for 0% -> 19%
where the time goes in v2:
time: 180 us; the launch traced here: 179 us
  waiting for transfers between devices  69.2 us (38%)
  starting transfers between devices  61.5 us (34%)
  Pallas kernels  40.5 us (22%)
  local copies, waits for them, and re-layouts  5.7 us (3%)
  other arithmetic  2.21 us (1%)
    ppermute x16, waiting for transfers between devices, push(): return lax.ppermute(block, 'bulk', route(dx, dy))  49 us
    pallas_call x1, Pallas kernels, local_part(): pl.pallas_call(local_kernel, name='local_part', grid_spec=pltpu.PrefetchS...  22.2 us
    ppermute x8, starting transfers between devices, swap(): return lax.ppermute(block, 'bulk', pairs)  21.7 us
    ppermute x16, starting transfers between devices, push(): return lax.ppermute(block, 'bulk', route(dx, dy))  20.2 us
    ppermute x4, starting transfers between devices, shifted(): return lax.ppermute(block, axis, pairs)  19.6 us
    ppermute x8, waiting for transfers between devices, swap(): return lax.ppermute(block, 'bulk', pairs)  14.4 us
    pallas_call x4, Pallas kernels, remote_part(): pl.pallas_call(functools.partial(remote_kernel, first, base), name='remot...  10.7 us
    ppermute x4, waiting for transfers between devices, shifted(): return lax.ppermute(block, axis, pairs)  5.81 us
  transfers between devices with their start and end apart: 28, of which 17 were waited for; matrix products, arithmetic and copies ran while one was open for 2% of the time, Pallas kernels for 19%

profile of v2, /device:TPU:32, one launch (start us, length us, event | category | flops | bytes accessed | tf_op | source)
XLA Modules:
  0.0 179.4 jit_solution(8516120107300853227)
XLA Ops:
  0.0 1.9 %copy-done = f32[48,128,128]{2,1,0:T(8,128)S(1)} copy-done((f32[48,128,128]{2,1,0:T(8,128)S(1)}, f32[48,128,128]{2,1,0:T(8,128)}, u32[]{:S(2)}) %copy-start) | copy-done | bytes 3145752
  2.6 2.8 %choose.1 = (f32[16,128,128]{2,1,0:T(8,128)}, f32[16,128,128]{2,1,0:T(8,128)}, f32[16,128,128]{2,1,0:T(8,128)}, f32[16,128,128]{2,1,0:T(8,128)}) custom-call(s32[2,32]{1,0:T(2,128)S(1)} %bitcast.1, f32[48,128,128]{2,1,0:T(8,128)S(1)} %copy-done), custom_call_target="tpu_custom_call" | custom-call | bytes 8388608 | tf_op jit(solution)/shard_map/choose/pallas_call | solution.py:59
  5.3 3.5 %collective-permute-start.2 = (f32[16,128,128]{2,1,0:T(8,128)}, f32[16,128,128]{2,1,0:T(8,128)S(1)}, u32[]{:S(2)}, u32[]{:S(2)}) collective-permute-start(f32[16,128,128]{2,1,0:T(8,128)} %get-tuple-element.45), channel_id=1, source_target_pairs={{0,1},{1,2},{2,3},{3,4},{4,5},{5,6},{6,7},{7,8},{8,9},{9,10},{10,1... | collective-permute-start | bytes 3145736 | tf_op jit(solution)/shard_map/ppermute | solution.py:311
  8.8 6.3 %collective-permute-start.3 = (f32[16,128,128]{2,1,0:T(8,128)}, f32[16,128,128]{2,1,0:T(8,128)}, u32[]{:S(2)}, u32[]{:S(2)}) collective-permute-start(f32[16,128,128]{2,1,0:T(8,128)} %get-tuple-element.46), channel_id=1, source_target_pairs={{1,0},{2,1},{3,2},{4,3},{5,4},{6,5},{7,6},{8,7},{9,8},{10,9},{11,1... | collective-permute-start | bytes 3145736 | tf_op jit(solution)/shard_map/ppermute | solution.py:311
  15.1 1.9 %collective-permute-start = (f32[16,128,128]{2,1,0:T(8,128)}, f32[16,128,128]{2,1,0:T(8,128)S(1)}, u32[]{:S(2)}, u32[]{:S(2)}) collective-permute-start(f32[16,128,128]{2,1,0:T(8,128)} %get-tuple-element.43), channel_id=1, source_target_pairs={{0,1},{1,2},{2,3},{3,4},{4,5},{5,6},{6,7},{7,8},{8,9},{9,10},{10,1... | collective-permute-start | bytes 3145736 | tf_op jit(solution)/shard_map/ppermute | solution.py:311
  17.1 7.9 %collective-permute-start.1 = (f32[16,128,128]{2,1,0:T(8,128)}, f32[16,128,128]{2,1,0:T(8,128)S(1)}, u32[]{:S(2)}, u32[]{:S(2)}) collective-permute-start(f32[16,128,128]{2,1,0:T(8,128)} %get-tuple-element.44), channel_id=1, source_target_pairs={{1,0},{2,1},{3,2},{4,3},{5,4},{6,5},{7,6},{8,7},{9,8},{10,9},{11,1... | collective-permute-start | bytes 3145736 | tf_op jit(solution)/shard_map/ppermute | solution.py:311
  26.8 1.9 %copy-done.1 = f32[48,128,128]{2,1,0:T(8,128)S(1)} copy-done((f32[48,128,128]{2,1,0:T(8,128)S(1)}, f32[48,128,128]{2,1,0:T(8,128)}, u32[]{:S(2)}) %copy-start.1) | copy-done | bytes 3145752
  28.7 22.2 %local_part.1 = (f32[16,128,128]{2,1,0:T(8,128)S(1)}, f32[16,128,128]{2,1,0:T(8,128)S(1)}, f32[16,128,128]{2,1,0:T(8,128)S(1)}, f32[16,128,128]{2,1,0:T(8,128)S(...) custom-call(s32[336]{0:T(512)S(1)} %reshape.6.col_ref, ...), custom_call_target="tpu_custom_call" | custom-call | flops 1000000000 | bytes 10000000 | tf_op jit(solution)/shard_map/local_part/pallas_call | solution.py:142
  50.9 3.4 %remote_part.6 = (f32[16,128,128]{2,1,0:T(8,128)S(1)}, f32[16,128,128]{2,1,0:T(8,128)S(1)}, f32[16,128,128]{2,1,0:T(8,128)S(1)}, f32[16,128,128]{2,1,0:T(8,128)S(1)}) custom-call(s32[72]{0:T(128)S(1)} %get-tuple-element.41.slot_ref, ...), custom_call_target="tpu_custom_call", output_to_operand_aliasing={{0}: (4, {}), {1}: (5, {}), {2}: (6, {}), {3}: (7, {})} | custom-call | flops 100000000 | bytes 1000000 | tf_op jit(solution)/shard_map/remote_part/pallas_call | solution.py:217
  54.3 4.4 %collective-permute-done.lower_ref = f32[16,128,128]{2,1,0:T(8,128)S(1)} collective-permute-done((f32[16,128,128]{2,1,0:T(8,128)}, f32[16,128,128]{2,1,0:T(8,128)S(1)}, u32[]{:S(2)}, u32[]{:S(2)}) %collective-permute-start) | collective-permute-done | bytes 1048608 | tf_op jit(solution)/shard_map/ppermute | solution.py:311
  60.1 2.3 %remote_part.7 = (f32[16,128,128]{2,1,0:T(8,128)S(1)}, f32[16,128,128]{2,1,0:T(8,128)S(1)}, f32[16,128,128]{2,1,0:T(8,128)S(1)}, f32[16,128,128]{2,1,0:T(8,128)S(1)}) custom-call(s32[72]{0:T(128)S(1)} %get-tuple-element.41.slot_ref, ...), custom_call_target="tpu_custom_call", output_to_operand_aliasing={{0}: (4, {}), {1}: (5, {}), {2}: (6, {}), {3}: (7, {})} | custom-call | flops 100000000 | bytes 1000000 | tf_op jit(solution)/shard_map/remote_part/pallas_call | solution.py:217
  63.0 1.6 collective-permute-start.5
  64.6 2.6 %collective-permute-start.16 = (f32[16,128,128]{2,1,0:T(8,128)S(1)}, f32[16,128,128]{2,1,0:T(8,128)S(1)}, u32[]{:S(2)}, u32[]{:S(2)}) collective-permute-start(f32[16,128,128]{2,1,0:T(8,128)S(1)} %get-tuple-element.73), channel_id=1, source_target_pairs={{0,3},{1,0},{2,1},{3,2},{4,7},{5,4},{6,5},{7,6},{8,11},{9,8},{10,9... | collective-permute-start | bytes 3145736 | tf_op jit(solution)/shard_map/ppermute | solution.py:294
  67.2 3.3 %remote_part.4 = (f32[8,128,128]{2,1,0:T(8,128)S(1)}, f32[8,128,128]{2,1,0:T(8,128)S(1)}, f32[16,128,128]{2,1,0:T(8,128)S(1)}, f32[8,128,128]{2,1,0:T(8,128)S(1)...) custom-call(s32[72]{0:T(128)S(1)} %get-tuple-element.41.slot_ref, ...), custom_call_target="tpu_custom_call", output_to_operand_aliasing={{0}: (4, {}), {1}: (5, {}), {2}: (6, {}), {3}: (7, {}), {4}... | custom-call | flops 100000000 | bytes 1000000 | tf_op jit(solution)/shard_map/remote_part/pallas_call | solution.py:217
  70.4 1.7 remote_part.5
  72.2 13.1 %collective-permute-done.4 = f32[16,128,128]{2,1,0:T(8,128)S(1)} collective-permute-done((f32[16,128,128]{2,1,0:T(8,128)S(1)}, f32[16,128,128]{2,1,0:T(8,128)S(1)}, u32[]{:S(2)}, u32[]{:S(2)}) %collective-permute-start.4) | collective-permute-done | bytes 1048608 | tf_op jit(solution)/shard_map/ppermute | solution.py:294
  85.3 3.1 %collective-permute-start.9 = (f32[8,128,128]{2,1,0:T(8,128)S(1)}, f32[8,128,128]{2,1,0:T(8,128)S(1)}, u32[]{:S(2)}, u32[]{:S(2)}) collective-permute-start(f32[8,128,128]{2,1,0:T(8,128)S(1)} %slice_add_fusion.4), channel_id=1, source_target_pairs={{0,12},{1,13},{2,14},{3,15},{4,0},{5,1},{6,2},{7,3},{8,4},{9,5},{1... | collective-permute-start | bytes 1572872 | tf_op jit(solution)/shard_map/ppermute | solution.py:294
  89.6 3.8 %collective-permute-start.21 = (f32[8,128,128]{2,1,0:T(8,128)S(1)}, f32[8,128,128]{2,1,0:T(8,128)S(1)}, u32[]{:S(2)}, u32[]{:S(2)}) collective-permute-start(f32[8,128,128]{2,1,0:T(8,128)S(1)} %slice_add_fusion), channel_id=1, source_target_pairs={{0,3},{1,0},{2,1},{3,2},{4,7},{5,4},{6,5},{7,6},{8,11},{9,8},{10,9... | collective-permute-start | bytes 1572872 | tf_op jit(solution)/shard_map/ppermute | solution.py:294
  93.7 4.2 %collective-permute-done.9 = f32[8,128,128]{2,1,0:T(8,128)S(1)} collective-permute-done((f32[8,128,128]{2,1,0:T(8,128)S(1)}, f32[8,128,128]{2,1,0:T(8,128)S(1)}, u32[]{:S(2)}, u32[]{:S(2)}) %collective-permute-start.9) | collective-permute-done | bytes 524320 | tf_op jit(solution)/shard_map/ppermute | solution.py:294
  97.9 3.6 %collective-permute-done.6 = f32[8,128,128]{2,1,0:T(8,128)S(1)} collective-permute-done((f32[8,128,128]{2,1,0:T(8,128)S(1)}, f32[8,128,128]{2,1,0:T(8,128)S(1)}, u32[]{:S(2)}, u32[]{:S(2)}) %collective-permute-start.6) | collective-permute-done | bytes 524320 | tf_op jit(solution)/shard_map/ppermute | solution.py:294
  101.7 7.4 %collective-permute-start.10 = (f32[8,128,128]{2,1,0:T(8,128)S(1)}, f32[8,128,128]{2,1,0:T(8,128)S(1)}, u32[]{:S(2)}, u32[]{:S(2)}) collective-permute-start(f32[8,128,128]{2,1,0:T(8,128)S(1)} %get-tuple-element.80), channel_id=1, source_target_pairs={{0,3},{1,2},{2,1},{3,0},{4,7},{5,6},{6,5},{7,4},{8,11},{9,10},{10,... | collective-permute-start | bytes 1572872 | tf_op jit(solution)/shard_map/ppermute | solution.py:305
  110.0 4.3 %collective-permute-start.22 = (f32[8,128,128]{2,1,0:T(8,128)S(1)}, f32[8,128,128]{2,1,0:T(8,128)S(1)}, u32[]{:S(2)}, u32[]{:S(2)}) collective-permute-start(f32[8,128,128]{2,1,0:T(8,128)S(1)} %get-tuple-element.78), channel_id=1, source_target_pairs={{0,12},{1,13},{2,14},{3,15},{4,8},{5,9},{6,10},{7,11},{8,4},{9,5},... | collective-permute-start | bytes 1572872 | tf_op jit(solution)/shard_map/ppermute | solution.py:305
  114.3 2.6 %collective-permute-done.7 = f32[8,128,128]{2,1,0:T(8,128)S(1)} collective-permute-done((f32[8,128,128]{2,1,0:T(8,128)S(1)}, f32[8,128,128]{2,1,0:T(8,128)S(1)}, u32[]{:S(2)}, u32[]{:S(2)}) %collective-permute-start.7) | collective-permute-done | bytes 524320 | tf_op jit(solution)/shard_map/ppermute | solution.py:305
  117.0 6.5 %collective-permute-start.8 = (f32[8,128,128]{2,1,0:T(8,128)S(1)}, f32[8,128,128]{2,1,0:T(8,128)S(1)}, u32[]{:S(2)}, u32[]{:S(2)}) collective-permute-start(f32[8,128,128]{2,1,0:T(8,128)S(1)} %add.158), channel_id=1, source_target_pairs={{0,3},{1,2},{2,1},{3,0},{4,7},{5,6},{6,5},{7,4},{8,11},{9,10},{10,... | collective-permute-start | bytes 1572872 | tf_op jit(solution)/shard_map/ppermute | solution.py:305
  124.0 3.1 %collective-permute-start.20 = (f32[8,128,128]{2,1,0:T(8,128)S(1)}, f32[8,128,128]{2,1,0:T(8,128)S(1)}, u32[]{:S(2)}, u32[]{:S(2)}) collective-permute-start(f32[8,128,128]{2,1,0:T(8,128)S(1)} %add.168), channel_id=1, source_target_pairs={{0,12},{1,13},{2,14},{3,15},{4,8},{5,9},{6,10},{7,11},{8,4},{9,5},... | collective-permute-start | bytes 1572872 | tf_op jit(solution)/shard_map/ppermute | solution.py:305
  127.3 8.0 %collective-permute-done.8 = f32[8,128,128]{2,1,0:T(8,128)S(1)} collective-permute-done((f32[8,128,128]{2,1,0:T(8,128)S(1)}, f32[8,128,128]{2,1,0:T(8,128)S(1)}, u32[]{:S(2)}, u32[]{:S(2)}) %collective-permute-start.8) | collective-permute-done | bytes 524320 | tf_op jit(solution)/shard_map/ppermute | solution.py:305
  139.2 1.9 %collective-permute-done.23 = f32[8,128,128]{2,1,0:T(8,128)S(1)} collective-permute-done((f32[8,128,128]{2,1,0:T(8,128)S(1)}, f32[8,128,128]{2,1,0:T(8,128)S(1)}, u32[]{:S(2)}, u32[]{:S(2)}) %collective-permute-start.23) | collective-permute-done | bytes 524320 | tf_op jit(solution)/shard_map/ppermute | solution.py:305
  141.4 2.0 %collective-permute-start.24 = (f32[16,128,128]{2,1,0:T(8,128)S(1)}, f32[16,128,128]{2,1,0:T(8,128)S(1)}, u32[]{:S(2)}, u32[]{:S(2)}) collective-permute-start(f32[16,128,128]{2,1,0:T(8,128)S(1)} %pad_maximum_fusion.1.refs_3_), channel_id=1, source_target_pairs={{0,1},{1,2},{2,3},{3,0},{4,5},{5,6},{6,7},{7,4},{8,9},{9,10},{10,1... | collective-permute-start | bytes 3145736 | tf_op jit(solution)/shard_map/ppermute | solution.py:294
  143.4 18.8 %collective-permute-done.14.refs_2_ = f32[16,128,128]{2,1,0:T(8,128)S(1)} collective-permute-done((f32[16,128,128]{2,1,0:T(8,128)S(1)}, f32[16,128,128]{2,1,0:T(8,128)S(1)}, u32[]{:S(2)}, u32[]{:S(2)}) %collective-permute-start.14) | collective-permute-done | bytes 1048608 | tf_op jit(solution)/shard_map/ppermute | solution.py:294
  166.7 3.3 %place.2.refs_4_ = f32[128,128,128]{2,1,0:T(8,128)} custom-call(f32[16,128,128]{2,1,0:T(8,128)S(1)} %pad_maximum_fusion.refs_0_, f32[16,128,128]{2,1,0:T(8,128)S(1)} %collective-permute-done.12.refs_1_, f32[16,128,128]{2,1,0:T(8,128)S(1)} %collective-permute-done.14.refs_2_, f32[16,128,128]{2,1,0:T(8,128)S(1)} %pad_maximum_fusion.1.refs_3_, ...), custom_call_target="tpu_custom_call" | custom-call | bytes 12582912 | tf_op jit(solution)/shard_map/place/pallas_call | solution.py:267
  170.0 4.8 %collective-permute-done.15.refs_1_ = f32[8,128,128]{2,1,0:T(8,128)S(1)} collective-permute-done((f32[8,128,128]{2,1,0:T(8,128)S(1)}, f32[8,128,128]{2,1,0:T(8,128)S(1)}, u32[]{:S(2)}, u32[]{:S(2)}) %collective-permute-start.15) | collective-permute-done | bytes 524320 | tf_op jit(solution)/shard_map/ppermute | solution.py:294
  174.8 2.0 %collective-permute-done.13.refs_0_ = f32[8,128,128]{2,1,0:T(8,128)S(1)} collective-permute-done((f32[8,128,128]{2,1,0:T(8,128)S(1)}, f32[8,128,128]{2,1,0:T(8,128)S(1)}, u32[]{:S(2)}, u32[]{:S(2)}) %collective-permute-start.13) | collective-permute-done | bytes 524320 | tf_op jit(solution)/shard_map/ppermute | solution.py:294
  (63 shorter events, 19.1 us)
Async XLA Ops:
  0.0 1.9 %copy-start = (f32[48,128,128]{2,1,0:T(8,128)S(1)}, f32[48,128,128]{2,1,0:T(8,128)}, u32[]{:S(2)}) copy-start(f32[48,128,128]{2,1,0:T(8,128)} %p_ref.1) | copy-start | bytes 9437188
  1.9 0.7 copy-start.2
  5.3 45.6 %collective-permute-start.2 = (f32[16,128,128]{2,1,0:T(8,128)}, f32[16,128,128]{2,1,0:T(8,128)S(1)}, u32[]{:S(2)}, u32[]{:S(2)}) collective-permute-start(f32[16,128,128]{2,1,0:T(8,128)} %get-tuple-element.45), channel_id=1, source_target_pairs={{0,1},{1,2},{2,3},{3,4},{4,5},{5,6},{6,7},{7,8},{8,9},{9,10},{10,1... | collective-permute-start | bytes 3145736 | tf_op jit(solution)/shard_map/ppermute | solution.py:311
  8.8 42.1 %collective-permute-start.3 = (f32[16,128,128]{2,1,0:T(8,128)}, f32[16,128,128]{2,1,0:T(8,128)}, u32[]{:S(2)}, u32[]{:S(2)}) collective-permute-start(f32[16,128,128]{2,1,0:T(8,128)} %get-tuple-element.46), channel_id=1, source_target_pairs={{1,0},{2,1},{3,2},{4,3},{5,4},{6,5},{7,6},{8,7},{9,8},{10,9},{11,1... | collective-permute-start | bytes 3145736 | tf_op jit(solution)/shard_map/ppermute | solution.py:311
  15.1 43.5 %collective-permute-start = (f32[16,128,128]{2,1,0:T(8,128)}, f32[16,128,128]{2,1,0:T(8,128)S(1)}, u32[]{:S(2)}, u32[]{:S(2)}) collective-permute-start(f32[16,128,128]{2,1,0:T(8,128)} %get-tuple-element.43), channel_id=1, source_target_pairs={{0,1},{1,2},{2,3},{3,4},{4,5},{5,6},{6,7},{7,8},{8,9},{9,10},{10,1... | collective-permute-start | bytes 3145736 | tf_op jit(solution)/shard_map/ppermute | solution.py:311
  17.1 43.1 %collective-permute-start.1 = (f32[16,128,128]{2,1,0:T(8,128)}, f32[16,128,128]{2,1,0:T(8,128)S(1)}, u32[]{:S(2)}, u32[]{:S(2)}) collective-permute-start(f32[16,128,128]{2,1,0:T(8,128)} %get-tuple-element.44), channel_id=1, source_target_pairs={{1,0},{2,1},{3,2},{4,3},{5,4},{6,5},{7,6},{8,7},{9,8},{10,9},{11,1... | collective-permute-start | bytes 3145736 | tf_op jit(solution)/shard_map/ppermute | solution.py:311
  26.8 1.9 %copy-start.1 = (f32[48,128,128]{2,1,0:T(8,128)S(1)}, f32[48,128,128]{2,1,0:T(8,128)}, u32[]{:S(2)}) copy-start(f32[48,128,128]{2,1,0:T(8,128)} %p_ref.1) | copy-start | bytes 9437188
  62.5 22.8 %collective-permute-start.4 = (f32[16,128,128]{2,1,0:T(8,128)S(1)}, f32[16,128,128]{2,1,0:T(8,128)S(1)}, u32[]{:S(2)}, u32[]{:S(2)}) collective-permute-start(f32[16,128,128]{2,1,0:T(8,128)S(1)} %get-tuple-element.68), channel_id=1, source_target_pairs={{0,12},{1,13},{2,14},{3,15},{4,0},{5,1},{6,2},{7,3},{8,4},{9,5},{1... | collective-permute-start | bytes 3145736 | tf_op jit(solution)/shard_map/ppermute | solution.py:294
  63.0 25.4 %collective-permute-start.5 = (f32[16,128,128]{2,1,0:T(8,128)S(1)}, f32[16,128,128]{2,1,0:T(8,128)S(1)}, u32[]{:S(2)}, u32[]{:S(2)}) collective-permute-start(f32[16,128,128]{2,1,0:T(8,128)S(1)} %get-tuple-element.70), channel_id=1, source_target_pairs={{0,4},{1,5},{2,6},{3,7},{4,8},{5,9},{6,10},{7,11},{8,12},{9,13},{1... | collective-permute-start | bytes 3145736 | tf_op jit(solution)/shard_map/ppermute | solution.py:294
  64.6 25.0 %collective-permute-start.16 = (f32[16,128,128]{2,1,0:T(8,128)S(1)}, f32[16,128,128]{2,1,0:T(8,128)S(1)}, u32[]{:S(2)}, u32[]{:S(2)}) collective-permute-start(f32[16,128,128]{2,1,0:T(8,128)S(1)} %get-tuple-element.73), channel_id=1, source_target_pairs={{0,3},{1,0},{2,1},{3,2},{4,7},{5,4},{6,5},{7,6},{8,11},{9,8},{10,9... | collective-permute-start | bytes 3145736 | tf_op jit(solution)/shard_map/ppermute | solution.py:294
  67.2 26.4 %collective-permute-start.17 = (f32[16,128,128]{2,1,0:T(8,128)S(1)}, f32[16,128,128]{2,1,0:T(8,128)S(1)}, u32[]{:S(2)}, u32[]{:S(2)}) collective-permute-start(f32[16,128,128]{2,1,0:T(8,128)S(1)} %get-tuple-element.75), channel_id=1, source_target_pairs={{0,1},{1,2},{2,3},{3,0},{4,5},{5,6},{6,7},{7,4},{8,9},{9,10},{10,1... | collective-permute-start | bytes 3145736 | tf_op jit(solution)/shard_map/ppermute | solution.py:294
  85.3 12.5 %collective-permute-start.9 = (f32[8,128,128]{2,1,0:T(8,128)S(1)}, f32[8,128,128]{2,1,0:T(8,128)S(1)}, u32[]{:S(2)}, u32[]{:S(2)}) collective-permute-start(f32[8,128,128]{2,1,0:T(8,128)S(1)} %slice_add_fusion.4), channel_id=1, source_target_pairs={{0,12},{1,13},{2,14},{3,15},{4,0},{5,1},{6,2},{7,3},{8,4},{9,5},{1... | collective-permute-start | bytes 1572872 | tf_op jit(solution)/shard_map/ppermute | solution.py:294
  88.5 12.9 %collective-permute-start.6 = (f32[8,128,128]{2,1,0:T(8,128)S(1)}, f32[8,128,128]{2,1,0:T(8,128)S(1)}, u32[]{:S(2)}, u32[]{:S(2)}) collective-permute-start(f32[8,128,128]{2,1,0:T(8,128)S(1)} %slice_add_fusion.6), channel_id=1, source_target_pairs={{0,4},{1,5},{2,6},{3,7},{4,8},{5,9},{6,10},{7,11},{8,12},{9,13},{1... | collective-permute-start | bytes 1572872 | tf_op jit(solution)/shard_map/ppermute | solution.py:294
  89.6 19.6 %collective-permute-start.21 = (f32[8,128,128]{2,1,0:T(8,128)S(1)}, f32[8,128,128]{2,1,0:T(8,128)S(1)}, u32[]{:S(2)}, u32[]{:S(2)}) collective-permute-start(f32[8,128,128]{2,1,0:T(8,128)S(1)} %slice_add_fusion), channel_id=1, source_target_pairs={{0,3},{1,0},{2,1},{3,2},{4,7},{5,4},{6,5},{7,6},{8,11},{9,8},{10,9... | collective-permute-start | bytes 1572872 | tf_op jit(solution)/shard_map/ppermute | solution.py:294
  93.6 16.1 %collective-permute-start.18 = (f32[8,128,128]{2,1,0:T(8,128)S(1)}, f32[8,128,128]{2,1,0:T(8,128)S(1)}, u32[]{:S(2)}, u32[]{:S(2)}) collective-permute-start(f32[8,128,128]{2,1,0:T(8,128)S(1)} %slice_add_fusion.2), channel_id=1, source_target_pairs={{0,1},{1,2},{2,3},{3,0},{4,5},{5,6},{6,7},{7,4},{8,9},{9,10},{10,1... | collective-permute-start | bytes 1572872 | tf_op jit(solution)/shard_map/ppermute | solution.py:294
  101.6 15.3 %collective-permute-start.7 = (f32[8,128,128]{2,1,0:T(8,128)S(1)}, f32[8,128,128]{2,1,0:T(8,128)S(1)}, u32[]{:S(2)}, u32[]{:S(2)}) collective-permute-start(f32[8,128,128]{2,1,0:T(8,128)S(1)} %get-tuple-element.79), channel_id=1, source_target_pairs={{0,1},{1,0},{2,3},{3,2},{4,5},{5,4},{6,7},{7,6},{8,9},{9,8},{10,11... | collective-permute-start | bytes 1572872 | tf_op jit(solution)/shard_map/ppermute | solution.py:305
  101.7 21.8 %collective-permute-start.10 = (f32[8,128,128]{2,1,0:T(8,128)S(1)}, f32[8,128,128]{2,1,0:T(8,128)S(1)}, u32[]{:S(2)}, u32[]{:S(2)}) collective-permute-start(f32[8,128,128]{2,1,0:T(8,128)S(1)} %get-tuple-element.80), channel_id=1, source_target_pairs={{0,3},{1,2},{2,1},{3,0},{4,7},{5,6},{6,5},{7,4},{8,11},{9,10},{10,... | collective-permute-start | bytes 1572872 | tf_op jit(solution)/shard_map/ppermute | solution.py:305
  109.9 14.0 %collective-permute-start.19 = (f32[8,128,128]{2,1,0:T(8,128)S(1)}, f32[8,128,128]{2,1,0:T(8,128)S(1)}, u32[]{:S(2)}, u32[]{:S(2)}) collective-permute-start(f32[8,128,128]{2,1,0:T(8,128)S(1)} %get-tuple-element.77), channel_id=1, source_target_pairs={{0,4},{1,5},{2,6},{3,7},{4,0},{5,1},{6,2},{7,3},{8,12},{9,13},{10,... | collective-permute-start | bytes 1572872 | tf_op jit(solution)/shard_map/ppermute | solution.py:305
  110.0 17.1 %collective-permute-start.22 = (f32[8,128,128]{2,1,0:T(8,128)S(1)}, f32[8,128,128]{2,1,0:T(8,128)S(1)}, u32[]{:S(2)}, u32[]{:S(2)}) collective-permute-start(f32[8,128,128]{2,1,0:T(8,128)S(1)} %get-tuple-element.78), channel_id=1, source_target_pairs={{0,12},{1,13},{2,14},{3,15},{4,8},{5,9},{6,10},{7,11},{8,4},{9,5},... | collective-permute-start | bytes 1572872 | tf_op jit(solution)/shard_map/ppermute | solution.py:305
  117.0 18.3 %collective-permute-start.8 = (f32[8,128,128]{2,1,0:T(8,128)S(1)}, f32[8,128,128]{2,1,0:T(8,128)S(1)}, u32[]{:S(2)}, u32[]{:S(2)}) collective-permute-start(f32[8,128,128]{2,1,0:T(8,128)S(1)} %add.158), channel_id=1, source_target_pairs={{0,3},{1,2},{2,1},{3,0},{4,7},{5,6},{6,5},{7,4},{8,11},{9,10},{10,... | collective-permute-start | bytes 1572872 | tf_op jit(solution)/shard_map/ppermute | solution.py:305
  123.6 13.3 %collective-permute-start.11 = (f32[8,128,128]{2,1,0:T(8,128)S(1)}, f32[8,128,128]{2,1,0:T(8,128)S(1)}, u32[]{:S(2)}, u32[]{:S(2)}) collective-permute-start(f32[8,128,128]{2,1,0:T(8,128)S(1)} %add.163), channel_id=1, source_target_pairs={{0,1},{1,0},{2,3},{3,2},{4,5},{5,4},{6,7},{7,6},{8,9},{9,8},{10,11... | collective-permute-start | bytes 1572872 | tf_op jit(solution)/shard_map/ppermute | solution.py:305
  124.0 15.2 %collective-permute-start.20 = (f32[8,128,128]{2,1,0:T(8,128)S(1)}, f32[8,128,128]{2,1,0:T(8,128)S(1)}, u32[]{:S(2)}, u32[]{:S(2)}) collective-permute-start(f32[8,128,128]{2,1,0:T(8,128)S(1)} %add.168), channel_id=1, source_target_pairs={{0,12},{1,13},{2,14},{3,15},{4,8},{5,9},{6,10},{7,11},{8,4},{9,5},... | collective-permute-start | bytes 1572872 | tf_op jit(solution)/shard_map/ppermute | solution.py:305
  127.2 14.0 %collective-permute-start.23 = (f32[8,128,128]{2,1,0:T(8,128)S(1)}, f32[8,128,128]{2,1,0:T(8,128)S(1)}, u32[]{:S(2)}, u32[]{:S(2)}) collective-permute-start(f32[8,128,128]{2,1,0:T(8,128)S(1)} %add.173), channel_id=1, source_target_pairs={{0,4},{1,5},{2,6},{3,7},{4,0},{5,1},{6,2},{7,3},{8,12},{9,13},{10,... | collective-permute-start | bytes 1572872 | tf_op jit(solution)/shard_map/ppermute | solution.py:305
  137.1 25.1 %collective-permute-start.14 = (f32[16,128,128]{2,1,0:T(8,128)S(1)}, f32[16,128,128]{2,1,0:T(8,128)S(1)}, u32[]{:S(2)}, u32[]{:S(2)}) collective-permute-start(f32[16,128,128]{2,1,0:T(8,128)S(1)} %pad_maximum_fusion.refs_0_), channel_id=1, source_target_pairs={{0,12},{1,13},{2,14},{3,15},{4,0},{5,1},{6,2},{7,3},{8,4},{9,5},{1... | collective-permute-start | bytes 3145736 | tf_op jit(solution)/shard_map/ppermute | solution.py:294
  138.2 25.5 %collective-permute-start.12 = (f32[16,128,128]{2,1,0:T(8,128)S(1)}, f32[16,128,128]{2,1,0:T(8,128)S(1)}, u32[]{:S(2)}, u32[]{:S(2)}) collective-permute-start(f32[16,128,128]{2,1,0:T(8,128)S(1)} %pad_maximum_fusion.refs_0_), channel_id=1, source_target_pairs={{0,4},{1,5},{2,6},{3,7},{4,8},{5,9},{6,10},{7,11},{8,12},{9,13},{1... | collective-permute-start | bytes 3145736 | tf_op jit(solution)/shard_map/ppermute | solution.py:294
  141.3 23.1 %collective-permute-start.26 = (f32[16,128,128]{2,1,0:T(8,128)S(1)}, f32[16,128,128]{2,1,0:T(8,128)S(1)}, u32[]{:S(2)}, u32[]{:S(2)}) collective-permute-start(f32[16,128,128]{2,1,0:T(8,128)S(1)} %pad_maximum_fusion.1.refs_3_), channel_id=1, source_target_pairs={{0,3},{1,0},{2,1},{3,2},{4,7},{5,4},{6,5},{7,6},{8,11},{9,8},{10,9... | collective-permute-start | bytes 3145736 | tf_op jit(solution)/shard_map/ppermute | solution.py:294
  141.4 24.1 %collective-permute-start.24 = (f32[16,128,128]{2,1,0:T(8,128)S(1)}, f32[16,128,128]{2,1,0:T(8,128)S(1)}, u32[]{:S(2)}, u32[]{:S(2)}) collective-permute-start(f32[16,128,128]{2,1,0:T(8,128)S(1)} %pad_maximum_fusion.1.refs_3_), channel_id=1, source_target_pairs={{0,1},{1,2},{2,3},{3,0},{4,5},{5,6},{6,7},{7,4},{8,9},{9,10},{10,1... | collective-permute-start | bytes 3145736 | tf_op jit(solution)/shard_map/ppermute | solution.py:294
  162.2 12.6 %collective-permute-start.15 = (f32[8,128,128]{2,1,0:T(8,128)S(1)}, f32[8,128,128]{2,1,0:T(8,128)S(1)}, u32[]{:S(2)}, u32[]{:S(2)}) collective-permute-start(f32[8,128,128]{2,1,0:T(8,128)S(1)} %slice.69), channel_id=1, source_target_pairs={{0,12},{1,13},{2,14},{3,15},{4,0},{5,1},{6,2},{7,3},{8,4},{9,5},{1... | collective-permute-start | bytes 1572872 | tf_op jit(solution)/shard_map/ppermute | solution.py:294
  163.8 13.0 %collective-permute-start.13 = (f32[8,128,128]{2,1,0:T(8,128)S(1)}, f32[8,128,128]{2,1,0:T(8,128)S(1)}, u32[]{:S(2)}, u32[]{:S(2)}) collective-permute-start(f32[8,128,128]{2,1,0:T(8,128)S(1)} %slice.68), channel_id=1, source_target_pairs={{0,4},{1,5},{2,6},{3,7},{4,8},{5,9},{6,10},{7,11},{8,12},{9,13},{1... | collective-permute-start | bytes 1572872 | tf_op jit(solution)/shard_map/ppermute | solution.py:294
  164.5 12.3 %collective-permute-start.27 = (f32[8,128,128]{2,1,0:T(8,128)S(1)}, f32[8,128,128]{2,1,0:T(8,128)S(1)}, u32[]{:S(2)}, u32[]{:S(2)}) collective-permute-start(f32[8,128,128]{2,1,0:T(8,128)S(1)} %slice.75), channel_id=1, source_target_pairs={{0,3},{1,0},{2,1},{3,2},{4,7},{5,4},{6,5},{7,6},{8,11},{9,8},{10,9... | collective-permute-start | bytes 1572872 | tf_op jit(solution)/shard_map/ppermute | solution.py:294
  165.5 12.3 %collective-permute-start.25 = (f32[8,128,128]{2,1,0:T(8,128)S(1)}, f32[8,128,128]{2,1,0:T(8,128)S(1)}, u32[]{:S(2)}, u32[]{:S(2)}) collective-permute-start(f32[8,128,128]{2,1,0:T(8,128)S(1)} %slice.74), channel_id=1, source_target_pairs={{0,1},{1,2},{2,3},{3,0},{4,5},{5,6},{6,7},{7,4},{8,9},{9,10},{10,1... | collective-permute-start | bytes 1572872 | tf_op jit(solution)/shard_map/ppermute | solution.py:294

commit v3 on v2

--- a/solution.py
+++ b/solution.py
@@ -36,39 +36,23 @@
     return fold(jnp.dot(left_pair, right_pair, preferred_element_type=F32))
 
 
-def choose_kernel(send_ref, p_ref, *rest):
-    outs, (held, load_sem, sem) = rest[:-3], rest[-3:]
-    load = pltpu.make_async_copy(p_ref, held, load_sem)
-    load.start()
-    load.wait()
-    for i, out in enumerate(outs):
-        side, first = i % 2, sum(outs[j].shape[0] for j in range(i % 2, i, 2))
-
-        @pl.loop(0, out.shape[0])
-        def _(j):
-            tile = jnp.maximum(send_ref[side, first + j], 0)
-            pltpu.make_async_copy(held.at[tile], out.at[j], sem.at[i]).start()
-
-    for i, out in enumerate(outs):
-        pltpu.make_async_copy(held.at[pl.ds(0, out.shape[0])], out, sem.at[i]).wait()
-
-
-def choose(send, p_tiles, sizes):
-    tile = p_tiles.shape[1:]
-    out = tuple(jax.ShapeDtypeStruct((size,) + tile, F32) for size in sizes for _ in range(2))
+def choose_kernel(first, send_ref, p_ref, low_ref, up_ref):
+    for j in range(low_ref.shape[0]):
+        for side, out in enumerate((low_ref, up_ref)):
+            out[j] = p_ref[jnp.maximum(send_ref[side, first + j], 0)]
+
+
+def choose(send, p_tiles, first, size):
+    out = jax.ShapeDtypeStruct((size,) + p_tiles.shape[1:], F32)
+    vmem = pl.BlockSpec(memory_space=pltpu.VMEM)
     return pl.pallas_call(
-        choose_kernel,
+        functools.partial(choose_kernel, first),
         name="choose",
-        out_shape=out,
-        in_specs=[pl.BlockSpec(memory_space=pltpu.SMEM), pl.BlockSpec(memory_space=pltpu.HBM)],
-        out_specs=(pl.BlockSpec(memory_space=pl.ANY),) * len(out),
-        scratch_shapes=[
-            pltpu.VMEM(p_tiles.shape, F32),
-            pltpu.SemaphoreType.DMA,
-            pltpu.SemaphoreType.DMA((len(out),)),
-        ],
-        compiler_params=pltpu.CompilerParams(vmem_limit_bytes=16 * MB),
-        cost_estimate=pl.CostEstimate(flops=0, bytes_accessed=4 * 32 * 65536, transcendentals=0),
+        out_shape=(out, out),
+        in_specs=[pl.BlockSpec(memory_space=pltpu.SMEM), vmem],
+        out_specs=(vmem, vmem),
+        compiler_params=pltpu.CompilerParams(vmem_limit_bytes=24 * MB),
+        cost_estimate=pl.CostEstimate(flops=0, bytes_accessed=10**6, transcendentals=0),
     )(send, p_tiles)
 
 
@@ -232,28 +216,21 @@
     ins = refs[:n]
     out_ref, held, load_sem, store_sem = refs[-4:]
     at = lax.axis_index("bulk")
-    x, y = at // SIDE, lax.rem(at, SIDE)
+    here = {"x": at // SIDE, "y": lax.rem(at, SIDE)}
     loads, stores = [], []
     first = 0
-    for ref, entries in zip(ins, pieces):
-        loads.append(pltpu.make_async_copy(ref, held.at[pl.ds(first, ref.shape[0])], load_sem.at[len(loads)]))
-        for where, size, ox, oy, h in entries:
-            ox, oy = (lax.rem(x + ox, SIDE), oy) if h == 0 else (ox, lax.rem(y + oy, SIDE))
-            where = where + (ox * SIDE + oy) * size
-            stores.append(
-                pltpu.make_async_copy(
-                    held.at[pl.ds(first, size)], out_ref.at[pl.ds(where, size)], store_sem.at[len(stores)]
-                )
-            )
-            first += size
+    for i, (ref, (where, axis, distance, stride)) in enumerate(zip(ins, pieces)):
+        if axis is not None:
+            where = where + lax.rem(here[axis] + distance, SIDE) * stride
+        size = ref.shape[0]
+        loads.append(pltpu.make_async_copy(ref, held.at[pl.ds(first, size)], load_sem.at[i]))
+        stores.append(pltpu.make_async_copy(held.at[pl.ds(first, size)], out_ref.at[pl.ds(where, size)], store_sem.at[i]))
+        first += size
     for load in loads:
         load.start()
-    started = 0
-    for load, entries in zip(loads, pieces):
+    for load, store in zip(loads, stores):
         load.wait()
-        for store in stores[started : started + len(entries)]:
-            store.start()
-        started += len(entries)
+        store.start()
     for store in stores:
         store.wait()
 
@@ -261,7 +238,6 @@
 def place(arrays, pieces, shape, out=None):
     anywhere = pl.BlockSpec(memory_space=pl.ANY)
     hbm = pl.BlockSpec(memory_space=pltpu.HBM)
-    count = sum(len(entries) for entries in pieces)
     held = sum(array.shape[0] for array in arrays)
     args = list(arrays) + ([] if out is None else [out])
     return pl.pallas_call(
@@ -273,7 +249,7 @@
         scratch_shapes=[
             pltpu.VMEM((held,) + shape[1:], F32),
             pltpu.SemaphoreType.DMA((len(arrays),)),
-            pltpu.SemaphoreType.DMA((count,)),
+            pltpu.SemaphoreType.DMA((len(arrays),)),
         ],
         compiler_params=pltpu.CompilerParams(vmem_limit_bytes=16 * MB),
         input_output_aliases={} if out is None else {len(arrays): 0},
@@ -311,36 +287,32 @@
     return lax.ppermute(block, axis, pairs)
 
 
-FIRST = 16
-EIGHTHS = (6, 7, 4, 1, 0, 2, 3, 5)
+FIRST = 22
+LANES = 2
+LAYOUT = (6, 7, 4, 1, 0, 2, 3, 5)
 
 
 def shards(p_tiles, a_tiles, col_ref, send_list, coarse_tile):
     tiles = 128
-    size = tiles // 2 // (SIDE * SIDE)
-    eighth = 2 * size
+    e = tiles // (8 * LANES)
+    mid = tiles // 2
+    axes = (("x", "y"), ("y", "x")) * (LANES // 2)
     capacity = send_list.shape[2]
     at = lax.axis_index("bulk")
-    x, y = at // SIDE, at % SIDE
-    half = coarse_tile // (tiles // 2)
-    owner = coarse_tile // size
-    ahead_x, ahead_y = (owner // SIDE - x) % SIDE, (owner - y) % SIDE
-    outer = jnp.where(half == 0, ahead_x, ahead_y)
-    inner = jnp.where(half == 0, owner % SIDE, owner // SIDE % SIDE)
-    key = outer * 2 + inner // 2
-    where = sum(jnp.where(key == i, at_eighth, 0) for i, at_eighth in enumerate(EIGHTHS))
-    target = ((where // 4 * 2 + half) * 4 + where % 4) * eighth + inner % 2 * size + coarse_tile % size
-
-    sizes = (FIRST, capacity - FIRST)
+    lane = coarse_tile // (8 * e)
+    shard = coarse_tile // (2 * e) % SIDE
+    key = (shard - jnp.where(lane % 2 == 0, at // SIDE, at % SIDE)) % SIDE * 2 + coarse_tile // e % 2
+    where = sum(jnp.where(key == i, at_eighth, 0) for i, at_eighth in enumerate(LAYOUT))
+    target = ((where // 4 * LANES + lane) * 4 + where % 4) * e + coarse_tile % e
+
     halo = []
-    sent = choose(send_list[0], p_tiles, sizes)
-    for i in range(len(sizes)):
-        lower = shifted(sent[2 * i + 1], ("group", "bulk"), 1)
-        upper = shifted(sent[2 * i], ("group", "bulk"), -1)
+    for first, size in ((0, FIRST), (FIRST, capacity - FIRST)):
+        to_lower, to_upper = choose(send_list[0], p_tiles, first, size)
+        lower = shifted(to_upper, ("group", "bulk"), 1)
+        upper = shifted(to_lower, ("group", "bulk"), -1)
         halo.append((lower, upper))
-    mid = tiles // 2
-    early_sizes = [n * eighth for n in (2, 2, 2, 2)]
-    late_sizes = [n * eighth for n in (1, 1, 2, 1, 1, 2)]
+    early_sizes = [2 * e, 2 * e] * LANES
+    late_sizes = [e, e, 2 * e] * LANES
     *parts, left, slot_tile = local_part(
         col_ref.reshape(-1), target.reshape(-1), p_tiles, a_tiles, early_sizes + late_sizes, 2 * capacity
     )
@@ -350,7 +322,6 @@
     firsts = remote_part(0, FIRST, slot_tile, left, *halo[1], early)
     rests = remote_part(mid, FIRST, slot_tile, left, *halo[1], late)
 
-    axes = (("x", "y"), ("y", "x"))
     owned = []
     arrived = [
         (push(firsts[2 * h], axis, 1), push(firsts[2 * h + 1], axis, -1)) for h, (axis, _) in enumerate(axes)
@@ -358,9 +329,9 @@
     for h, (axis, _) in enumerate(axes):
         up, down, kept = rests[3 * h : 3 * h + 3]
         from_below, from_above = arrived[h]
-        up = push(up + from_below[:eighth], axis, 1)
-        down = push(down + from_above[:eighth], axis, -1)
-        owned.append((kept[:eighth] + from_above[eighth:] + up, kept[eighth:] + from_below[eighth:] + down))
+        up = push(up + from_below[:e], axis, 1)
+        down = push(down + from_above[:e], axis, -1)
+        owned.append((kept[:e] + from_above[e:] + up, kept[e:] + from_below[e:] + down))
     gathered = []
     for h, (_, axis) in enumerate(axes):
         one, two = owned[h]
@@ -368,21 +339,15 @@
         one, two = one + swap(one, axis, 1), two + swap(two, axis, 0)
         gathered.append(jnp.concatenate([one, two]))
     first, first_pieces, last, last_pieces = [], [], [], []
-
-    def entry(h, outer, inner):
-        return (h * mid, size) + ((outer, inner) if h == 0 else (inner, outer)) + (h,)
-
     for h, (axis, _) in enumerate(axes):
         behind = push(gathered[h], axis, 1)
         ahead = push(gathered[h], axis, -1)
-        far_one = push(behind[:eighth], axis, 1)
-        far_two = push(ahead[eighth:], axis, -1)
-        for array, outer in ((gathered[h], 0), (behind, 3), (ahead, 1)):
-            first.append(array)
-            first_pieces.append([entry(h, outer, i) for i in range(SIDE)])
-        for array, inners in ((far_one, (0, 1)), (far_two, (2, 3))):
-            last.append(array)
-            last_pieces.append([entry(h, 2, i) for i in inners])
+        far_one = push(behind[:e], axis, 1)
+        far_two = push(ahead[e:], axis, -1)
+        first += [gathered[h], behind, ahead]
+        first_pieces += [(8 * h * e, axis, distance, 2 * e) for distance in (0, 3, 1)]
+        last += [far_one, far_two]
+        last_pieces += [(8 * h * e + side * e, axis, 2, 2 * e) for side in range(2)]
     shape = (tiles,) + p_tiles.shape[2:] * 2
     out = place(first, first_pieces, shape)
     return place(last, last_pieces, shape, out)

time: 180 us -> 180 us (level); the launches traced: 179 us -> 178 us
  local copies, waits for them, and re-layouts: 5.7 us -> 3.14 us
  Pallas kernels: 40.5 us -> 42.8 us
    unnamed x7 -> x11, local copies, waits for them, and re-layouts: 5.23 us -> 2.67 us
    pallas_call x1 -> x2, Pallas kernels: 2.75 us -> 4.03 us  [choose(): pl.pallas_call(functools.partial(choose_kernel, first), name='choose', ou...]
  transfers between devices with their start and end apart: 28 -> 28, of which waited for: 17 -> 15; matrix products, arithmetic and copies ran while one was open for 2% -> 1% of each run, Pallas kernels for 19% -> 21%
where the time goes in v3:
time: 180 us; the launch traced here: 178 us
  waiting for transfers between devices  68.2 us (38%)
  starting transfers between devices  61.6 us (34%)
  Pallas kernels  42.8 us (24%)
  local copies, waits for them, and re-layouts  3.14 us (2%)
    ppermute x16, waiting for transfers between devices, push(): return lax.ppermute(block, 'bulk', route(dx, dy))  47.9 us
    pallas_call x1, Pallas kernels, local_part(): pl.pallas_call(local_kernel, name='local_part', grid_spec=pltpu.PrefetchS...  22.2 us
    ppermute x8, starting transfers between devices, swap(): return lax.ppermute(block, 'bulk', pairs)  22 us
    ppermute x16, starting transfers between devices, push(): return lax.ppermute(block, 'bulk', route(dx, dy))  20 us
    ppermute x4, starting transfers between devices, shifted(): return lax.ppermute(block, axis, pairs)  19.5 us
    ppermute x8, waiting for transfers between devices, swap(): return lax.ppermute(block, 'bulk', pairs)  14.1 us
    pallas_call x4, Pallas kernels, remote_part(): pl.pallas_call(functools.partial(remote_kernel, first, base), name='remot...  11.8 us
    ppermute x4, waiting for transfers between devices, shifted(): return lax.ppermute(block, axis, pairs)  6.25 us
  transfers between devices with their start and end apart: 28, of which 15 were waited for; matrix products, arithmetic and copies ran while one was open for 1% of the time, Pallas kernels for 21%

profile of v3, /device:TPU:32, one launch (start us, length us, event | category | flops | bytes accessed | tf_op | source)
XLA Modules:
  0.0 177.5 jit_solution(17514462505664879132)
XLA Ops:
  0.0 1.9 %copy-done = f32[48,128,128]{2,1,0:T(8,128)S(1)} copy-done((f32[48,128,128]{2,1,0:T(8,128)S(1)}, f32[48,128,128]{2,1,0:T(8,128)}, u32[]{:S(2)}) %copy-start) | copy-done | bytes 3145752
  2.6 2.3 %choose.3 = (f32[22,128,128]{2,1,0:T(8,128)}, f32[22,128,128]{2,1,0:T(8,128)}) custom-call(s32[2,32]{1,0:T(2,128)S(1)} %bitcast.1, f32[48,128,128]{2,1,0:T(8,128)S(1)} %copy-done), custom_call_target="tpu_custom_call" | custom-call | bytes 1000000 | tf_op jit(solution)/shard_map/choose/pallas_call | solution.py:48
  4.9 3.5 %collective-permute-start.2 = (f32[22,128,128]{2,1,0:T(8,128)}, f32[22,128,128]{2,1,0:T(8,128)}, u32[]{:S(2)}, u32[]{:S(2)}) collective-permute-start(f32[22,128,128]{2,1,0:T(8,128)} %get-tuple-element.45), channel_id=1, source_target_pairs={{0,1},{1,2},{2,3},{3,4},{4,5},{5,6},{6,7},{7,8},{8,9},{9,10},{10,1... | collective-permute-start | bytes 4325384 | tf_op jit(solution)/shard_map/ppermute | solution.py:287
  8.4 6.3 %collective-permute-start.3 = (f32[22,128,128]{2,1,0:T(8,128)}, f32[22,128,128]{2,1,0:T(8,128)}, u32[]{:S(2)}, u32[]{:S(2)}) collective-permute-start(f32[22,128,128]{2,1,0:T(8,128)} %get-tuple-element.46), channel_id=1, source_target_pairs={{1,0},{2,1},{3,2},{4,3},{5,4},{6,5},{7,6},{8,7},{9,8},{10,9},{11,1... | collective-permute-start | bytes 4325384 | tf_op jit(solution)/shard_map/ppermute | solution.py:287
  14.7 1.7 choose.2
  16.4 1.9 %collective-permute-start = (f32[10,128,128]{2,1,0:T(8,128)}, f32[10,128,128]{2,1,0:T(8,128)}, u32[]{:S(2)}, u32[]{:S(2)}) collective-permute-start(f32[10,128,128]{2,1,0:T(8,128)} %get-tuple-element.43), channel_id=1, source_target_pairs={{0,1},{1,2},{2,3},{3,4},{4,5},{5,6},{6,7},{7,8},{8,9},{9,10},{10,1... | collective-permute-start | bytes 1966088 | tf_op jit(solution)/shard_map/ppermute | solution.py:287
  18.3 7.9 %collective-permute-start.1 = (f32[10,128,128]{2,1,0:T(8,128)}, f32[10,128,128]{2,1,0:T(8,128)}, u32[]{:S(2)}, u32[]{:S(2)}) collective-permute-start(f32[10,128,128]{2,1,0:T(8,128)} %get-tuple-element.44), channel_id=1, source_target_pairs={{1,0},{2,1},{3,2},{4,3},{5,4},{6,5},{7,6},{8,7},{9,8},{10,9},{11,1... | collective-permute-start | bytes 1966088 | tf_op jit(solution)/shard_map/ppermute | solution.py:287
  26.7 22.2 %local_part.1 = (f32[16,128,128]{2,1,0:T(8,128)S(1)}, f32[16,128,128]{2,1,0:T(8,128)S(1)}, f32[16,128,128]{2,1,0:T(8,128)S(1)}, f32[16,128,128]{2,1,0:T(8,128)S(...) custom-call(s32[336]{0:T(512)S(1)} %reshape.6.col_ref, ...), custom_call_target="tpu_custom_call" | custom-call | flops 1000000000 | bytes 10000000 | tf_op jit(solution)/shard_map/local_part/pallas_call | solution.py:126
  48.9 4.5 %remote_part.6 = (f32[16,128,128]{2,1,0:T(8,128)S(1)}, f32[16,128,128]{2,1,0:T(8,128)S(1)}, f32[16,128,128]{2,1,0:T(8,128)S(1)}, f32[16,128,128]{2,1,0:T(8,128)S(1)}) custom-call(s32[72]{0:T(128)S(1)} %get-tuple-element.41.slot_ref, ...), custom_call_target="tpu_custom_call", output_to_operand_aliasing={{0}: (4, {}), {1}: (5, {}), {2}: (6, {}), {3}: (7, {})} | custom-call | flops 100000000 | bytes 1000000 | tf_op jit(solution)/shard_map/remote_part/pallas_call | solution.py:201
  53.4 4.9 %collective-permute-done.lower_ref = f32[10,128,128]{2,1,0:T(8,128)} collective-permute-done((f32[10,128,128]{2,1,0:T(8,128)}, f32[10,128,128]{2,1,0:T(8,128)}, u32[]{:S(2)}, u32[]{:S(2)}) %collective-permute-start) | collective-permute-done | bytes 655392 | tf_op jit(solution)/shard_map/ppermute | solution.py:287
  63.3 3.4 %collective-permute-start.16 = (f32[16,128,128]{2,1,0:T(8,128)S(1)}, f32[16,128,128]{2,1,0:T(8,128)S(1)}, u32[]{:S(2)}, u32[]{:S(2)}) collective-permute-start(f32[16,128,128]{2,1,0:T(8,128)S(1)} %get-tuple-element.73), channel_id=1, source_target_pairs={{0,3},{1,0},{2,1},{3,2},{4,7},{5,4},{6,5},{7,6},{8,11},{9,8},{10,9... | collective-permute-start | bytes 3145736 | tf_op jit(solution)/shard_map/ppermute | solution.py:270
  66.7 4.4 %remote_part.4 = (f32[8,128,128]{2,1,0:T(8,128)S(1)}, f32[8,128,128]{2,1,0:T(8,128)S(1)}, f32[16,128,128]{2,1,0:T(8,128)S(1)}, f32[8,128,128]{2,1,0:T(8,128)S(1)...) custom-call(s32[72]{0:T(128)S(1)} %get-tuple-element.41.slot_ref, ...), custom_call_target="tpu_custom_call", output_to_operand_aliasing={{0}: (4, {}), {1}: (5, {}), {2}: (6, {}), {3}: (7, {}), {4}... | custom-call | flops 100000000 | bytes 1000000 | tf_op jit(solution)/shard_map/remote_part/pallas_call | solution.py:201
  72.6 12.8 %collective-permute-done.4 = f32[16,128,128]{2,1,0:T(8,128)S(1)} collective-permute-done((f32[16,128,128]{2,1,0:T(8,128)S(1)}, f32[16,128,128]{2,1,0:T(8,128)S(1)}, u32[]{:S(2)}, u32[]{:S(2)}) %collective-permute-start.4) | collective-permute-done | bytes 1048608 | tf_op jit(solution)/shard_map/ppermute | solution.py:270
  85.5 2.0 %collective-permute-start.9 = (f32[8,128,128]{2,1,0:T(8,128)S(1)}, f32[8,128,128]{2,1,0:T(8,128)S(1)}, u32[]{:S(2)}, u32[]{:S(2)}) collective-permute-start(f32[8,128,128]{2,1,0:T(8,128)S(1)} %slice_add_fusion.4), channel_id=1, source_target_pairs={{0,12},{1,13},{2,14},{3,15},{4,0},{5,1},{6,2},{7,3},{8,4},{9,5},{1... | collective-permute-start | bytes 1572872 | tf_op jit(solution)/shard_map/ppermute | solution.py:270
  87.7 1.7 collective-permute-done.16
  89.5 3.8 %collective-permute-start.21 = (f32[8,128,128]{2,1,0:T(8,128)S(1)}, f32[8,128,128]{2,1,0:T(8,128)S(1)}, u32[]{:S(2)}, u32[]{:S(2)}) collective-permute-start(f32[8,128,128]{2,1,0:T(8,128)S(1)} %slice_add_fusion), channel_id=1, source_target_pairs={{0,3},{1,0},{2,1},{3,2},{4,7},{5,4},{6,5},{7,6},{8,11},{9,8},{10,9... | collective-permute-start | bytes 1572872 | tf_op jit(solution)/shard_map/ppermute | solution.py:270
  93.6 4.0 %collective-permute-done.9 = f32[8,128,128]{2,1,0:T(8,128)S(1)} collective-permute-done((f32[8,128,128]{2,1,0:T(8,128)S(1)}, f32[8,128,128]{2,1,0:T(8,128)S(1)}, u32[]{:S(2)}, u32[]{:S(2)}) %collective-permute-start.9) | collective-permute-done | bytes 524320 | tf_op jit(solution)/shard_map/ppermute | solution.py:270
  97.6 2.6 %collective-permute-done.6 = f32[8,128,128]{2,1,0:T(8,128)S(1)} collective-permute-done((f32[8,128,128]{2,1,0:T(8,128)S(1)}, f32[8,128,128]{2,1,0:T(8,128)S(1)}, u32[]{:S(2)}, u32[]{:S(2)}) %collective-permute-start.6) | collective-permute-done | bytes 524320 | tf_op jit(solution)/shard_map/ppermute | solution.py:270
  100.3 2.7 %collective-permute-start.7 = (f32[8,128,128]{2,1,0:T(8,128)S(1)}, f32[8,128,128]{2,1,0:T(8,128)S(1)}, u32[]{:S(2)}, u32[]{:S(2)}) collective-permute-start(f32[8,128,128]{2,1,0:T(8,128)S(1)} %get-tuple-element.79), channel_id=1, source_target_pairs={{0,1},{1,0},{2,3},{3,2},{4,5},{5,4},{6,7},{7,6},{8,9},{9,8},{10,11... | collective-permute-start | bytes 1572872 | tf_op jit(solution)/shard_map/ppermute | solution.py:281
  103.0 6.4 %collective-permute-start.10 = (f32[8,128,128]{2,1,0:T(8,128)S(1)}, f32[8,128,128]{2,1,0:T(8,128)S(1)}, u32[]{:S(2)}, u32[]{:S(2)}) collective-permute-start(f32[8,128,128]{2,1,0:T(8,128)S(1)} %get-tuple-element.80), channel_id=1, source_target_pairs={{0,3},{1,2},{2,1},{3,0},{4,7},{5,6},{6,5},{7,4},{8,11},{9,10},{10,... | collective-permute-start | bytes 1572872 | tf_op jit(solution)/shard_map/ppermute | solution.py:281
  109.7 3.8 %collective-permute-start.22 = (f32[8,128,128]{2,1,0:T(8,128)S(1)}, f32[8,128,128]{2,1,0:T(8,128)S(1)}, u32[]{:S(2)}, u32[]{:S(2)}) collective-permute-start(f32[8,128,128]{2,1,0:T(8,128)S(1)} %get-tuple-element.78), channel_id=1, source_target_pairs={{0,12},{1,13},{2,14},{3,15},{4,8},{5,9},{6,10},{7,11},{8,4},{9,5},... | collective-permute-start | bytes 1572872 | tf_op jit(solution)/shard_map/ppermute | solution.py:281
  113.5 3.5 %collective-permute-done.7 = f32[8,128,128]{2,1,0:T(8,128)S(1)} collective-permute-done((f32[8,128,128]{2,1,0:T(8,128)S(1)}, f32[8,128,128]{2,1,0:T(8,128)S(1)}, u32[]{:S(2)}, u32[]{:S(2)}) %collective-permute-start.7) | collective-permute-done | bytes 524320 | tf_op jit(solution)/shard_map/ppermute | solution.py:281
  117.1 6.2 %collective-permute-start.8 = (f32[8,128,128]{2,1,0:T(8,128)S(1)}, f32[8,128,128]{2,1,0:T(8,128)S(1)}, u32[]{:S(2)}, u32[]{:S(2)}) collective-permute-start(f32[8,128,128]{2,1,0:T(8,128)S(1)} %add.148), channel_id=1, source_target_pairs={{0,3},{1,2},{2,1},{3,0},{4,7},{5,6},{6,5},{7,4},{8,11},{9,10},{10,... | collective-permute-start | bytes 1572872 | tf_op jit(solution)/shard_map/ppermute | solution.py:281
  123.6 2.7 %collective-permute-start.20 = (f32[8,128,128]{2,1,0:T(8,128)S(1)}, f32[8,128,128]{2,1,0:T(8,128)S(1)}, u32[]{:S(2)}, u32[]{:S(2)}) collective-permute-start(f32[8,128,128]{2,1,0:T(8,128)S(1)} %add.158), channel_id=1, source_target_pairs={{0,12},{1,13},{2,14},{3,15},{4,8},{5,9},{6,10},{7,11},{8,4},{9,5},... | collective-permute-start | bytes 1572872 | tf_op jit(solution)/shard_map/ppermute | solution.py:281
  126.5 8.1 %collective-permute-done.8 = f32[8,128,128]{2,1,0:T(8,128)S(1)} collective-permute-done((f32[8,128,128]{2,1,0:T(8,128)S(1)}, f32[8,128,128]{2,1,0:T(8,128)S(1)}, u32[]{:S(2)}, u32[]{:S(2)}) %collective-permute-start.8) | collective-permute-done | bytes 524320 | tf_op jit(solution)/shard_map/ppermute | solution.py:281
  134.7 1.6 collective-permute-done.11
  141.7 19.1 %collective-permute-done.14.refs_2_ = f32[16,128,128]{2,1,0:T(8,128)S(1)} collective-permute-done((f32[16,128,128]{2,1,0:T(8,128)S(1)}, f32[16,128,128]{2,1,0:T(8,128)S(1)}, u32[]{:S(2)}, u32[]{:S(2)}) %collective-permute-start.14) | collective-permute-done | bytes 1048608 | tf_op jit(solution)/shard_map/ppermute | solution.py:270
  160.8 1.8 %collective-permute-start.15 = (f32[8,128,128]{2,1,0:T(8,128)S(1)}, f32[8,128,128]{2,1,0:T(8,128)S(1)}, u32[]{:S(2)}, u32[]{:S(2)}) collective-permute-start(f32[8,128,128]{2,1,0:T(8,128)S(1)} %slice.69), channel_id=1, source_target_pairs={{0,12},{1,13},{2,14},{3,15},{4,0},{5,1},{6,2},{7,3},{8,4},{9,5},{1... | collective-permute-start | bytes 1572872 | tf_op jit(solution)/shard_map/ppermute | solution.py:270
  165.2 3.2 %place.2.refs_4_ = f32[128,128,128]{2,1,0:T(8,128)} custom-call(f32[16,128,128]{2,1,0:T(8,128)S(1)} %pad_maximum_fusion.refs_0_, f32[16,128,128]{2,1,0:T(8,128)S(1)} %collective-permute-done.12.refs_1_, f32[16,128,128]{2,1,0:T(8,128)S(1)} %collective-permute-done.14.refs_2_, f32[16,128,128]{2,1,0:T(8,128)S(1)} %pad_maximum_fusion.1.refs_3_, ...), custom_call_target="tpu_custom_call" | custom-call | bytes 12582912 | tf_op jit(solution)/shard_map/place/pallas_call | solution.py:243
  168.4 4.5 %collective-permute-done.15.refs_1_ = f32[8,128,128]{2,1,0:T(8,128)S(1)} collective-permute-done((f32[8,128,128]{2,1,0:T(8,128)S(1)}, f32[8,128,128]{2,1,0:T(8,128)S(1)}, u32[]{:S(2)}, u32[]{:S(2)}) %collective-permute-start.15) | collective-permute-done | bytes 524320 | tf_op jit(solution)/shard_map/ppermute | solution.py:270
  173.0 2.3 %collective-permute-done.13.refs_0_ = f32[8,128,128]{2,1,0:T(8,128)S(1)} collective-permute-done((f32[8,128,128]{2,1,0:T(8,128)S(1)}, f32[8,128,128]{2,1,0:T(8,128)S(1)}, u32[]{:S(2)}, u32[]{:S(2)}) %collective-permute-start.13) | collective-permute-done | bytes 524320 | tf_op jit(solution)/shard_map/ppermute | solution.py:270
  176.0 1.5 place.3
  (68 shorter events, 18.1 us)
Async XLA Ops:
  0.0 1.9 %copy-start = (f32[48,128,128]{2,1,0:T(8,128)S(1)}, f32[48,128,128]{2,1,0:T(8,128)}, u32[]{:S(2)}) copy-start(f32[48,128,128]{2,1,0:T(8,128)} %p_ref.3) | copy-start | bytes 9437188
  2.6 23.6 %copy-start.4 = (s32[48,7]{0,1:T(8,128)S(1)}, s32[48,7]{0,1:T(8,128)}, u32[]{:S(2)}) copy-start(s32[48,7]{0,1:T(8,128)} %param.9) | copy-start | bytes 4036
  2.6 23.9 %copy-start.3 = (s32[48,7]{0,1:T(8,128)S(1)}, s32[48,7]{0,1:T(8,128)}, u32[]{:S(2)}) copy-start(s32[48,7]{0,1:T(8,128)} %param.7) | copy-start | bytes 4036
  2.6 24.1 %copy-start.1 = (f32[48,128,128]{2,1,0:T(8,128)S(1)}, f32[48,128,128]{2,1,0:T(8,128)}, u32[]{:S(2)}) copy-start(f32[48,128,128]{2,1,0:T(8,128)} %p_ref.3) | copy-start | bytes 9437188
  4.9 44.0 %collective-permute-start.2 = (f32[22,128,128]{2,1,0:T(8,128)}, f32[22,128,128]{2,1,0:T(8,128)}, u32[]{:S(2)}, u32[]{:S(2)}) collective-permute-start(f32[22,128,128]{2,1,0:T(8,128)} %get-tuple-element.45), channel_id=1, source_target_pairs={{0,1},{1,2},{2,3},{3,4},{4,5},{5,6},{6,7},{7,8},{8,9},{9,10},{10,1... | collective-permute-start | bytes 4325384 | tf_op jit(solution)/shard_map/ppermute | solution.py:287
  8.4 40.6 %collective-permute-start.3 = (f32[22,128,128]{2,1,0:T(8,128)}, f32[22,128,128]{2,1,0:T(8,128)}, u32[]{:S(2)}, u32[]{:S(2)}) collective-permute-start(f32[22,128,128]{2,1,0:T(8,128)} %get-tuple-element.46), channel_id=1, source_target_pairs={{1,0},{2,1},{3,2},{4,3},{5,4},{6,5},{7,6},{8,7},{9,8},{10,9},{11,1... | collective-permute-start | bytes 4325384 | tf_op jit(solution)/shard_map/ppermute | solution.py:287
  16.4 41.9 %collective-permute-start = (f32[10,128,128]{2,1,0:T(8,128)}, f32[10,128,128]{2,1,0:T(8,128)}, u32[]{:S(2)}, u32[]{:S(2)}) collective-permute-start(f32[10,128,128]{2,1,0:T(8,128)} %get-tuple-element.43), channel_id=1, source_target_pairs={{0,1},{1,2},{2,3},{3,4},{4,5},{5,6},{6,7},{7,8},{8,9},{9,10},{10,1... | collective-permute-start | bytes 1966088 | tf_op jit(solution)/shard_map/ppermute | solution.py:287
  18.3 41.4 %collective-permute-start.1 = (f32[10,128,128]{2,1,0:T(8,128)}, f32[10,128,128]{2,1,0:T(8,128)}, u32[]{:S(2)}, u32[]{:S(2)}) collective-permute-start(f32[10,128,128]{2,1,0:T(8,128)} %get-tuple-element.44), channel_id=1, source_target_pairs={{1,0},{2,1},{3,2},{4,3},{5,4},{6,5},{7,6},{8,7},{9,8},{10,9},{11,1... | collective-permute-start | bytes 1966088 | tf_op jit(solution)/shard_map/ppermute | solution.py:287
  61.2 24.2 %collective-permute-start.4 = (f32[16,128,128]{2,1,0:T(8,128)S(1)}, f32[16,128,128]{2,1,0:T(8,128)S(1)}, u32[]{:S(2)}, u32[]{:S(2)}) collective-permute-start(f32[16,128,128]{2,1,0:T(8,128)S(1)} %get-tuple-element.68), channel_id=1, source_target_pairs={{0,12},{1,13},{2,14},{3,15},{4,0},{5,1},{6,2},{7,3},{8,4},{9,5},{1... | collective-permute-start | bytes 3145736 | tf_op jit(solution)/shard_map/ppermute | solution.py:270
  62.4 25.1 %collective-permute-start.5 = (f32[16,128,128]{2,1,0:T(8,128)S(1)}, f32[16,128,128]{2,1,0:T(8,128)S(1)}, u32[]{:S(2)}, u32[]{:S(2)}) collective-permute-start(f32[16,128,128]{2,1,0:T(8,128)S(1)} %get-tuple-element.70), channel_id=1, source_target_pairs={{0,4},{1,5},{2,6},{3,7},{4,8},{5,9},{6,10},{7,11},{8,12},{9,13},{1... | collective-permute-start | bytes 3145736 | tf_op jit(solution)/shard_map/ppermute | solution.py:270
  63.3 26.1 %collective-permute-start.16 = (f32[16,128,128]{2,1,0:T(8,128)S(1)}, f32[16,128,128]{2,1,0:T(8,128)S(1)}, u32[]{:S(2)}, u32[]{:S(2)}) collective-permute-start(f32[16,128,128]{2,1,0:T(8,128)S(1)} %get-tuple-element.73), channel_id=1, source_target_pairs={{0,3},{1,0},{2,1},{3,2},{4,7},{5,4},{6,5},{7,6},{8,11},{9,8},{10,9... | collective-permute-start | bytes 3145736 | tf_op jit(solution)/shard_map/ppermute | solution.py:270
  66.7 26.7 %collective-permute-start.17 = (f32[16,128,128]{2,1,0:T(8,128)S(1)}, f32[16,128,128]{2,1,0:T(8,128)S(1)}, u32[]{:S(2)}, u32[]{:S(2)}) collective-permute-start(f32[16,128,128]{2,1,0:T(8,128)S(1)} %get-tuple-element.75), channel_id=1, source_target_pairs={{0,1},{1,2},{2,3},{3,0},{4,5},{5,6},{6,7},{7,4},{8,9},{9,10},{10,1... | collective-permute-start | bytes 3145736 | tf_op jit(solution)/shard_map/ppermute | solution.py:270
  85.5 12.1 %collective-permute-start.9 = (f32[8,128,128]{2,1,0:T(8,128)S(1)}, f32[8,128,128]{2,1,0:T(8,128)S(1)}, u32[]{:S(2)}, u32[]{:S(2)}) collective-permute-start(f32[8,128,128]{2,1,0:T(8,128)S(1)} %slice_add_fusion.4), channel_id=1, source_target_pairs={{0,12},{1,13},{2,14},{3,15},{4,0},{5,1},{6,2},{7,3},{8,4},{9,5},{1... | collective-permute-start | bytes 1572872 | tf_op jit(solution)/shard_map/ppermute | solution.py:270
  87.6 12.6 %collective-permute-start.6 = (f32[8,128,128]{2,1,0:T(8,128)S(1)}, f32[8,128,128]{2,1,0:T(8,128)S(1)}, u32[]{:S(2)}, u32[]{:S(2)}) collective-permute-start(f32[8,128,128]{2,1,0:T(8,128)S(1)} %slice_add_fusion.6), channel_id=1, source_target_pairs={{0,4},{1,5},{2,6},{3,7},{4,8},{5,9},{6,10},{7,11},{8,12},{9,13},{1... | collective-permute-start | bytes 1572872 | tf_op jit(solution)/shard_map/ppermute | solution.py:270
  89.5 19.9 %collective-permute-start.21 = (f32[8,128,128]{2,1,0:T(8,128)S(1)}, f32[8,128,128]{2,1,0:T(8,128)S(1)}, u32[]{:S(2)}, u32[]{:S(2)}) collective-permute-start(f32[8,128,128]{2,1,0:T(8,128)S(1)} %slice_add_fusion), channel_id=1, source_target_pairs={{0,3},{1,0},{2,1},{3,2},{4,7},{5,4},{6,5},{7,6},{8,11},{9,8},{10,9... | collective-permute-start | bytes 1572872 | tf_op jit(solution)/shard_map/ppermute | solution.py:270
  93.5 15.9 %collective-permute-start.18 = (f32[8,128,128]{2,1,0:T(8,128)S(1)}, f32[8,128,128]{2,1,0:T(8,128)S(1)}, u32[]{:S(2)}, u32[]{:S(2)}) collective-permute-start(f32[8,128,128]{2,1,0:T(8,128)S(1)} %slice_add_fusion.2), channel_id=1, source_target_pairs={{0,1},{1,2},{2,3},{3,0},{4,5},{5,6},{6,7},{7,4},{8,9},{9,10},{10,1... | collective-permute-start | bytes 1572872 | tf_op jit(solution)/shard_map/ppermute | solution.py:270
  100.3 16.7 %collective-permute-start.7 = (f32[8,128,128]{2,1,0:T(8,128)S(1)}, f32[8,128,128]{2,1,0:T(8,128)S(1)}, u32[]{:S(2)}, u32[]{:S(2)}) collective-permute-start(f32[8,128,128]{2,1,0:T(8,128)S(1)} %get-tuple-element.79), channel_id=1, source_target_pairs={{0,1},{1,0},{2,3},{3,2},{4,5},{5,4},{6,7},{7,6},{8,9},{9,8},{10,11... | collective-permute-start | bytes 1572872 | tf_op jit(solution)/shard_map/ppermute | solution.py:281
  103.0 20.3 %collective-permute-start.10 = (f32[8,128,128]{2,1,0:T(8,128)S(1)}, f32[8,128,128]{2,1,0:T(8,128)S(1)}, u32[]{:S(2)}, u32[]{:S(2)}) collective-permute-start(f32[8,128,128]{2,1,0:T(8,128)S(1)} %get-tuple-element.80), channel_id=1, source_target_pairs={{0,3},{1,2},{2,1},{3,0},{4,7},{5,6},{6,5},{7,4},{8,11},{9,10},{10,... | collective-permute-start | bytes 1572872 | tf_op jit(solution)/shard_map/ppermute | solution.py:281
  109.6 13.9 %collective-permute-start.19 = (f32[8,128,128]{2,1,0:T(8,128)S(1)}, f32[8,128,128]{2,1,0:T(8,128)S(1)}, u32[]{:S(2)}, u32[]{:S(2)}) collective-permute-start(f32[8,128,128]{2,1,0:T(8,128)S(1)} %get-tuple-element.77), channel_id=1, source_target_pairs={{0,4},{1,5},{2,6},{3,7},{4,0},{5,1},{6,2},{7,3},{8,12},{9,13},{10,... | collective-permute-start | bytes 1572872 | tf_op jit(solution)/shard_map/ppermute | solution.py:281
  109.7 16.6 %collective-permute-start.22 = (f32[8,128,128]{2,1,0:T(8,128)S(1)}, f32[8,128,128]{2,1,0:T(8,128)S(1)}, u32[]{:S(2)}, u32[]{:S(2)}) collective-permute-start(f32[8,128,128]{2,1,0:T(8,128)S(1)} %get-tuple-element.78), channel_id=1, source_target_pairs={{0,12},{1,13},{2,14},{3,15},{4,8},{5,9},{6,10},{7,11},{8,4},{9,5},... | collective-permute-start | bytes 1572872 | tf_op jit(solution)/shard_map/ppermute | solution.py:281
  117.1 17.5 %collective-permute-start.8 = (f32[8,128,128]{2,1,0:T(8,128)S(1)}, f32[8,128,128]{2,1,0:T(8,128)S(1)}, u32[]{:S(2)}, u32[]{:S(2)}) collective-permute-start(f32[8,128,128]{2,1,0:T(8,128)S(1)} %add.148), channel_id=1, source_target_pairs={{0,3},{1,2},{2,1},{3,0},{4,7},{5,6},{6,5},{7,4},{8,11},{9,10},{10,... | collective-permute-start | bytes 1572872 | tf_op jit(solution)/shard_map/ppermute | solution.py:281
  123.4 12.8 %collective-permute-start.11 = (f32[8,128,128]{2,1,0:T(8,128)S(1)}, f32[8,128,128]{2,1,0:T(8,128)S(1)}, u32[]{:S(2)}, u32[]{:S(2)}) collective-permute-start(f32[8,128,128]{2,1,0:T(8,128)S(1)} %add.153), channel_id=1, source_target_pairs={{0,1},{1,0},{2,3},{3,2},{4,5},{5,4},{6,7},{7,6},{8,9},{9,8},{10,11... | collective-permute-start | bytes 1572872 | tf_op jit(solution)/shard_map/ppermute | solution.py:281
  123.6 14.9 %collective-permute-start.20 = (f32[8,128,128]{2,1,0:T(8,128)S(1)}, f32[8,128,128]{2,1,0:T(8,128)S(1)}, u32[]{:S(2)}, u32[]{:S(2)}) collective-permute-start(f32[8,128,128]{2,1,0:T(8,128)S(1)} %add.158), channel_id=1, source_target_pairs={{0,12},{1,13},{2,14},{3,15},{4,8},{5,9},{6,10},{7,11},{8,4},{9,5},... | collective-permute-start | bytes 1572872 | tf_op jit(solution)/shard_map/ppermute | solution.py:281
  126.4 13.0 %collective-permute-start.23 = (f32[8,128,128]{2,1,0:T(8,128)S(1)}, f32[8,128,128]{2,1,0:T(8,128)S(1)}, u32[]{:S(2)}, u32[]{:S(2)}) collective-permute-start(f32[8,128,128]{2,1,0:T(8,128)S(1)} %add.163), channel_id=1, source_target_pairs={{0,4},{1,5},{2,6},{3,7},{4,0},{5,1},{6,2},{7,3},{8,12},{9,13},{10,... | collective-permute-start | bytes 1572872 | tf_op jit(solution)/shard_map/ppermute | solution.py:281
  136.4 24.4 %collective-permute-start.14 = (f32[16,128,128]{2,1,0:T(8,128)S(1)}, f32[16,128,128]{2,1,0:T(8,128)S(1)}, u32[]{:S(2)}, u32[]{:S(2)}) collective-permute-start(f32[16,128,128]{2,1,0:T(8,128)S(1)} %pad_maximum_fusion.refs_0_), channel_id=1, source_target_pairs={{0,12},{1,13},{2,14},{3,15},{4,0},{5,1},{6,2},{7,3},{8,4},{9,5},{1... | collective-permute-start | bytes 3145736 | tf_op jit(solution)/shard_map/ppermute | solution.py:270
  137.5 25.1 %collective-permute-start.12 = (f32[16,128,128]{2,1,0:T(8,128)S(1)}, f32[16,128,128]{2,1,0:T(8,128)S(1)}, u32[]{:S(2)}, u32[]{:S(2)}) collective-permute-start(f32[16,128,128]{2,1,0:T(8,128)S(1)} %pad_maximum_fusion.refs_0_), channel_id=1, source_target_pairs={{0,4},{1,5},{2,6},{3,7},{4,8},{5,9},{6,10},{7,11},{8,12},{9,13},{1... | collective-permute-start | bytes 3145736 | tf_op jit(solution)/shard_map/ppermute | solution.py:270
  139.6 23.4 %collective-permute-start.26 = (f32[16,128,128]{2,1,0:T(8,128)S(1)}, f32[16,128,128]{2,1,0:T(8,128)S(1)}, u32[]{:S(2)}, u32[]{:S(2)}) collective-permute-start(f32[16,128,128]{2,1,0:T(8,128)S(1)} %pad_maximum_fusion.1.refs_3_), channel_id=1, source_target_pairs={{0,3},{1,0},{2,1},{3,2},{4,7},{5,4},{6,5},{7,6},{8,11},{9,8},{10,9... | collective-permute-start | bytes 3145736 | tf_op jit(solution)/shard_map/ppermute | solution.py:270
  140.2 24.1 %collective-permute-start.24 = (f32[16,128,128]{2,1,0:T(8,128)S(1)}, f32[16,128,128]{2,1,0:T(8,128)S(1)}, u32[]{:S(2)}, u32[]{:S(2)}) collective-permute-start(f32[16,128,128]{2,1,0:T(8,128)S(1)} %pad_maximum_fusion.1.refs_3_), channel_id=1, source_target_pairs={{0,1},{1,2},{2,3},{3,0},{4,5},{5,6},{6,7},{7,4},{8,9},{9,10},{10,1... | collective-permute-start | bytes 3145736 | tf_op jit(solution)/shard_map/ppermute | solution.py:270
  160.8 12.2 %collective-permute-start.15 = (f32[8,128,128]{2,1,0:T(8,128)S(1)}, f32[8,128,128]{2,1,0:T(8,128)S(1)}, u32[]{:S(2)}, u32[]{:S(2)}) collective-permute-start(f32[8,128,128]{2,1,0:T(8,128)S(1)} %slice.69), channel_id=1, source_target_pairs={{0,12},{1,13},{2,14},{3,15},{4,0},{5,1},{6,2},{7,3},{8,4},{9,5},{1... | collective-permute-start | bytes 1572872 | tf_op jit(solution)/shard_map/ppermute | solution.py:270
  162.7 12.6 %collective-permute-start.13 = (f32[8,128,128]{2,1,0:T(8,128)S(1)}, f32[8,128,128]{2,1,0:T(8,128)S(1)}, u32[]{:S(2)}, u32[]{:S(2)}) collective-permute-start(f32[8,128,128]{2,1,0:T(8,128)S(1)} %slice.68), channel_id=1, source_target_pairs={{0,4},{1,5},{2,6},{3,7},{4,8},{5,9},{6,10},{7,11},{8,12},{9,13},{1... | collective-permute-start | bytes 1572872 | tf_op jit(solution)/shard_map/ppermute | solution.py:270
  163.0 12.3 %collective-permute-start.27 = (f32[8,128,128]{2,1,0:T(8,128)S(1)}, f32[8,128,128]{2,1,0:T(8,128)S(1)}, u32[]{:S(2)}, u32[]{:S(2)}) collective-permute-start(f32[8,128,128]{2,1,0:T(8,128)S(1)} %slice.75), channel_id=1, source_target_pairs={{0,3},{1,0},{2,1},{3,2},{4,7},{5,4},{6,5},{7,6},{8,11},{9,8},{10,9... | collective-permute-start | bytes 1572872 | tf_op jit(solution)/shard_map/ppermute | solution.py:270
  164.4 11.6 %collective-permute-start.25 = (f32[8,128,128]{2,1,0:T(8,128)S(1)}, f32[8,128,128]{2,1,0:T(8,128)S(1)}, u32[]{:S(2)}, u32[]{:S(2)}) collective-permute-start(f32[8,128,128]{2,1,0:T(8,128)S(1)} %slice.74), channel_id=1, source_target_pairs={{0,1},{1,2},{2,3},{3,0},{4,5},{5,6},{6,7},{7,4},{8,9},{9,10},{10,1... | collective-permute-start | bytes 1572872 | tf_op jit(solution)/shard_map/ppermute | solution.py:270
  (1 other events, 0.7 us)

commit v4 on v3

--- a/solution.py
+++ b/solution.py
@@ -36,10 +36,14 @@
     return fold(jnp.dot(left_pair, right_pair, preferred_element_type=F32))
 
 
-def choose_kernel(first, send_ref, p_ref, low_ref, up_ref):
+def choose_kernel(first, send_ref, p_ref, low_ref, up_ref, sem):
+    outs = (low_ref, up_ref)
     for j in range(low_ref.shape[0]):
-        for side, out in enumerate((low_ref, up_ref)):
-            out[j] = p_ref[jnp.maximum(send_ref[side, first + j], 0)]
+        for side, out in enumerate(outs):
+            tile = jnp.maximum(send_ref[side, first + j], 0)
+            pltpu.make_async_copy(p_ref.at[tile], out.at[j], sem.at[side]).start()
+    for side, out in enumerate(outs):
+        pltpu.make_async_copy(p_ref.at[pl.ds(0, out.shape[0])], out, sem.at[side]).wait()
 
 
 def choose(send, p_tiles, first, size):
@@ -49,9 +53,10 @@
         functools.partial(choose_kernel, first),
         name="choose",
         out_shape=(out, out),
-        in_specs=[pl.BlockSpec(memory_space=pltpu.SMEM), vmem],
+        in_specs=[pl.BlockSpec(memory_space=pltpu.SMEM), pl.BlockSpec(memory_space=pl.ANY)],
         out_specs=(vmem, vmem),
-        compiler_params=pltpu.CompilerParams(vmem_limit_bytes=24 * MB),
+        scratch_shapes=[pltpu.SemaphoreType.DMA((2,))],
+        compiler_params=pltpu.CompilerParams(vmem_limit_bytes=58 * MB),
         cost_estimate=pl.CostEstimate(flops=0, bytes_accessed=10**6, transcendentals=0),
     )(send, p_tiles)
 
@@ -287,7 +292,7 @@
     return lax.ppermute(block, axis, pairs)
 
 
-FIRST = 22
+FIRST = 20
 LANES = 2
 LAYOUT = (6, 7, 4, 1, 0, 2, 3, 5)
 

time: 180 us -> 179 us (level); the launches traced: 178 us -> 179 us
  Pallas kernels: 42.8 us -> 47.3 us
  waiting for transfers between devices: 68.2 us -> 65.3 us
  local copies, waits for them, and re-layouts: 3.14 us -> 0.57 us
  starting transfers between devices: 61.6 us -> 64 us
    pallas_call x2, Pallas kernels: 4.03 us -> 8.2 us  [choose(): pl.pallas_call(functools.partial(choose_kernel, first), name='choose', ou...]
    unnamed x11 -> x7, local copies, waits for them, and re-layouts: 2.67 us -> 0.1 us
    ppermute x8, starting transfers between devices: 22 us -> 24.5 us  [swap(): return lax.ppermute(block, 'bulk', pairs)]
    ppermute x4, waiting for transfers between devices: 6.25 us -> 4.44 us  [shifted(): return lax.ppermute(block, axis, pairs)]
  transfers between devices with their start and end apart: 28 -> 28, of which waited for: 15 -> 15; matrix products, arithmetic and copies ran while one was open for 1% -> 1% of each run, Pallas kernels for 21% -> 22%
where the time goes in v4:
time: 179 us
  waiting for transfers between devices  65.3 us (36%)
  starting transfers between devices  64 us (36%)
  Pallas kernels  47.3 us (26%)
    ppermute x16, waiting for transfers between devices, push(): return lax.ppermute(block, 'bulk', route(dx, dy))  47.3 us
    ppermute x8, starting transfers between devices, swap(): return lax.ppermute(block, 'bulk', pairs)  24.5 us
    pallas_call x1, Pallas kernels, local_part(): pl.pallas_call(local_kernel, name='local_part', grid_spec=pltpu.PrefetchS...  22.2 us
    ppermute x16, starting transfers between devices, push(): return lax.ppermute(block, 'bulk', route(dx, dy))  20 us
    ppermute x4, starting transfers between devices, shifted(): return lax.ppermute(block, axis, pairs)  19.6 us
    ppermute x8, waiting for transfers between devices, swap(): return lax.ppermute(block, 'bulk', pairs)  13.6 us
    pallas_call x4, Pallas kernels, remote_part(): pl.pallas_call(functools.partial(remote_kernel, first, base), name='remot...  12.2 us
    pallas_call x2, Pallas kernels, choose(): pl.pallas_call(functools.partial(choose_kernel, first), name='choose', ou...  8.2 us
  transfers between devices with their start and end apart: 28, of which 15 were waited for; matrix products, arithmetic and copies ran while one was open for 1% of the time, Pallas kernels for 22%

profile of v4, /device:TPU:32, one launch (start us, length us, event | category | flops | bytes accessed | tf_op | source)
XLA Modules:
  0.0 179.1 jit_solution(6549324201185659412)
XLA Ops:
  0.0 4.2 %choose.3 = (f32[20,128,128]{2,1,0:T(8,128)}, f32[20,128,128]{2,1,0:T(8,128)}) custom-call(s32[2,32]{1,0:T(2,128)} %bitcast.1, f32[48,128,128]{2,1,0:T(8,128)} %p_ref.3), custom_call_target="tpu_custom_call" | custom-call | bytes 1000000 | tf_op jit(solution)/shard_map/choose/pallas_call | solution.py:52
  4.2 3.5 %collective-permute-start.2 = (f32[20,128,128]{2,1,0:T(8,128)}, f32[20,128,128]{2,1,0:T(8,128)}, u32[]{:S(2)}, u32[]{:S(2)}) collective-permute-start(f32[20,128,128]{2,1,0:T(8,128)} %get-tuple-element.45), channel_id=1, source_target_pairs={{0,1},{1,2},{2,3},{3,4},{4,5},{5,6},{6,7},{7,8},{8,9},{9,10},{10,1... | collective-permute-start | bytes 3932168 | tf_op jit(solution)/shard_map/ppermute | solution.py:292
  7.7 6.3 %collective-permute-start.3 = (f32[20,128,128]{2,1,0:T(8,128)}, f32[20,128,128]{2,1,0:T(8,128)}, u32[]{:S(2)}, u32[]{:S(2)}) collective-permute-start(f32[20,128,128]{2,1,0:T(8,128)} %get-tuple-element.46), channel_id=1, source_target_pairs={{1,0},{2,1},{3,2},{4,3},{5,4},{6,5},{7,6},{8,7},{9,8},{10,9},{11,1... | collective-permute-start | bytes 3932168 | tf_op jit(solution)/shard_map/ppermute | solution.py:292
  14.0 4.0 %choose.2 = (f32[12,128,128]{2,1,0:T(8,128)}, f32[12,128,128]{2,1,0:T(8,128)}) custom-call(s32[2,32]{1,0:T(2,128)} %bitcast.2, f32[48,128,128]{2,1,0:T(8,128)} %p_ref.3), custom_call_target="tpu_custom_call" | custom-call | bytes 1000000 | tf_op jit(solution)/shard_map/choose/pallas_call | solution.py:52
  18.0 1.9 %collective-permute-start = (f32[12,128,128]{2,1,0:T(8,128)}, f32[12,128,128]{2,1,0:T(8,128)}, u32[]{:S(2)}, u32[]{:S(2)}) collective-permute-start(f32[12,128,128]{2,1,0:T(8,128)} %get-tuple-element.43), channel_id=1, source_target_pairs={{0,1},{1,2},{2,3},{3,4},{4,5},{5,6},{6,7},{7,8},{8,9},{9,10},{10,1... | collective-permute-start | bytes 2359304 | tf_op jit(solution)/shard_map/ppermute | solution.py:292
  20.0 7.9 %collective-permute-start.1 = (f32[12,128,128]{2,1,0:T(8,128)}, f32[12,128,128]{2,1,0:T(8,128)}, u32[]{:S(2)}, u32[]{:S(2)}) collective-permute-start(f32[12,128,128]{2,1,0:T(8,128)} %get-tuple-element.44), channel_id=1, source_target_pairs={{1,0},{2,1},{3,2},{4,3},{5,4},{6,5},{7,6},{8,7},{9,8},{10,9},{11,1... | collective-permute-start | bytes 2359304 | tf_op jit(solution)/shard_map/ppermute | solution.py:292
  28.4 22.2 %local_part.1 = (f32[16,128,128]{2,1,0:T(8,128)S(1)}, f32[16,128,128]{2,1,0:T(8,128)S(1)}, f32[16,128,128]{2,1,0:T(8,128)S(1)}, f32[16,128,128]{2,1,0:T(8,128)S(...) custom-call(s32[336]{0:T(512)S(1)} %reshape.6.col_ref, ...), custom_call_target="tpu_custom_call" | custom-call | flops 1000000000 | bytes 10000000 | tf_op jit(solution)/shard_map/local_part/pallas_call | solution.py:131
  50.6 4.0 %remote_part.6 = (f32[16,128,128]{2,1,0:T(8,128)S(1)}, f32[16,128,128]{2,1,0:T(8,128)S(1)}, f32[16,128,128]{2,1,0:T(8,128)S(1)}, f32[16,128,128]{2,1,0:T(8,128)S(1)}) custom-call(s32[72]{0:T(128)S(1)} %get-tuple-element.41.slot_ref, ...), custom_call_target="tpu_custom_call", output_to_operand_aliasing={{0}: (4, {}), {1}: (5, {}), {2}: (6, {}), {3}: (7, {})} | custom-call | flops 100000000 | bytes 1000000 | tf_op jit(solution)/shard_map/remote_part/pallas_call | solution.py:206
  54.5 3.1 %collective-permute-done.lower_ref = f32[12,128,128]{2,1,0:T(8,128)} collective-permute-done((f32[12,128,128]{2,1,0:T(8,128)}, f32[12,128,128]{2,1,0:T(8,128)}, u32[]{:S(2)}, u32[]{:S(2)}) %collective-permute-start) | collective-permute-done | bytes 786464 | tf_op jit(solution)/shard_map/ppermute | solution.py:292
  59.0 2.0 %remote_part.7 = (f32[16,128,128]{2,1,0:T(8,128)S(1)}, f32[16,128,128]{2,1,0:T(8,128)S(1)}, f32[16,128,128]{2,1,0:T(8,128)S(1)}, f32[16,128,128]{2,1,0:T(8,128)S(1)}) custom-call(s32[72]{0:T(128)S(1)} %get-tuple-element.41.slot_ref, ...), custom_call_target="tpu_custom_call", output_to_operand_aliasing={{0}: (4, {}), {1}: (5, {}), {2}: (6, {}), {3}: (7, {})} | custom-call | flops 100000000 | bytes 1000000 | tf_op jit(solution)/shard_map/remote_part/pallas_call | solution.py:206
  61.0 1.6 collective-permute-start.4
  63.1 2.6 %collective-permute-start.16 = (f32[16,128,128]{2,1,0:T(8,128)S(1)}, f32[16,128,128]{2,1,0:T(8,128)S(1)}, u32[]{:S(2)}, u32[]{:S(2)}) collective-permute-start(f32[16,128,128]{2,1,0:T(8,128)S(1)} %get-tuple-element.73), channel_id=1, source_target_pairs={{0,3},{1,0},{2,1},{3,2},{4,7},{5,4},{6,5},{7,6},{8,11},{9,8},{10,9... | collective-permute-start | bytes 3145736 | tf_op jit(solution)/shard_map/ppermute | solution.py:275
  65.7 4.2 %remote_part.4 = (f32[8,128,128]{2,1,0:T(8,128)S(1)}, f32[8,128,128]{2,1,0:T(8,128)S(1)}, f32[16,128,128]{2,1,0:T(8,128)S(1)}, f32[8,128,128]{2,1,0:T(8,128)S(1)...) custom-call(s32[72]{0:T(128)S(1)} %get-tuple-element.41.slot_ref, ...), custom_call_target="tpu_custom_call", output_to_operand_aliasing={{0}: (4, {}), {1}: (5, {}), {2}: (6, {}), {3}: (7, {}), {4}... | custom-call | flops 100000000 | bytes 1000000 | tf_op jit(solution)/shard_map/remote_part/pallas_call | solution.py:206
  69.9 2.0 %remote_part.5 = (f32[8,128,128]{2,1,0:T(8,128)S(1)}, f32[8,128,128]{2,1,0:T(8,128)S(1)}, f32[16,128,128]{2,1,0:T(8,128)S(1)}, f32[8,128,128]{2,1,0:T(8,128)S(1)...) custom-call(s32[72]{0:T(128)S(1)} %get-tuple-element.41.slot_ref, ...), custom_call_target="tpu_custom_call", output_to_operand_aliasing={{0}: (4, {}), {1}: (5, {}), {2}: (6, {}), {3}: (7, {}), {4}... | custom-call | flops 100000000 | bytes 1000000 | tf_op jit(solution)/shard_map/remote_part/pallas_call | solution.py:206
  72.0 12.5 %collective-permute-done.4 = f32[16,128,128]{2,1,0:T(8,128)S(1)} collective-permute-done((f32[16,128,128]{2,1,0:T(8,128)S(1)}, f32[16,128,128]{2,1,0:T(8,128)S(1)}, u32[]{:S(2)}, u32[]{:S(2)}) %collective-permute-start.4) | collective-permute-done | bytes 1048608 | tf_op jit(solution)/shard_map/ppermute | solution.py:275
  84.6 2.7 %collective-permute-start.9 = (f32[8,128,128]{2,1,0:T(8,128)S(1)}, f32[8,128,128]{2,1,0:T(8,128)S(1)}, u32[]{:S(2)}, u32[]{:S(2)}) collective-permute-start(f32[8,128,128]{2,1,0:T(8,128)S(1)} %slice_add_fusion.4), channel_id=1, source_target_pairs={{0,12},{1,13},{2,14},{3,15},{4,0},{5,1},{6,2},{7,3},{8,4},{9,5},{1... | collective-permute-start | bytes 1572872 | tf_op jit(solution)/shard_map/ppermute | solution.py:275
  87.6 3.9 %collective-permute-start.21 = (f32[8,128,128]{2,1,0:T(8,128)S(1)}, f32[8,128,128]{2,1,0:T(8,128)S(1)}, u32[]{:S(2)}, u32[]{:S(2)}) collective-permute-start(f32[8,128,128]{2,1,0:T(8,128)S(1)} %slice_add_fusion), channel_id=1, source_target_pairs={{0,3},{1,0},{2,1},{3,2},{4,7},{5,4},{6,5},{7,6},{8,11},{9,8},{10,9... | collective-permute-start | bytes 1572872 | tf_op jit(solution)/shard_map/ppermute | solution.py:275
  91.6 4.3 %collective-permute-done.9 = f32[8,128,128]{2,1,0:T(8,128)S(1)} collective-permute-done((f32[8,128,128]{2,1,0:T(8,128)S(1)}, f32[8,128,128]{2,1,0:T(8,128)S(1)}, u32[]{:S(2)}, u32[]{:S(2)}) %collective-permute-start.9) | collective-permute-done | bytes 524320 | tf_op jit(solution)/shard_map/ppermute | solution.py:275
  96.0 3.6 %collective-permute-done.6 = f32[8,128,128]{2,1,0:T(8,128)S(1)} collective-permute-done((f32[8,128,128]{2,1,0:T(8,128)S(1)}, f32[8,128,128]{2,1,0:T(8,128)S(1)}, u32[]{:S(2)}, u32[]{:S(2)}) %collective-permute-start.6) | collective-permute-done | bytes 524320 | tf_op jit(solution)/shard_map/ppermute | solution.py:275
  99.8 1.6 collective-permute-start.7
  101.4 5.7 %collective-permute-start.10 = (f32[8,128,128]{2,1,0:T(8,128)S(1)}, f32[8,128,128]{2,1,0:T(8,128)S(1)}, u32[]{:S(2)}, u32[]{:S(2)}) collective-permute-start(f32[8,128,128]{2,1,0:T(8,128)S(1)} %get-tuple-element.80), channel_id=1, source_target_pairs={{0,3},{1,2},{2,1},{3,0},{4,7},{5,6},{6,5},{7,4},{8,11},{9,10},{10,... | collective-permute-start | bytes 1572872 | tf_op jit(solution)/shard_map/ppermute | solution.py:286
  108.8 4.5 %collective-permute-start.22 = (f32[8,128,128]{2,1,0:T(8,128)S(1)}, f32[8,128,128]{2,1,0:T(8,128)S(1)}, u32[]{:S(2)}, u32[]{:S(2)}) collective-permute-start(f32[8,128,128]{2,1,0:T(8,128)S(1)} %get-tuple-element.78), channel_id=1, source_target_pairs={{0,12},{1,13},{2,14},{3,15},{4,8},{5,9},{6,10},{7,11},{8,4},{9,5},... | collective-permute-start | bytes 1572872 | tf_op jit(solution)/shard_map/ppermute | solution.py:286
  114.4 7.0 %collective-permute-start.8 = (f32[8,128,128]{2,1,0:T(8,128)S(1)}, f32[8,128,128]{2,1,0:T(8,128)S(1)}, u32[]{:S(2)}, u32[]{:S(2)}) collective-permute-start(f32[8,128,128]{2,1,0:T(8,128)S(1)} %add.148), channel_id=1, source_target_pairs={{0,3},{1,2},{2,1},{3,0},{4,7},{5,6},{6,5},{7,4},{8,11},{9,10},{10,... | collective-permute-start | bytes 1572872 | tf_op jit(solution)/shard_map/ppermute | solution.py:286
  121.7 4.1 %collective-permute-start.20 = (f32[8,128,128]{2,1,0:T(8,128)S(1)}, f32[8,128,128]{2,1,0:T(8,128)S(1)}, u32[]{:S(2)}, u32[]{:S(2)}) collective-permute-start(f32[8,128,128]{2,1,0:T(8,128)S(1)} %add.158), channel_id=1, source_target_pairs={{0,12},{1,13},{2,14},{3,15},{4,8},{5,9},{6,10},{7,11},{8,4},{9,5},... | collective-permute-start | bytes 1572872 | tf_op jit(solution)/shard_map/ppermute | solution.py:286
  126.0 7.2 %collective-permute-done.8 = f32[8,128,128]{2,1,0:T(8,128)S(1)} collective-permute-done((f32[8,128,128]{2,1,0:T(8,128)S(1)}, f32[8,128,128]{2,1,0:T(8,128)S(1)}, u32[]{:S(2)}, u32[]{:S(2)}) %collective-permute-start.8) | collective-permute-done | bytes 524320 | tf_op jit(solution)/shard_map/ppermute | solution.py:286
  135.1 1.7 collective-permute-start.14
  137.8 3.1 %collective-permute-done.23 = f32[8,128,128]{2,1,0:T(8,128)S(1)} collective-permute-done((f32[8,128,128]{2,1,0:T(8,128)S(1)}, f32[8,128,128]{2,1,0:T(8,128)S(1)}, u32[]{:S(2)}, u32[]{:S(2)}) %collective-permute-start.23) | collective-permute-done | bytes 524320 | tf_op jit(solution)/shard_map/ppermute | solution.py:286
  141.1 2.0 %collective-permute-start.24 = (f32[16,128,128]{2,1,0:T(8,128)S(1)}, f32[16,128,128]{2,1,0:T(8,128)S(1)}, u32[]{:S(2)}, u32[]{:S(2)}) collective-permute-start(f32[16,128,128]{2,1,0:T(8,128)S(1)} %pad_maximum_fusion.1.refs_3_), channel_id=1, source_target_pairs={{0,1},{1,2},{2,3},{3,0},{4,5},{5,6},{6,7},{7,4},{8,9},{9,10},{10,1... | collective-permute-start | bytes 3145736 | tf_op jit(solution)/shard_map/ppermute | solution.py:275
  143.1 18.7 %collective-permute-done.14.refs_2_ = f32[16,128,128]{2,1,0:T(8,128)S(1)} collective-permute-done((f32[16,128,128]{2,1,0:T(8,128)S(1)}, f32[16,128,128]{2,1,0:T(8,128)S(1)}, u32[]{:S(2)}, u32[]{:S(2)}) %collective-permute-start.14) | collective-permute-done | bytes 1048608 | tf_op jit(solution)/shard_map/ppermute | solution.py:275
  166.3 3.2 %place.2.refs_4_ = f32[128,128,128]{2,1,0:T(8,128)} custom-call(f32[16,128,128]{2,1,0:T(8,128)S(1)} %pad_maximum_fusion.refs_0_, f32[16,128,128]{2,1,0:T(8,128)S(1)} %collective-permute-done.12.refs_1_, f32[16,128,128]{2,1,0:T(8,128)S(1)} %collective-permute-done.14.refs_2_, f32[16,128,128]{2,1,0:T(8,128)S(1)} %pad_maximum_fusion.1.refs_3_, ...), custom_call_target="tpu_custom_call" | custom-call | bytes 12582912 | tf_op jit(solution)/shard_map/place/pallas_call | solution.py:248
  169.5 4.8 %collective-permute-done.15.refs_1_ = f32[8,128,128]{2,1,0:T(8,128)S(1)} collective-permute-done((f32[8,128,128]{2,1,0:T(8,128)S(1)}, f32[8,128,128]{2,1,0:T(8,128)S(1)}, u32[]{:S(2)}, u32[]{:S(2)}) %collective-permute-start.15) | collective-permute-done | bytes 524320 | tf_op jit(solution)/shard_map/ppermute | solution.py:275
  174.3 3.0 %collective-permute-done.13.refs_0_ = f32[8,128,128]{2,1,0:T(8,128)S(1)} collective-permute-done((f32[8,128,128]{2,1,0:T(8,128)S(1)}, f32[8,128,128]{2,1,0:T(8,128)S(1)}, u32[]{:S(2)}, u32[]{:S(2)}) %collective-permute-start.13) | collective-permute-done | bytes 524320 | tf_op jit(solution)/shard_map/ppermute | solution.py:275
  (64 shorter events, 15.6 us)
Async XLA Ops:
  0.0 27.8 %copy-start.2 = (s32[48,7]{0,1:T(8,128)S(1)}, s32[48,7]{0,1:T(8,128)}, u32[]{:S(2)}) copy-start(s32[48,7]{0,1:T(8,128)} %param.9) | copy-start | bytes 4036
  0.0 28.1 %copy-start.1 = (s32[48,7]{0,1:T(8,128)S(1)}, s32[48,7]{0,1:T(8,128)}, u32[]{:S(2)}) copy-start(s32[48,7]{0,1:T(8,128)} %param.7) | copy-start | bytes 4036
  0.0 28.3 %copy-start = (f32[48,128,128]{2,1,0:T(8,128)S(1)}, f32[48,128,128]{2,1,0:T(8,128)}, u32[]{:S(2)}) copy-start(f32[48,128,128]{2,1,0:T(8,128)} %p_ref.3) | copy-start | bytes 9437188
  4.2 46.4 %collective-permute-start.2 = (f32[20,128,128]{2,1,0:T(8,128)}, f32[20,128,128]{2,1,0:T(8,128)}, u32[]{:S(2)}, u32[]{:S(2)}) collective-permute-start(f32[20,128,128]{2,1,0:T(8,128)} %get-tuple-element.45), channel_id=1, source_target_pairs={{0,1},{1,2},{2,3},{3,4},{4,5},{5,6},{6,7},{7,8},{8,9},{9,10},{10,1... | collective-permute-start | bytes 3932168 | tf_op jit(solution)/shard_map/ppermute | solution.py:292
  7.7 42.9 %collective-permute-start.3 = (f32[20,128,128]{2,1,0:T(8,128)}, f32[20,128,128]{2,1,0:T(8,128)}, u32[]{:S(2)}, u32[]{:S(2)}) collective-permute-start(f32[20,128,128]{2,1,0:T(8,128)} %get-tuple-element.46), channel_id=1, source_target_pairs={{1,0},{2,1},{3,2},{4,3},{5,4},{6,5},{7,6},{8,7},{9,8},{10,9},{11,1... | collective-permute-start | bytes 3932168 | tf_op jit(solution)/shard_map/ppermute | solution.py:292
  18.0 39.6 %collective-permute-start = (f32[12,128,128]{2,1,0:T(8,128)}, f32[12,128,128]{2,1,0:T(8,128)}, u32[]{:S(2)}, u32[]{:S(2)}) collective-permute-start(f32[12,128,128]{2,1,0:T(8,128)} %get-tuple-element.43), channel_id=1, source_target_pairs={{0,1},{1,2},{2,3},{3,4},{4,5},{5,6},{6,7},{7,8},{8,9},{9,10},{10,1... | collective-permute-start | bytes 2359304 | tf_op jit(solution)/shard_map/ppermute | solution.py:292
  20.0 39.0 %collective-permute-start.1 = (f32[12,128,128]{2,1,0:T(8,128)}, f32[12,128,128]{2,1,0:T(8,128)}, u32[]{:S(2)}, u32[]{:S(2)}) collective-permute-start(f32[12,128,128]{2,1,0:T(8,128)} %get-tuple-element.44), channel_id=1, source_target_pairs={{1,0},{2,1},{3,2},{4,3},{5,4},{6,5},{7,6},{8,7},{9,8},{10,9},{11,1... | collective-permute-start | bytes 2359304 | tf_op jit(solution)/shard_map/ppermute | solution.py:292
  61.0 23.5 %collective-permute-start.4 = (f32[16,128,128]{2,1,0:T(8,128)S(1)}, f32[16,128,128]{2,1,0:T(8,128)S(1)}, u32[]{:S(2)}, u32[]{:S(2)}) collective-permute-start(f32[16,128,128]{2,1,0:T(8,128)S(1)} %get-tuple-element.68), channel_id=1, source_target_pairs={{0,12},{1,13},{2,14},{3,15},{4,0},{5,1},{6,2},{7,3},{8,4},{9,5},{1... | collective-permute-start | bytes 3145736 | tf_op jit(solution)/shard_map/ppermute | solution.py:275
  62.6 24.7 %collective-permute-start.5 = (f32[16,128,128]{2,1,0:T(8,128)S(1)}, f32[16,128,128]{2,1,0:T(8,128)S(1)}, u32[]{:S(2)}, u32[]{:S(2)}) collective-permute-start(f32[16,128,128]{2,1,0:T(8,128)S(1)} %get-tuple-element.70), channel_id=1, source_target_pairs={{0,4},{1,5},{2,6},{3,7},{4,8},{5,9},{6,10},{7,11},{8,12},{9,13},{1... | collective-permute-start | bytes 3145736 | tf_op jit(solution)/shard_map/ppermute | solution.py:275
  63.1 24.4 %collective-permute-start.16 = (f32[16,128,128]{2,1,0:T(8,128)S(1)}, f32[16,128,128]{2,1,0:T(8,128)S(1)}, u32[]{:S(2)}, u32[]{:S(2)}) collective-permute-start(f32[16,128,128]{2,1,0:T(8,128)S(1)} %get-tuple-element.73), channel_id=1, source_target_pairs={{0,3},{1,0},{2,1},{3,2},{4,7},{5,4},{6,5},{7,6},{8,11},{9,8},{10,9... | collective-permute-start | bytes 3145736 | tf_op jit(solution)/shard_map/ppermute | solution.py:275
  65.7 25.8 %collective-permute-start.17 = (f32[16,128,128]{2,1,0:T(8,128)S(1)}, f32[16,128,128]{2,1,0:T(8,128)S(1)}, u32[]{:S(2)}, u32[]{:S(2)}) collective-permute-start(f32[16,128,128]{2,1,0:T(8,128)S(1)} %get-tuple-element.75), channel_id=1, source_target_pairs={{0,1},{1,2},{2,3},{3,0},{4,5},{5,6},{6,7},{7,4},{8,9},{9,10},{10,1... | collective-permute-start | bytes 3145736 | tf_op jit(solution)/shard_map/ppermute | solution.py:275
  84.6 11.4 %collective-permute-start.9 = (f32[8,128,128]{2,1,0:T(8,128)S(1)}, f32[8,128,128]{2,1,0:T(8,128)S(1)}, u32[]{:S(2)}, u32[]{:S(2)}) collective-permute-start(f32[8,128,128]{2,1,0:T(8,128)S(1)} %slice_add_fusion.4), channel_id=1, source_target_pairs={{0,12},{1,13},{2,14},{3,15},{4,0},{5,1},{6,2},{7,3},{8,4},{9,5},{1... | collective-permute-start | bytes 1572872 | tf_op jit(solution)/shard_map/ppermute | solution.py:275
  87.4 12.2 %collective-permute-start.6 = (f32[8,128,128]{2,1,0:T(8,128)S(1)}, f32[8,128,128]{2,1,0:T(8,128)S(1)}, u32[]{:S(2)}, u32[]{:S(2)}) collective-permute-start(f32[8,128,128]{2,1,0:T(8,128)S(1)} %slice_add_fusion.6), channel_id=1, source_target_pairs={{0,4},{1,5},{2,6},{3,7},{4,8},{5,9},{6,10},{7,11},{8,12},{9,13},{1... | collective-permute-start | bytes 1572872 | tf_op jit(solution)/shard_map/ppermute | solution.py:275
  87.6 19.5 %collective-permute-start.21 = (f32[8,128,128]{2,1,0:T(8,128)S(1)}, f32[8,128,128]{2,1,0:T(8,128)S(1)}, u32[]{:S(2)}, u32[]{:S(2)}) collective-permute-start(f32[8,128,128]{2,1,0:T(8,128)S(1)} %slice_add_fusion), channel_id=1, source_target_pairs={{0,3},{1,0},{2,1},{3,2},{4,7},{5,4},{6,5},{7,6},{8,11},{9,8},{10,9... | collective-permute-start | bytes 1572872 | tf_op jit(solution)/shard_map/ppermute | solution.py:275
  91.6 15.6 %collective-permute-start.18 = (f32[8,128,128]{2,1,0:T(8,128)S(1)}, f32[8,128,128]{2,1,0:T(8,128)S(1)}, u32[]{:S(2)}, u32[]{:S(2)}) collective-permute-start(f32[8,128,128]{2,1,0:T(8,128)S(1)} %slice_add_fusion.2), channel_id=1, source_target_pairs={{0,1},{1,2},{2,3},{3,0},{4,5},{5,6},{6,7},{7,4},{8,9},{9,10},{10,1... | collective-permute-start | bytes 1572872 | tf_op jit(solution)/shard_map/ppermute | solution.py:275
  99.8 14.6 %collective-permute-start.7 = (f32[8,128,128]{2,1,0:T(8,128)S(1)}, f32[8,128,128]{2,1,0:T(8,128)S(1)}, u32[]{:S(2)}, u32[]{:S(2)}) collective-permute-start(f32[8,128,128]{2,1,0:T(8,128)S(1)} %get-tuple-element.79), channel_id=1, source_target_pairs={{0,1},{1,0},{2,3},{3,2},{4,5},{5,4},{6,7},{7,6},{8,9},{9,8},{10,11... | collective-permute-start | bytes 1572872 | tf_op jit(solution)/shard_map/ppermute | solution.py:286
  101.4 20.1 %collective-permute-start.10 = (f32[8,128,128]{2,1,0:T(8,128)S(1)}, f32[8,128,128]{2,1,0:T(8,128)S(1)}, u32[]{:S(2)}, u32[]{:S(2)}) collective-permute-start(f32[8,128,128]{2,1,0:T(8,128)S(1)} %get-tuple-element.80), channel_id=1, source_target_pairs={{0,3},{1,2},{2,1},{3,0},{4,7},{5,6},{6,5},{7,4},{8,11},{9,10},{10,... | collective-permute-start | bytes 1572872 | tf_op jit(solution)/shard_map/ppermute | solution.py:286
  107.3 14.3 %collective-permute-start.19 = (f32[8,128,128]{2,1,0:T(8,128)S(1)}, f32[8,128,128]{2,1,0:T(8,128)S(1)}, u32[]{:S(2)}, u32[]{:S(2)}) collective-permute-start(f32[8,128,128]{2,1,0:T(8,128)S(1)} %get-tuple-element.77), channel_id=1, source_target_pairs={{0,4},{1,5},{2,6},{3,7},{4,0},{5,1},{6,2},{7,3},{8,12},{9,13},{10,... | collective-permute-start | bytes 1572872 | tf_op jit(solution)/shard_map/ppermute | solution.py:286
  108.8 17.1 %collective-permute-start.22 = (f32[8,128,128]{2,1,0:T(8,128)S(1)}, f32[8,128,128]{2,1,0:T(8,128)S(1)}, u32[]{:S(2)}, u32[]{:S(2)}) collective-permute-start(f32[8,128,128]{2,1,0:T(8,128)S(1)} %get-tuple-element.78), channel_id=1, source_target_pairs={{0,12},{1,13},{2,14},{3,15},{4,8},{5,9},{6,10},{7,11},{8,4},{9,5},... | collective-permute-start | bytes 1572872 | tf_op jit(solution)/shard_map/ppermute | solution.py:286
  114.4 18.8 %collective-permute-start.8 = (f32[8,128,128]{2,1,0:T(8,128)S(1)}, f32[8,128,128]{2,1,0:T(8,128)S(1)}, u32[]{:S(2)}, u32[]{:S(2)}) collective-permute-start(f32[8,128,128]{2,1,0:T(8,128)S(1)} %add.148), channel_id=1, source_target_pairs={{0,3},{1,2},{2,1},{3,0},{4,7},{5,6},{6,5},{7,4},{8,11},{9,10},{10,... | collective-permute-start | bytes 1572872 | tf_op jit(solution)/shard_map/ppermute | solution.py:286
  121.5 13.4 %collective-permute-start.11 = (f32[8,128,128]{2,1,0:T(8,128)S(1)}, f32[8,128,128]{2,1,0:T(8,128)S(1)}, u32[]{:S(2)}, u32[]{:S(2)}) collective-permute-start(f32[8,128,128]{2,1,0:T(8,128)S(1)} %add.153), channel_id=1, source_target_pairs={{0,1},{1,0},{2,3},{3,2},{4,5},{5,4},{6,7},{7,6},{8,9},{9,8},{10,11... | collective-permute-start | bytes 1572872 | tf_op jit(solution)/shard_map/ppermute | solution.py:286
  121.7 16.0 %collective-permute-start.20 = (f32[8,128,128]{2,1,0:T(8,128)S(1)}, f32[8,128,128]{2,1,0:T(8,128)S(1)}, u32[]{:S(2)}, u32[]{:S(2)}) collective-permute-start(f32[8,128,128]{2,1,0:T(8,128)S(1)} %add.158), channel_id=1, source_target_pairs={{0,12},{1,13},{2,14},{3,15},{4,8},{5,9},{6,10},{7,11},{8,4},{9,5},... | collective-permute-start | bytes 1572872 | tf_op jit(solution)/shard_map/ppermute | solution.py:286
  125.9 14.9 %collective-permute-start.23 = (f32[8,128,128]{2,1,0:T(8,128)S(1)}, f32[8,128,128]{2,1,0:T(8,128)S(1)}, u32[]{:S(2)}, u32[]{:S(2)}) collective-permute-start(f32[8,128,128]{2,1,0:T(8,128)S(1)} %add.163), channel_id=1, source_target_pairs={{0,4},{1,5},{2,6},{3,7},{4,0},{5,1},{6,2},{7,3},{8,12},{9,13},{10,... | collective-permute-start | bytes 1572872 | tf_op jit(solution)/shard_map/ppermute | solution.py:286
  135.1 26.7 %collective-permute-start.14 = (f32[16,128,128]{2,1,0:T(8,128)S(1)}, f32[16,128,128]{2,1,0:T(8,128)S(1)}, u32[]{:S(2)}, u32[]{:S(2)}) collective-permute-start(f32[16,128,128]{2,1,0:T(8,128)S(1)} %pad_maximum_fusion.refs_0_), channel_id=1, source_target_pairs={{0,12},{1,13},{2,14},{3,15},{4,0},{5,1},{6,2},{7,3},{8,4},{9,5},{1... | collective-permute-start | bytes 3145736 | tf_op jit(solution)/shard_map/ppermute | solution.py:275
  136.8 26.5 %collective-permute-start.12 = (f32[16,128,128]{2,1,0:T(8,128)S(1)}, f32[16,128,128]{2,1,0:T(8,128)S(1)}, u32[]{:S(2)}, u32[]{:S(2)}) collective-permute-start(f32[16,128,128]{2,1,0:T(8,128)S(1)} %pad_maximum_fusion.refs_0_), channel_id=1, source_target_pairs={{0,4},{1,5},{2,6},{3,7},{4,8},{5,9},{6,10},{7,11},{8,12},{9,13},{1... | collective-permute-start | bytes 3145736 | tf_op jit(solution)/shard_map/ppermute | solution.py:275
  141.0 23.0 %collective-permute-start.26 = (f32[16,128,128]{2,1,0:T(8,128)S(1)}, f32[16,128,128]{2,1,0:T(8,128)S(1)}, u32[]{:S(2)}, u32[]{:S(2)}) collective-permute-start(f32[16,128,128]{2,1,0:T(8,128)S(1)} %pad_maximum_fusion.1.refs_3_), channel_id=1, source_target_pairs={{0,3},{1,0},{2,1},{3,2},{4,7},{5,4},{6,5},{7,6},{8,11},{9,8},{10,9... | collective-permute-start | bytes 3145736 | tf_op jit(solution)/shard_map/ppermute | solution.py:275
  141.1 23.7 %collective-permute-start.24 = (f32[16,128,128]{2,1,0:T(8,128)S(1)}, f32[16,128,128]{2,1,0:T(8,128)S(1)}, u32[]{:S(2)}, u32[]{:S(2)}) collective-permute-start(f32[16,128,128]{2,1,0:T(8,128)S(1)} %pad_maximum_fusion.1.refs_3_), channel_id=1, source_target_pairs={{0,1},{1,2},{2,3},{3,0},{4,5},{5,6},{6,7},{7,4},{8,9},{9,10},{10,1... | collective-permute-start | bytes 3145736 | tf_op jit(solution)/shard_map/ppermute | solution.py:275
  161.8 12.5 %collective-permute-start.15 = (f32[8,128,128]{2,1,0:T(8,128)S(1)}, f32[8,128,128]{2,1,0:T(8,128)S(1)}, u32[]{:S(2)}, u32[]{:S(2)}) collective-permute-start(f32[8,128,128]{2,1,0:T(8,128)S(1)} %slice.69), channel_id=1, source_target_pairs={{0,12},{1,13},{2,14},{3,15},{4,0},{5,1},{6,2},{7,3},{8,4},{9,5},{1... | collective-permute-start | bytes 1572872 | tf_op jit(solution)/shard_map/ppermute | solution.py:275
  163.3 14.0 %collective-permute-start.13 = (f32[8,128,128]{2,1,0:T(8,128)S(1)}, f32[8,128,128]{2,1,0:T(8,128)S(1)}, u32[]{:S(2)}, u32[]{:S(2)}) collective-permute-start(f32[8,128,128]{2,1,0:T(8,128)S(1)} %slice.68), channel_id=1, source_target_pairs={{0,4},{1,5},{2,6},{3,7},{4,8},{5,9},{6,10},{7,11},{8,12},{9,13},{1... | collective-permute-start | bytes 1572872 | tf_op jit(solution)/shard_map/ppermute | solution.py:275
  164.1 13.2 %collective-permute-start.27 = (f32[8,128,128]{2,1,0:T(8,128)S(1)}, f32[8,128,128]{2,1,0:T(8,128)S(1)}, u32[]{:S(2)}, u32[]{:S(2)}) collective-permute-start(f32[8,128,128]{2,1,0:T(8,128)S(1)} %slice.75), channel_id=1, source_target_pairs={{0,3},{1,0},{2,1},{3,2},{4,7},{5,4},{6,5},{7,6},{8,11},{9,8},{10,9... | collective-permute-start | bytes 1572872 | tf_op jit(solution)/shard_map/ppermute | solution.py:275
  164.8 12.7 %collective-permute-start.25 = (f32[8,128,128]{2,1,0:T(8,128)S(1)}, f32[8,128,128]{2,1,0:T(8,128)S(1)}, u32[]{:S(2)}, u32[]{:S(2)}) collective-permute-start(f32[8,128,128]{2,1,0:T(8,128)S(1)} %slice.74), channel_id=1, source_target_pairs={{0,1},{1,2},{2,3},{3,0},{4,5},{5,6},{6,7},{7,4},{8,9},{9,10},{10,1... | collective-permute-start | bytes 1572872 | tf_op jit(solution)/shard_map/ppermute | solution.py:275

commit v5 on v4

--- a/solution.py
+++ b/solution.py
@@ -157,21 +157,20 @@
 GROUP = 4
 
 
-def remote_kernel(first, base, slot_ref, left_ref, lower_ref, upper_ref, *refs):
+def remote_kernel(first, base, slot_ref, left_ref, received_ref, *refs):
     parts, todo = refs[len(refs) // 2 : -1], refs[-1]
-    capacity = lower_ref.shape[0]
-    slots = (left_ref.shape[0] - 1) // 2
-    places = 2 * capacity + GROUP
+    capacity = received_ref.shape[0]
+    places = capacity + GROUP
     held = sum(part.shape[0] for part in parts)
 
     def find(j, n):
-        place = slot_ref[jnp.where(j < capacity, base + j, slots + base + j - capacity)] - first
+        place = slot_ref[base + j] - first
         wanted = (place >= 0) & (place < held)
         todo[n] = j
         todo[n + places] = place
         return n + wanted.astype(jnp.int32)
 
-    count = lax.fori_loop(0, 2 * capacity, find, jnp.int32(0))
+    count = lax.fori_loop(0, capacity, find, jnp.int32(0))
     for i in range(GROUP):
         todo[count + i] = 0
         todo[count + i + places] = -1
@@ -180,10 +179,7 @@
         terms = []
         for i in range(GROUP):
             j = todo[g * GROUP + i]
-            above = j >= capacity
-            k = jnp.where(above, j - capacity, j)
-            received = jnp.where(above, upper_ref[k], lower_ref[k])
-            terms.append(product(row_pair(left_ref[base + k + jnp.where(above, slots, 0)]), column_pair(received)))
+            terms.append(product(row_pair(left_ref[base + j]), column_pair(received_ref[j])))
         for i, term in enumerate(terms):
             place = todo[g * GROUP + i + places]
             start = 0
@@ -200,20 +196,20 @@
     lax.fori_loop(0, (count + GROUP - 1) // GROUP, step, 0)
 
 
-def remote_part(first, base, slots, left, lower, upper, parts):
+def remote_part(first, base, slots, left, received, parts):
     n = len(parts)
     vmem = pl.BlockSpec(memory_space=pltpu.VMEM)
     return pl.pallas_call(
         functools.partial(remote_kernel, first, base),
         name="remote_part",
         out_shape=tuple(jax.ShapeDtypeStruct(part.shape, F32) for part in parts),
-        in_specs=[pl.BlockSpec(memory_space=pltpu.SMEM)] + [vmem] * (3 + n),
+        in_specs=[pl.BlockSpec(memory_space=pltpu.SMEM)] + [vmem] * (2 + n),
         out_specs=(vmem,) * n,
-        scratch_shapes=[pltpu.SMEM((4 * lower.shape[0] + 2 * GROUP,), jnp.int32)],
-        input_output_aliases={4 + i: i for i in range(n)},
+        scratch_shapes=[pltpu.SMEM((2 * received.shape[0] + 2 * GROUP,), jnp.int32)],
+        input_output_aliases={3 + i: i for i in range(n)},
         compiler_params=pltpu.CompilerParams(vmem_limit_bytes=24 * MB),
         cost_estimate=pl.CostEstimate(flops=10**8, bytes_accessed=10**6, transcendentals=0),
-    )(slots, left, lower, upper, *parts)
+    )(slots, left, received, *parts)
 
 
 def place_kernel(pieces, *refs):
@@ -322,10 +318,11 @@
         col_ref.reshape(-1), target.reshape(-1), p_tiles, a_tiles, early_sizes + late_sizes, 2 * capacity
     )
     early, late = parts[: len(early_sizes)], parts[len(early_sizes) :]
-    early = remote_part(0, 0, slot_tile, left, *halo[0], early)
-    late = remote_part(mid, 0, slot_tile, left, *halo[0], late)
-    firsts = remote_part(0, FIRST, slot_tile, left, *halo[1], early)
-    rests = remote_part(mid, FIRST, slot_tile, left, *halo[1], late)
+    firsts, rests = early, late
+    for base, received in ((0, halo[0]), (FIRST, halo[1])):
+        for side, tiles_in in enumerate(received):
+            firsts = remote_part(0, side * capacity + base, slot_tile, left, tiles_in, firsts)
+            rests = remote_part(mid, side * capacity + base, slot_tile, left, tiles_in, rests)
 
     owned = []
     arrived = [

time: 179 us -> 180 us (level); the launches traced: 179 us -> 178 us
  starting transfers between devices: 64 us -> 59.9 us
  Pallas kernels: 47.3 us -> 50.6 us
    pallas_call x4 -> x8, Pallas kernels: 12.2 us -> 16.1 us  [remote_part(): pl.pallas_call(functools.partial(remote_kernel, first, base), name='remot...]
    ppermute x8, starting transfers between devices: 24.5 us -> 20.9 us  [swap(): return lax.ppermute(block, 'bulk', pairs)]
    ppermute x4, waiting for transfers between devices: 4.44 us -> 2.43 us  [shifted(): return lax.ppermute(block, axis, pairs)]
  transfers between devices with their start and end apart: 28 -> 28, of which waited for: 15 -> 12; matrix products, arithmetic and copies ran while one was open for 1% -> 1% of each run, Pallas kernels for 22% -> 25%
where the time goes in v5:
time: 180 us; the launch traced here: 178 us
  waiting for transfers between devices  64.7 us (36%)
  starting transfers between devices  59.9 us (33%)
  Pallas kernels  50.6 us (28%)
    ppermute x16, waiting for transfers between devices, push(): return lax.ppermute(block, 'bulk', route(dx, dy))  47.7 us
    pallas_call x1, Pallas kernels, local_part(): pl.pallas_call(local_kernel, name='local_part', grid_spec=pltpu.PrefetchS...  22.2 us
    ppermute x8, starting transfers between devices, swap(): return lax.ppermute(block, 'bulk', pairs)  20.9 us
    ppermute x4, starting transfers between devices, shifted(): return lax.ppermute(block, axis, pairs)  19.6 us
    ppermute x16, starting transfers between devices, push(): return lax.ppermute(block, 'bulk', route(dx, dy))  19.5 us
    pallas_call x8, Pallas kernels, remote_part(): pl.pallas_call(functools.partial(remote_kernel, first, base), name='remot...  16.1 us
    ppermute x8, waiting for transfers between devices, swap(): return lax.ppermute(block, 'bulk', pairs)  14.6 us
    pallas_call x2, Pallas kernels, choose(): pl.pallas_call(functools.partial(choose_kernel, first), name='choose', ou...  7.64 us
  transfers between devices with their start and end apart: 28, of which 12 were waited for; matrix products, arithmetic and copies ran while one was open for 1% of the time, Pallas kernels for 25%

profile of v5, /device:TPU:32, one launch (start us, length us, event | category | flops | bytes accessed | tf_op | source)
XLA Modules:
  0.0 177.9 jit_solution(8521603813555691239)
XLA Ops:
  0.0 4.2 %choose.3 = (f32[20,128,128]{2,1,0:T(8,128)}, f32[20,128,128]{2,1,0:T(8,128)}) custom-call(s32[2,32]{1,0:T(2,128)} %bitcast.1, f32[48,128,128]{2,1,0:T(8,128)} %p_ref.3), custom_call_target="tpu_custom_call" | custom-call | bytes 1000000 | tf_op jit(solution)/shard_map/choose/pallas_call | solution.py:52
  4.2 3.5 %collective-permute-start.3 = (f32[20,128,128]{2,1,0:T(8,128)}, f32[20,128,128]{2,1,0:T(8,128)}, u32[]{:S(2)}, u32[]{:S(2)}) collective-permute-start(f32[20,128,128]{2,1,0:T(8,128)} %get-tuple-element.66), channel_id=1, source_target_pairs={{0,1},{1,2},{2,3},{3,4},{4,5},{5,6},{6,7},{7,8},{8,9},{9,10},{10,1... | collective-permute-start | bytes 3932168 | tf_op jit(solution)/shard_map/ppermute | solution.py:288
  7.7 6.3 %collective-permute-start.2 = (f32[20,128,128]{2,1,0:T(8,128)}, f32[20,128,128]{2,1,0:T(8,128)}, u32[]{:S(2)}, u32[]{:S(2)}) collective-permute-start(f32[20,128,128]{2,1,0:T(8,128)} %get-tuple-element.65), channel_id=1, source_target_pairs={{1,0},{2,1},{3,2},{4,3},{5,4},{6,5},{7,6},{8,7},{9,8},{10,9},{11,1... | collective-permute-start | bytes 3932168 | tf_op jit(solution)/shard_map/ppermute | solution.py:288
  14.0 3.5 %choose.2 = (f32[12,128,128]{2,1,0:T(8,128)}, f32[12,128,128]{2,1,0:T(8,128)}) custom-call(s32[2,32]{1,0:T(2,128)} %bitcast.2, f32[48,128,128]{2,1,0:T(8,128)} %p_ref.3), custom_call_target="tpu_custom_call" | custom-call | bytes 1000000 | tf_op jit(solution)/shard_map/choose/pallas_call | solution.py:52
  17.5 1.9 %collective-permute-start.1 = (f32[12,128,128]{2,1,0:T(8,128)}, f32[12,128,128]{2,1,0:T(8,128)}, u32[]{:S(2)}, u32[]{:S(2)}) collective-permute-start(f32[12,128,128]{2,1,0:T(8,128)} %get-tuple-element.64), channel_id=1, source_target_pairs={{0,1},{1,2},{2,3},{3,4},{4,5},{5,6},{6,7},{7,8},{8,9},{9,10},{10,1... | collective-permute-start | bytes 2359304 | tf_op jit(solution)/shard_map/ppermute | solution.py:288
  19.4 7.9 %collective-permute-start = (f32[12,128,128]{2,1,0:T(8,128)}, f32[12,128,128]{2,1,0:T(8,128)}, u32[]{:S(2)}, u32[]{:S(2)}) collective-permute-start(f32[12,128,128]{2,1,0:T(8,128)} %get-tuple-element.63), channel_id=1, source_target_pairs={{1,0},{2,1},{3,2},{4,3},{5,4},{6,5},{7,6},{8,7},{9,8},{10,9},{11,1... | collective-permute-start | bytes 2359304 | tf_op jit(solution)/shard_map/ppermute | solution.py:288
  27.8 22.2 %local_part.1 = (f32[16,128,128]{2,1,0:T(8,128)S(1)}, f32[16,128,128]{2,1,0:T(8,128)S(1)}, f32[16,128,128]{2,1,0:T(8,128)S(1)}, f32[16,128,128]{2,1,0:T(8,128)S(...) custom-call(s32[336]{0:T(512)S(1)} %reshape.6.col_ref, ...), custom_call_target="tpu_custom_call" | custom-call | flops 1000000000 | bytes 10000000 | tf_op jit(solution)/shard_map/local_part/pallas_call | solution.py:131
  50.0 2.9 %remote_part.12 = (f32[16,128,128]{2,1,0:T(8,128)S(1)}, f32[16,128,128]{2,1,0:T(8,128)S(1)}, f32[16,128,128]{2,1,0:T(8,128)S(1)}, f32[16,128,128]{2,1,0:T(8,128)S(1)}) custom-call(s32[72]{0:T(128)S(1)} %get-tuple-element.61.slot_ref, ...), custom_call_target="tpu_custom_call", output_to_operand_aliasing={{0}: (3, {}), {1}: (4, {}), {2}: (5, {}), {3}: (6, {})} | custom-call | flops 100000000 | bytes 1000000 | tf_op jit(solution)/shard_map/remote_part/pallas_call | solution.py:202
  53.0 2.2 %remote_part.13 = (f32[16,128,128]{2,1,0:T(8,128)S(1)}, f32[16,128,128]{2,1,0:T(8,128)S(1)}, f32[16,128,128]{2,1,0:T(8,128)S(1)}, f32[16,128,128]{2,1,0:T(8,128)S(1)}) custom-call(s32[72]{0:T(128)S(1)} %get-tuple-element.61.slot_ref, ...), custom_call_target="tpu_custom_call", output_to_operand_aliasing={{0}: (3, {}), {1}: (4, {}), {2}: (5, {}), {3}: (6, {})} | custom-call | flops 100000000 | bytes 1000000 | tf_op jit(solution)/shard_map/remote_part/pallas_call | solution.py:202
  55.2 2.4 %collective-permute-done.1.received_ref = f32[12,128,128]{2,1,0:T(8,128)} collective-permute-done((f32[12,128,128]{2,1,0:T(8,128)}, f32[12,128,128]{2,1,0:T(8,128)}, u32[]{:S(2)}, u32[]{:S(2)}) %collective-permute-start.1) | collective-permute-done | bytes 786464 | tf_op jit(solution)/shard_map/ppermute | solution.py:288
  57.6 1.6 remote_part.14
  60.5 1.8 collective-permute-start.4
  62.6 3.0 %collective-permute-start.16 = (f32[16,128,128]{2,1,0:T(8,128)S(1)}, f32[16,128,128]{2,1,0:T(8,128)S(1)}, u32[]{:S(2)}, u32[]{:S(2)}) collective-permute-start(f32[16,128,128]{2,1,0:T(8,128)S(1)} %get-tuple-element.113), channel_id=1, source_target_pairs={{0,3},{1,0},{2,1},{3,2},{4,7},{5,4},{6,5},{7,6},{8,11},{9,8},{10,9... | collective-permute-start | bytes 3145736 | tf_op jit(solution)/shard_map/ppermute | solution.py:271
  65.7 2.3 %remote_part.8 = (f32[8,128,128]{2,1,0:T(8,128)S(1)}, f32[8,128,128]{2,1,0:T(8,128)S(1)}, f32[16,128,128]{2,1,0:T(8,128)S(1)}, f32[8,128,128]{2,1,0:T(8,128)S(1)...) custom-call(s32[72]{0:T(128)S(1)} %get-tuple-element.61.slot_ref, ...), custom_call_target="tpu_custom_call", output_to_operand_aliasing={{0}: (3, {}), {1}: (4, {}), {2}: (5, {}), {3}: (6, {}), {4}... | custom-call | flops 100000000 | bytes 1000000 | tf_op jit(solution)/shard_map/remote_part/pallas_call | solution.py:202
  68.0 2.8 %remote_part.9 = (f32[8,128,128]{2,1,0:T(8,128)S(1)}, f32[8,128,128]{2,1,0:T(8,128)S(1)}, f32[16,128,128]{2,1,0:T(8,128)S(1)}, f32[8,128,128]{2,1,0:T(8,128)S(1)...) custom-call(s32[72]{0:T(128)S(1)} %get-tuple-element.61.slot_ref, ...), custom_call_target="tpu_custom_call", output_to_operand_aliasing={{0}: (3, {}), {1}: (4, {}), {2}: (5, {}), {3}: (6, {}), {4}... | custom-call | flops 100000000 | bytes 1000000 | tf_op jit(solution)/shard_map/remote_part/pallas_call | solution.py:202
  70.8 1.7 remote_part.10
  73.7 12.4 %collective-permute-done.4 = f32[16,128,128]{2,1,0:T(8,128)S(1)} collective-permute-done((f32[16,128,128]{2,1,0:T(8,128)S(1)}, f32[16,128,128]{2,1,0:T(8,128)S(1)}, u32[]{:S(2)}, u32[]{:S(2)}) %collective-permute-start.4) | collective-permute-done | bytes 1048608 | tf_op jit(solution)/shard_map/ppermute | solution.py:271
  88.5 3.4 %collective-permute-start.21 = (f32[8,128,128]{2,1,0:T(8,128)S(1)}, f32[8,128,128]{2,1,0:T(8,128)S(1)}, u32[]{:S(2)}, u32[]{:S(2)}) collective-permute-start(f32[8,128,128]{2,1,0:T(8,128)S(1)} %slice_add_fusion), channel_id=1, source_target_pairs={{0,3},{1,0},{2,1},{3,2},{4,7},{5,4},{6,5},{7,6},{8,11},{9,8},{10,9... | collective-permute-start | bytes 1572872 | tf_op jit(solution)/shard_map/ppermute | solution.py:271
  92.1 7.6 %collective-permute-done.9 = f32[8,128,128]{2,1,0:T(8,128)S(1)} collective-permute-done((f32[8,128,128]{2,1,0:T(8,128)S(1)}, f32[8,128,128]{2,1,0:T(8,128)S(1)}, u32[]{:S(2)}, u32[]{:S(2)}) %collective-permute-start.9) | collective-permute-done | bytes 524320 | tf_op jit(solution)/shard_map/ppermute | solution.py:271
  101.4 6.5 %collective-permute-start.10 = (f32[8,128,128]{2,1,0:T(8,128)S(1)}, f32[8,128,128]{2,1,0:T(8,128)S(1)}, u32[]{:S(2)}, u32[]{:S(2)}) collective-permute-start(f32[8,128,128]{2,1,0:T(8,128)S(1)} %get-tuple-element.120), channel_id=1, source_target_pairs={{0,3},{1,2},{2,1},{3,0},{4,7},{5,6},{6,5},{7,4},{8,11},{9,10},{10,... | collective-permute-start | bytes 1572872 | tf_op jit(solution)/shard_map/ppermute | solution.py:282
  108.3 4.0 %collective-permute-start.22 = (f32[8,128,128]{2,1,0:T(8,128)S(1)}, f32[8,128,128]{2,1,0:T(8,128)S(1)}, u32[]{:S(2)}, u32[]{:S(2)}) collective-permute-start(f32[8,128,128]{2,1,0:T(8,128)S(1)} %get-tuple-element.118), channel_id=1, source_target_pairs={{0,12},{1,13},{2,14},{3,15},{4,8},{5,9},{6,10},{7,11},{8,4},{9,5},... | collective-permute-start | bytes 1572872 | tf_op jit(solution)/shard_map/ppermute | solution.py:282
  112.2 3.0 %collective-permute-done.7 = f32[8,128,128]{2,1,0:T(8,128)S(1)} collective-permute-done((f32[8,128,128]{2,1,0:T(8,128)S(1)}, f32[8,128,128]{2,1,0:T(8,128)S(1)}, u32[]{:S(2)}, u32[]{:S(2)}) %collective-permute-start.7) | collective-permute-done | bytes 524320 | tf_op jit(solution)/shard_map/ppermute | solution.py:282
  115.4 6.7 %collective-permute-start.8 = (f32[8,128,128]{2,1,0:T(8,128)S(1)}, f32[8,128,128]{2,1,0:T(8,128)S(1)}, u32[]{:S(2)}, u32[]{:S(2)}) collective-permute-start(f32[8,128,128]{2,1,0:T(8,128)S(1)} %add.148), channel_id=1, source_target_pairs={{0,3},{1,2},{2,1},{3,0},{4,7},{5,6},{6,5},{7,4},{8,11},{9,10},{10,... | collective-permute-start | bytes 1572872 | tf_op jit(solution)/shard_map/ppermute | solution.py:282
  122.3 3.4 %collective-permute-start.20 = (f32[8,128,128]{2,1,0:T(8,128)S(1)}, f32[8,128,128]{2,1,0:T(8,128)S(1)}, u32[]{:S(2)}, u32[]{:S(2)}) collective-permute-start(f32[8,128,128]{2,1,0:T(8,128)S(1)} %add.158), channel_id=1, source_target_pairs={{0,12},{1,13},{2,14},{3,15},{4,8},{5,9},{6,10},{7,11},{8,4},{9,5},... | collective-permute-start | bytes 1572872 | tf_op jit(solution)/shard_map/ppermute | solution.py:282
  125.9 7.8 %collective-permute-done.8 = f32[8,128,128]{2,1,0:T(8,128)S(1)} collective-permute-done((f32[8,128,128]{2,1,0:T(8,128)S(1)}, f32[8,128,128]{2,1,0:T(8,128)S(1)}, u32[]{:S(2)}, u32[]{:S(2)}) %collective-permute-start.8) | collective-permute-done | bytes 524320 | tf_op jit(solution)/shard_map/ppermute | solution.py:282
  137.8 2.2 %collective-permute-done.23 = f32[8,128,128]{2,1,0:T(8,128)S(1)} collective-permute-done((f32[8,128,128]{2,1,0:T(8,128)S(1)}, f32[8,128,128]{2,1,0:T(8,128)S(1)}, u32[]{:S(2)}, u32[]{:S(2)}) %collective-permute-start.23) | collective-permute-done | bytes 524320 | tf_op jit(solution)/shard_map/ppermute | solution.py:282
  140.2 2.0 %collective-permute-start.24 = (f32[16,128,128]{2,1,0:T(8,128)S(1)}, f32[16,128,128]{2,1,0:T(8,128)S(1)}, u32[]{:S(2)}, u32[]{:S(2)}) collective-permute-start(f32[16,128,128]{2,1,0:T(8,128)S(1)} %pad_maximum_fusion.1.refs_3_), channel_id=1, source_target_pairs={{0,1},{1,2},{2,3},{3,0},{4,5},{5,6},{6,7},{7,4},{8,9},{9,10},{10,1... | collective-permute-start | bytes 3145736 | tf_op jit(solution)/shard_map/ppermute | solution.py:271
  142.2 18.5 %collective-permute-done.14.refs_2_ = f32[16,128,128]{2,1,0:T(8,128)S(1)} collective-permute-done((f32[16,128,128]{2,1,0:T(8,128)S(1)}, f32[16,128,128]{2,1,0:T(8,128)S(1)}, u32[]{:S(2)}, u32[]{:S(2)}) %collective-permute-start.14) | collective-permute-done | bytes 1048608 | tf_op jit(solution)/shard_map/ppermute | solution.py:271
  160.8 1.7 collective-permute-start.15
  165.3 3.2 %place.2.refs_4_ = f32[128,128,128]{2,1,0:T(8,128)} custom-call(f32[16,128,128]{2,1,0:T(8,128)S(1)} %pad_maximum_fusion.refs_0_, f32[16,128,128]{2,1,0:T(8,128)S(1)} %collective-permute-done.12.refs_1_, f32[16,128,128]{2,1,0:T(8,128)S(1)} %collective-permute-done.14.refs_2_, f32[16,128,128]{2,1,0:T(8,128)S(1)} %pad_maximum_fusion.1.refs_3_, ...), custom_call_target="tpu_custom_call" | custom-call | bytes 12582912 | tf_op jit(solution)/shard_map/place/pallas_call | solution.py:244
  168.5 4.7 %collective-permute-done.15.refs_1_ = f32[8,128,128]{2,1,0:T(8,128)S(1)} collective-permute-done((f32[8,128,128]{2,1,0:T(8,128)S(1)}, f32[8,128,128]{2,1,0:T(8,128)S(1)}, u32[]{:S(2)}, u32[]{:S(2)}) %collective-permute-start.15) | collective-permute-done | bytes 524320 | tf_op jit(solution)/shard_map/ppermute | solution.py:271
  173.1 2.4 %collective-permute-done.13.refs_0_ = f32[8,128,128]{2,1,0:T(8,128)S(1)} collective-permute-done((f32[8,128,128]{2,1,0:T(8,128)S(1)}, f32[8,128,128]{2,1,0:T(8,128)S(1)}, u32[]{:S(2)}, u32[]{:S(2)}) %collective-permute-start.13) | collective-permute-done | bytes 524320 | tf_op jit(solution)/shard_map/ppermute | solution.py:271
  (68 shorter events, 17.7 us)
Async XLA Ops:
  0.0 27.3 %copy-start.2 = (s32[48,7]{0,1:T(8,128)S(1)}, s32[48,7]{0,1:T(8,128)}, u32[]{:S(2)}) copy-start(s32[48,7]{0,1:T(8,128)} %param.9) | copy-start | bytes 4036
  0.0 27.6 %copy-start.1 = (s32[48,7]{0,1:T(8,128)S(1)}, s32[48,7]{0,1:T(8,128)}, u32[]{:S(2)}) copy-start(s32[48,7]{0,1:T(8,128)} %param.7) | copy-start | bytes 4036
  0.0 27.8 %copy-start = (f32[48,128,128]{2,1,0:T(8,128)S(1)}, f32[48,128,128]{2,1,0:T(8,128)}, u32[]{:S(2)}) copy-start(f32[48,128,128]{2,1,0:T(8,128)} %p_ref.3) | copy-start | bytes 9437188
  4.2 45.8 %collective-permute-start.3 = (f32[20,128,128]{2,1,0:T(8,128)}, f32[20,128,128]{2,1,0:T(8,128)}, u32[]{:S(2)}, u32[]{:S(2)}) collective-permute-start(f32[20,128,128]{2,1,0:T(8,128)} %get-tuple-element.66), channel_id=1, source_target_pairs={{0,1},{1,2},{2,3},{3,4},{4,5},{5,6},{6,7},{7,8},{8,9},{9,10},{10,1... | collective-permute-start | bytes 3932168 | tf_op jit(solution)/shard_map/ppermute | solution.py:288
  7.7 45.3 %collective-permute-start.2 = (f32[20,128,128]{2,1,0:T(8,128)}, f32[20,128,128]{2,1,0:T(8,128)}, u32[]{:S(2)}, u32[]{:S(2)}) collective-permute-start(f32[20,128,128]{2,1,0:T(8,128)} %get-tuple-element.65), channel_id=1, source_target_pairs={{1,0},{2,1},{3,2},{4,3},{5,4},{6,5},{7,6},{8,7},{9,8},{10,9},{11,1... | collective-permute-start | bytes 3932168 | tf_op jit(solution)/shard_map/ppermute | solution.py:288
  17.5 40.2 %collective-permute-start.1 = (f32[12,128,128]{2,1,0:T(8,128)}, f32[12,128,128]{2,1,0:T(8,128)}, u32[]{:S(2)}, u32[]{:S(2)}) collective-permute-start(f32[12,128,128]{2,1,0:T(8,128)} %get-tuple-element.64), channel_id=1, source_target_pairs={{0,1},{1,2},{2,3},{3,4},{4,5},{5,6},{6,7},{7,8},{8,9},{9,10},{10,1... | collective-permute-start | bytes 2359304 | tf_op jit(solution)/shard_map/ppermute | solution.py:288
  19.4 39.9 %collective-permute-start = (f32[12,128,128]{2,1,0:T(8,128)}, f32[12,128,128]{2,1,0:T(8,128)}, u32[]{:S(2)}, u32[]{:S(2)}) collective-permute-start(f32[12,128,128]{2,1,0:T(8,128)} %get-tuple-element.63), channel_id=1, source_target_pairs={{1,0},{2,1},{3,2},{4,3},{5,4},{6,5},{7,6},{8,7},{9,8},{10,9},{11,1... | collective-permute-start | bytes 2359304 | tf_op jit(solution)/shard_map/ppermute | solution.py:288
  60.5 25.6 %collective-permute-start.4 = (f32[16,128,128]{2,1,0:T(8,128)S(1)}, f32[16,128,128]{2,1,0:T(8,128)S(1)}, u32[]{:S(2)}, u32[]{:S(2)}) collective-permute-start(f32[16,128,128]{2,1,0:T(8,128)S(1)} %get-tuple-element.108), channel_id=1, source_target_pairs={{0,12},{1,13},{2,14},{3,15},{4,0},{5,1},{6,2},{7,3},{8,4},{9,5},{1... | collective-permute-start | bytes 3145736 | tf_op jit(solution)/shard_map/ppermute | solution.py:271
  62.3 25.4 %collective-permute-start.5 = (f32[16,128,128]{2,1,0:T(8,128)S(1)}, f32[16,128,128]{2,1,0:T(8,128)S(1)}, u32[]{:S(2)}, u32[]{:S(2)}) collective-permute-start(f32[16,128,128]{2,1,0:T(8,128)S(1)} %get-tuple-element.110), channel_id=1, source_target_pairs={{0,4},{1,5},{2,6},{3,7},{4,8},{5,9},{6,10},{7,11},{8,12},{9,13},{1... | collective-permute-start | bytes 3145736 | tf_op jit(solution)/shard_map/ppermute | solution.py:271
  62.6 25.8 %collective-permute-start.16 = (f32[16,128,128]{2,1,0:T(8,128)S(1)}, f32[16,128,128]{2,1,0:T(8,128)S(1)}, u32[]{:S(2)}, u32[]{:S(2)}) collective-permute-start(f32[16,128,128]{2,1,0:T(8,128)S(1)} %get-tuple-element.113), channel_id=1, source_target_pairs={{0,3},{1,0},{2,1},{3,2},{4,7},{5,4},{6,5},{7,6},{8,11},{9,8},{10,9... | collective-permute-start | bytes 3145736 | tf_op jit(solution)/shard_map/ppermute | solution.py:271
  65.7 26.2 %collective-permute-start.17 = (f32[16,128,128]{2,1,0:T(8,128)S(1)}, f32[16,128,128]{2,1,0:T(8,128)S(1)}, u32[]{:S(2)}, u32[]{:S(2)}) collective-permute-start(f32[16,128,128]{2,1,0:T(8,128)S(1)} %get-tuple-element.115), channel_id=1, source_target_pairs={{0,1},{1,2},{2,3},{3,0},{4,5},{5,6},{6,7},{7,4},{8,9},{9,10},{10,1... | collective-permute-start | bytes 3145736 | tf_op jit(solution)/shard_map/ppermute | solution.py:271
  86.2 13.5 %collective-permute-start.9 = (f32[8,128,128]{2,1,0:T(8,128)S(1)}, f32[8,128,128]{2,1,0:T(8,128)S(1)}, u32[]{:S(2)}, u32[]{:S(2)}) collective-permute-start(f32[8,128,128]{2,1,0:T(8,128)S(1)} %slice_add_fusion.4), channel_id=1, source_target_pairs={{0,12},{1,13},{2,14},{3,15},{4,0},{5,1},{6,2},{7,3},{8,4},{9,5},{1... | collective-permute-start | bytes 1572872 | tf_op jit(solution)/shard_map/ppermute | solution.py:271
  87.8 13.3 %collective-permute-start.6 = (f32[8,128,128]{2,1,0:T(8,128)S(1)}, f32[8,128,128]{2,1,0:T(8,128)S(1)}, u32[]{:S(2)}, u32[]{:S(2)}) collective-permute-start(f32[8,128,128]{2,1,0:T(8,128)S(1)} %slice_add_fusion.6), channel_id=1, source_target_pairs={{0,4},{1,5},{2,6},{3,7},{4,8},{5,9},{6,10},{7,11},{8,12},{9,13},{1... | collective-permute-start | bytes 1572872 | tf_op jit(solution)/shard_map/ppermute | solution.py:271
  88.5 19.4 %collective-permute-start.21 = (f32[8,128,128]{2,1,0:T(8,128)S(1)}, f32[8,128,128]{2,1,0:T(8,128)S(1)}, u32[]{:S(2)}, u32[]{:S(2)}) collective-permute-start(f32[8,128,128]{2,1,0:T(8,128)S(1)} %slice_add_fusion), channel_id=1, source_target_pairs={{0,3},{1,0},{2,1},{3,2},{4,7},{5,4},{6,5},{7,6},{8,11},{9,8},{10,9... | collective-permute-start | bytes 1572872 | tf_op jit(solution)/shard_map/ppermute | solution.py:271
  92.0 15.9 %collective-permute-start.18 = (f32[8,128,128]{2,1,0:T(8,128)S(1)}, f32[8,128,128]{2,1,0:T(8,128)S(1)}, u32[]{:S(2)}, u32[]{:S(2)}) collective-permute-start(f32[8,128,128]{2,1,0:T(8,128)S(1)} %slice_add_fusion.2), channel_id=1, source_target_pairs={{0,1},{1,2},{2,3},{3,0},{4,5},{5,6},{6,7},{7,4},{8,9},{9,10},{10,1... | collective-permute-start | bytes 1572872 | tf_op jit(solution)/shard_map/ppermute | solution.py:271
  101.3 13.9 %collective-permute-start.7 = (f32[8,128,128]{2,1,0:T(8,128)S(1)}, f32[8,128,128]{2,1,0:T(8,128)S(1)}, u32[]{:S(2)}, u32[]{:S(2)}) collective-permute-start(f32[8,128,128]{2,1,0:T(8,128)S(1)} %get-tuple-element.119), channel_id=1, source_target_pairs={{0,1},{1,0},{2,3},{3,2},{4,5},{5,4},{6,7},{7,6},{8,9},{9,8},{10,11... | collective-permute-start | bytes 1572872 | tf_op jit(solution)/shard_map/ppermute | solution.py:282
  101.4 20.6 %collective-permute-start.10 = (f32[8,128,128]{2,1,0:T(8,128)S(1)}, f32[8,128,128]{2,1,0:T(8,128)S(1)}, u32[]{:S(2)}, u32[]{:S(2)}) collective-permute-start(f32[8,128,128]{2,1,0:T(8,128)S(1)} %get-tuple-element.120), channel_id=1, source_target_pairs={{0,3},{1,2},{2,1},{3,0},{4,7},{5,6},{6,5},{7,4},{8,11},{9,10},{10,... | collective-permute-start | bytes 1572872 | tf_op jit(solution)/shard_map/ppermute | solution.py:282
  108.2 14.1 %collective-permute-start.19 = (f32[8,128,128]{2,1,0:T(8,128)S(1)}, f32[8,128,128]{2,1,0:T(8,128)S(1)}, u32[]{:S(2)}, u32[]{:S(2)}) collective-permute-start(f32[8,128,128]{2,1,0:T(8,128)S(1)} %get-tuple-element.117), channel_id=1, source_target_pairs={{0,4},{1,5},{2,6},{3,7},{4,0},{5,1},{6,2},{7,3},{8,12},{9,13},{10,... | collective-permute-start | bytes 1572872 | tf_op jit(solution)/shard_map/ppermute | solution.py:282
  108.3 17.4 %collective-permute-start.22 = (f32[8,128,128]{2,1,0:T(8,128)S(1)}, f32[8,128,128]{2,1,0:T(8,128)S(1)}, u32[]{:S(2)}, u32[]{:S(2)}) collective-permute-start(f32[8,128,128]{2,1,0:T(8,128)S(1)} %get-tuple-element.118), channel_id=1, source_target_pairs={{0,12},{1,13},{2,14},{3,15},{4,8},{5,9},{6,10},{7,11},{8,4},{9,5},... | collective-permute-start | bytes 1572872 | tf_op jit(solution)/shard_map/ppermute | solution.py:282
  115.4 18.3 %collective-permute-start.8 = (f32[8,128,128]{2,1,0:T(8,128)S(1)}, f32[8,128,128]{2,1,0:T(8,128)S(1)}, u32[]{:S(2)}, u32[]{:S(2)}) collective-permute-start(f32[8,128,128]{2,1,0:T(8,128)S(1)} %add.148), channel_id=1, source_target_pairs={{0,3},{1,2},{2,1},{3,0},{4,7},{5,6},{6,5},{7,4},{8,11},{9,10},{10,... | collective-permute-start | bytes 1572872 | tf_op jit(solution)/shard_map/ppermute | solution.py:282
  122.2 13.1 %collective-permute-start.11 = (f32[8,128,128]{2,1,0:T(8,128)S(1)}, f32[8,128,128]{2,1,0:T(8,128)S(1)}, u32[]{:S(2)}, u32[]{:S(2)}) collective-permute-start(f32[8,128,128]{2,1,0:T(8,128)S(1)} %add.153), channel_id=1, source_target_pairs={{0,1},{1,0},{2,3},{3,2},{4,5},{5,4},{6,7},{7,6},{8,9},{9,8},{10,11... | collective-permute-start | bytes 1572872 | tf_op jit(solution)/shard_map/ppermute | solution.py:282
  122.3 15.4 %collective-permute-start.20 = (f32[8,128,128]{2,1,0:T(8,128)S(1)}, f32[8,128,128]{2,1,0:T(8,128)S(1)}, u32[]{:S(2)}, u32[]{:S(2)}) collective-permute-start(f32[8,128,128]{2,1,0:T(8,128)S(1)} %add.158), channel_id=1, source_target_pairs={{0,12},{1,13},{2,14},{3,15},{4,8},{5,9},{6,10},{7,11},{8,4},{9,5},... | collective-permute-start | bytes 1572872 | tf_op jit(solution)/shard_map/ppermute | solution.py:282
  125.8 14.2 %collective-permute-start.23 = (f32[8,128,128]{2,1,0:T(8,128)S(1)}, f32[8,128,128]{2,1,0:T(8,128)S(1)}, u32[]{:S(2)}, u32[]{:S(2)}) collective-permute-start(f32[8,128,128]{2,1,0:T(8,128)S(1)} %add.163), channel_id=1, source_target_pairs={{0,4},{1,5},{2,6},{3,7},{4,0},{5,1},{6,2},{7,3},{8,12},{9,13},{10,... | collective-permute-start | bytes 1572872 | tf_op jit(solution)/shard_map/ppermute | solution.py:282
  135.4 25.3 %collective-permute-start.14 = (f32[16,128,128]{2,1,0:T(8,128)S(1)}, f32[16,128,128]{2,1,0:T(8,128)S(1)}, u32[]{:S(2)}, u32[]{:S(2)}) collective-permute-start(f32[16,128,128]{2,1,0:T(8,128)S(1)} %pad_maximum_fusion.refs_0_), channel_id=1, source_target_pairs={{0,12},{1,13},{2,14},{3,15},{4,0},{5,1},{6,2},{7,3},{8,4},{9,5},{1... | collective-permute-start | bytes 3145736 | tf_op jit(solution)/shard_map/ppermute | solution.py:271
  137.0 25.5 %collective-permute-start.12 = (f32[16,128,128]{2,1,0:T(8,128)S(1)}, f32[16,128,128]{2,1,0:T(8,128)S(1)}, u32[]{:S(2)}, u32[]{:S(2)}) collective-permute-start(f32[16,128,128]{2,1,0:T(8,128)S(1)} %pad_maximum_fusion.refs_0_), channel_id=1, source_target_pairs={{0,4},{1,5},{2,6},{3,7},{4,8},{5,9},{6,10},{7,11},{8,12},{9,13},{1... | collective-permute-start | bytes 3145736 | tf_op jit(solution)/shard_map/ppermute | solution.py:271
  140.1 22.9 %collective-permute-start.26 = (f32[16,128,128]{2,1,0:T(8,128)S(1)}, f32[16,128,128]{2,1,0:T(8,128)S(1)}, u32[]{:S(2)}, u32[]{:S(2)}) collective-permute-start(f32[16,128,128]{2,1,0:T(8,128)S(1)} %pad_maximum_fusion.1.refs_3_), channel_id=1, source_target_pairs={{0,3},{1,0},{2,1},{3,2},{4,7},{5,4},{6,5},{7,6},{8,11},{9,8},{10,9... | collective-permute-start | bytes 3145736 | tf_op jit(solution)/shard_map/ppermute | solution.py:271
  140.2 23.6 %collective-permute-start.24 = (f32[16,128,128]{2,1,0:T(8,128)S(1)}, f32[16,128,128]{2,1,0:T(8,128)S(1)}, u32[]{:S(2)}, u32[]{:S(2)}) collective-permute-start(f32[16,128,128]{2,1,0:T(8,128)S(1)} %pad_maximum_fusion.1.refs_3_), channel_id=1, source_target_pairs={{0,1},{1,2},{2,3},{3,0},{4,5},{5,6},{6,7},{7,4},{8,9},{9,10},{10,1... | collective-permute-start | bytes 3145736 | tf_op jit(solution)/shard_map/ppermute | solution.py:271
  160.8 12.3 %collective-permute-start.15 = (f32[8,128,128]{2,1,0:T(8,128)S(1)}, f32[8,128,128]{2,1,0:T(8,128)S(1)}, u32[]{:S(2)}, u32[]{:S(2)}) collective-permute-start(f32[8,128,128]{2,1,0:T(8,128)S(1)} %slice.69), channel_id=1, source_target_pairs={{0,12},{1,13},{2,14},{3,15},{4,0},{5,1},{6,2},{7,3},{8,4},{9,5},{1... | collective-permute-start | bytes 1572872 | tf_op jit(solution)/shard_map/ppermute | solution.py:271
  162.5 13.0 %collective-permute-start.13 = (f32[8,128,128]{2,1,0:T(8,128)S(1)}, f32[8,128,128]{2,1,0:T(8,128)S(1)}, u32[]{:S(2)}, u32[]{:S(2)}) collective-permute-start(f32[8,128,128]{2,1,0:T(8,128)S(1)} %slice.68), channel_id=1, source_target_pairs={{0,4},{1,5},{2,6},{3,7},{4,8},{5,9},{6,10},{7,11},{8,12},{9,13},{1... | collective-permute-start | bytes 1572872 | tf_op jit(solution)/shard_map/ppermute | solution.py:271
  163.1 12.5 %collective-permute-start.27 = (f32[8,128,128]{2,1,0:T(8,128)S(1)}, f32[8,128,128]{2,1,0:T(8,128)S(1)}, u32[]{:S(2)}, u32[]{:S(2)}) collective-permute-start(f32[8,128,128]{2,1,0:T(8,128)S(1)} %slice.75), channel_id=1, source_target_pairs={{0,3},{1,0},{2,1},{3,2},{4,7},{5,4},{6,5},{7,6},{8,11},{9,8},{10,9... | collective-permute-start | bytes 1572872 | tf_op jit(solution)/shard_map/ppermute | solution.py:271
  163.9 12.3 %collective-permute-start.25 = (f32[8,128,128]{2,1,0:T(8,128)S(1)}, f32[8,128,128]{2,1,0:T(8,128)S(1)}, u32[]{:S(2)}, u32[]{:S(2)}) collective-permute-start(f32[8,128,128]{2,1,0:T(8,128)S(1)} %slice.74), channel_id=1, source_target_pairs={{0,1},{1,2},{2,3},{3,0},{4,5},{5,6},{6,7},{7,4},{8,9},{9,10},{10,1... | collective-permute-start | bytes 1572872 | tf_op jit(solution)/shard_map/ppermute | solution.py:271
